TPU v7x, 32 devices: a whole 2x2x4 slice. The times are simulated.
32 devices in a mesh: dp: 8 (over z, y), fsdp: 4 (over x, core).
Axes of the slice: x: 2, y: 2, z: 4, core: 2. Of those that a mesh axis runs over, the one named last changes fastest.
Arguments:
- latents: bfloat16 [24576, 768], P(('dp', 'fsdp')), may hold values from -6 to 6
- noise_draw: bfloat16 [24576, 768], P(('dp', 'fsdp')), may hold values from -6 to 6
- text_states: bfloat16 [96, 128, 768], P(('dp', 'fsdp')), may hold values from -6 to 6
- time_steps: int32 [96], P(('dp', 'fsdp')), may hold values from 0 to 999
- item_lengths: int32 [32, 3], P(('dp', 'fsdp')), may hold values from 1 to 512, 768 in all within a row
- text_lengths: int32 [96], P(('dp', 'fsdp')), may hold values from 1 to 128
- cotangent: bfloat16 [24576, 768], P(('dp', 'fsdp')), may hold values from -6 to 6
- time_in: bfloat16 [256, 768], P('fsdp', 'dp'), may hold values from -0.375 to 0.375
- time_out: bfloat16 [768, 768], P('fsdp', 'dp'), may hold values from -0.21875 to 0.21875
- modulation: bfloat16 [768, 6912], P('fsdp', 'dp'), may hold values from -0.21875 to 0.21875
- self_project: bfloat16 [768, 2304], P('fsdp', 'dp'), may hold values from -0.21875 to 0.21875
- self_output: bfloat16 [768, 768], P('fsdp', 'dp'), may hold values from -0.875 to 0.875
- cross_query: bfloat16 [768, 768], P('fsdp', 'dp'), may hold values from -0.21875 to 0.21875
- cross_memory: bfloat16 [768, 1536], P('fsdp', 'dp'), may hold values from -0.21875 to 0.21875
- cross_output: bfloat16 [768, 768], P('fsdp', 'dp'), may hold values from -0.625 to 0.625
- up_project: bfloat16 [768, 3072], P('fsdp', 'dp'), may hold values from -0.21875 to 0.21875
- down_project: bfloat16 [3072, 768], P('fsdp', 'dp'), may hold values from -0.109375 to 0.109375
Outputs:
- block_out: bfloat16 [24576, 768], P(('dp', 'fsdp'))
- latents_grad: float32 [24576, 768], P(('dp', 'fsdp'))
- time_in_grad: float32 [256, 768], P('fsdp', 'dp')
- time_out_grad: float32 [768, 768], P('fsdp', 'dp')
- modulation_grad: float32 [768, 6912], P('fsdp', 'dp')
- self_project_grad: float32 [768, 2304], P('fsdp', 'dp')
- self_output_grad: float32 [768, 768], P('fsdp', 'dp')
- cross_query_grad: float32 [768, 768], P('fsdp', 'dp')
- cross_memory_grad: float32 [768, 1536], P('fsdp', 'dp')
- cross_output_grad: float32 [768, 768], P('fsdp', 'dp')
- up_project_grad: float32 [768, 3072], P('fsdp', 'dp')
- down_project_grad: float32 [3072, 768], P('fsdp', 'dp')
Inputs may be any that keep to these rules, and one draw needn't show every extreme that they name: `item_lengths`: each device's 3 lengths sum to 768; one of them is 512.
All inputs are finite; a program needn't handle non-finite values.
Results may differ from a plain program's by a relative error of at most 0.022.
Values may be sent and summed in bfloat16 or wider, within the bound.
A program may use at most 256 MiB of HBM per device.

v0:
```python
from functools import partial
import math

import jax
import jax.numpy as jnp
from jax import lax
from jax.sharding import PartitionSpec as P

HEADS = 12
FREQ = 256
HD = 64


HIGHEST = lax.Precision.HIGHEST


def high_dot(left, right):
    return jnp.dot(left, right, precision=HIGHEST, preferred_element_type=jnp.float32)


def narrow_dot(left, right):
    return jnp.dot(left, right, preferred_element_type=jnp.float32)


def modulate(stream, offset, stretch):
    center = stream - jnp.mean(stream, axis=1, keepdims=True)
    spread = jnp.mean(center * center, axis=1, keepdims=True)
    return center * lax.rsqrt(spread + 1e-06) * (1.0 + stretch) + offset


def layout(frame_count, lengths_row, text_row, text_width):
    item_ends = jnp.cumsum(lengths_row)
    places = jnp.arange(frame_count, dtype=jnp.int32)
    owners = jnp.sum((places[:, None] >= item_ends[None, :]).astype(jnp.int32), axis=1)
    member = (owners[:, None] == jnp.arange(lengths_row.shape[0], dtype=jnp.int32)[None, :]).astype(
        jnp.float32
    )
    same_item = owners[:, None] == owners[None, :]
    slot_index = jnp.arange(lengths_row.shape[0] * text_width, dtype=jnp.int32)
    slot_item = slot_index // text_width
    slot_live = slot_index % text_width < jnp.repeat(text_row, text_width)
    text_mask = (slot_item[None, :] == owners[:, None]) & slot_live[None, :]
    return (member, same_item, text_mask)


def plan(step_row):
    levels = step_row.astype(jnp.float32)
    cumulative = jnp.cos(0.5 * math.pi * (levels / 1000.0 + 0.008) / 1.008) ** 2
    half_width = FREQ // 2
    frequency = jnp.exp(-math.log(10000.0) * jnp.arange(half_width, dtype=jnp.float32) / half_width)
    angles = levels[:, None] * frequency[None, :]
    embedding = jnp.concatenate([jnp.cos(angles), jnp.sin(angles)], axis=1)
    return (jnp.sqrt(cumulative), jnp.sqrt(1.0 - cumulative), embedding)


def time_path(embedding, first_weight, second_weight):
    hidden_time = jax.nn.silu(high_dot(embedding, first_weight))
    return jax.nn.silu(high_dot(hidden_time, second_weight))


def split_heads(rows):
    return rows.reshape(rows.shape[0], HEADS, -1).transpose(1, 0, 2)


def join_heads(stacked):
    return stacked.transpose(1, 0, 2).reshape(stacked.shape[1], -1)


def attend_forward(queries, key_rows, value_rows, allowed, factor):

    def single(parts):
        head_query, head_key, head_value = parts
        scores = jnp.where(allowed, narrow_dot(head_query, head_key.T) * factor, -1e30)
        largest = jnp.max(scores, axis=1, keepdims=True)
        raised = jnp.exp(scores - largest)
        totals = jnp.sum(raised, axis=1, keepdims=True)
        probs = raised / totals
        result = narrow_dot(probs.astype(jnp.bfloat16), head_value).astype(jnp.bfloat16)
        return (result, largest[:, 0] + jnp.log(totals[:, 0]))

    joined, log_total = lax.map(
        single, (split_heads(queries), split_heads(key_rows), split_heads(value_rows))
    )
    return (join_heads(joined), log_total)


def attend_backward(queries, key_rows, value_rows, allowed, factor, log_total, grad_rows):

    def single(parts):
        head_query, head_key, head_value, head_total, head_grad = parts
        scores = jnp.where(allowed, narrow_dot(head_query, head_key.T) * factor, -1e30)
        probs = jnp.exp(scores - head_total[:, None])
        value_grad = narrow_dot(probs.astype(jnp.bfloat16).T, head_grad)
        prob_grad = narrow_dot(head_grad, head_value.T)
        score_grad = probs * (prob_grad - jnp.sum(probs * prob_grad, axis=1, keepdims=True))
        scaled = score_grad.astype(jnp.bfloat16) * factor
        return (narrow_dot(scaled, head_key), narrow_dot(scaled.T, head_query), value_grad)

    query_grad, key_grad, value_grad = lax.map(
        single,
        (
            split_heads(queries),
            split_heads(key_rows),
            split_heads(value_rows),
            log_total,
            split_heads(grad_rows),
        ),
    )
    return (join_heads(query_grad), join_heads(key_grad), join_heads(value_grad))


def body(
    latents,
    noise_draw,
    text_states,
    time_steps,
    item_lengths,
    text_lengths,
    cotangent,
    time_in,
    time_out,
    modulation,
    self_project,
    self_output,
    cross_query,
    cross_memory,
    cross_output,
    up_project,
    down_project,
):
    row_parts = (
        lax.all_gather(time_in, "fsdp", axis=0, tiled=True),
        lax.all_gather(time_out, "fsdp", axis=0, tiled=True),
        lax.all_gather(modulation, "fsdp", axis=0, tiled=True),
        lax.all_gather(self_project, "fsdp", axis=0, tiled=True),
        lax.all_gather(self_output, "fsdp", axis=0, tiled=True),
        lax.all_gather(cross_query, "fsdp", axis=0, tiled=True),
        lax.all_gather(cross_memory, "fsdp", axis=0, tiled=True),
        lax.all_gather(cross_output, "fsdp", axis=0, tiled=True),
        lax.all_gather(up_project, "fsdp", axis=0, tiled=True),
        lax.all_gather(down_project, "fsdp", axis=0, tiled=True),
    )
    forward_set = (
        lax.all_gather(row_parts[0], "dp", axis=1, tiled=True),
        lax.all_gather(row_parts[1], "dp", axis=1, tiled=True),
        lax.all_gather(row_parts[2], "dp", axis=1, tiled=True),
        lax.all_gather(row_parts[3], "dp", axis=1, tiled=True),
        lax.all_gather(row_parts[4], "dp", axis=1, tiled=True),
        lax.all_gather(row_parts[5], "dp", axis=1, tiled=True),
        lax.all_gather(row_parts[6], "dp", axis=1, tiled=True),
        lax.all_gather(row_parts[7], "dp", axis=1, tiled=True),
        lax.all_gather(row_parts[8], "dp", axis=1, tiled=True),
        lax.all_gather(row_parts[9], "dp", axis=1, tiled=True),
    )
    frames = latents.shape[0]
    member, same_item, text_mask = layout(
        frames, item_lengths[0], text_lengths, text_states.shape[1]
    )
    keep_part, noise_part, embedding = plan(time_steps)
    keep_rows = high_dot(member, keep_part[:, None])
    stream = keep_rows * latents.astype(jnp.float32) + high_dot(
        member, noise_part[:, None]
    ) * noise_draw.astype(jnp.float32)
    condition = time_path(
        embedding, forward_set[0].astype(jnp.float32), forward_set[1].astype(jnp.float32)
    )
    cond_low = condition.astype(jnp.bfloat16)
    mod_rows = narrow_dot(cond_low, forward_set[2])
    mod_terms = jnp.split(high_dot(member, mod_rows), 9, axis=1)
    factor = float(HD) ** (-0.5)
    normed_one, pull_one = jax.vjp(modulate, stream, mod_terms[0], mod_terms[1])
    normed_one = normed_one.astype(jnp.bfloat16)
    packed = narrow_dot(normed_one, forward_set[3]).astype(jnp.bfloat16)
    query_a, key_a, value_a = jnp.split(packed, 3, axis=1)
    attended, total_one = attend_forward(query_a, key_a, value_a, same_item, factor)
    branch_one = narrow_dot(attended, forward_set[4])
    stream_one = stream + mod_terms[2] * branch_one
    normed_two, pull_two = jax.vjp(modulate, stream_one, mod_terms[3], mod_terms[4])
    normed_two = normed_two.astype(jnp.bfloat16)
    query_b = narrow_dot(normed_two, forward_set[5]).astype(jnp.bfloat16)
    text_flat = text_states.reshape(-1, text_states.shape[2])
    memory = narrow_dot(text_flat, forward_set[6]).astype(jnp.bfloat16)
    key_b, value_b = jnp.split(memory, 2, axis=1)
    crossed, total_two = attend_forward(query_b, key_b, value_b, text_mask, factor)
    branch_two = narrow_dot(crossed, forward_set[7])
    stream_two = stream_one + mod_terms[5] * branch_two
    normed_three, pull_three = jax.vjp(modulate, stream_two, mod_terms[6], mod_terms[7])
    normed_three = normed_three.astype(jnp.bfloat16)
    inner_rows = narrow_dot(normed_three, forward_set[8])
    active, gelu_pull = jax.vjp(partial(jax.nn.gelu, approximate=True), inner_rows)
    active = active.astype(jnp.bfloat16)
    branch_three = narrow_dot(active, forward_set[9])
    block_out = (stream_two + mod_terms[8] * branch_three).astype(jnp.bfloat16)
    again_parts = (
        lax.all_gather(time_in, "fsdp", axis=0, tiled=True),
        lax.all_gather(time_out, "fsdp", axis=0, tiled=True),
        lax.all_gather(modulation, "fsdp", axis=0, tiled=True),
        lax.all_gather(self_project, "fsdp", axis=0, tiled=True),
        lax.all_gather(self_output, "fsdp", axis=0, tiled=True),
        lax.all_gather(cross_query, "fsdp", axis=0, tiled=True),
        lax.all_gather(cross_memory, "fsdp", axis=0, tiled=True),
        lax.all_gather(cross_output, "fsdp", axis=0, tiled=True),
        lax.all_gather(up_project, "fsdp", axis=0, tiled=True),
        lax.all_gather(down_project, "fsdp", axis=0, tiled=True),
    )
    back_set = (
        lax.all_gather(again_parts[0], "dp", axis=1, tiled=True),
        lax.all_gather(again_parts[1], "dp", axis=1, tiled=True),
        lax.all_gather(again_parts[2], "dp", axis=1, tiled=True),
        lax.all_gather(again_parts[3], "dp", axis=1, tiled=True),
        lax.all_gather(again_parts[4], "dp", axis=1, tiled=True),
        lax.all_gather(again_parts[5], "dp", axis=1, tiled=True),
        lax.all_gather(again_parts[6], "dp", axis=1, tiled=True),
        lax.all_gather(again_parts[7], "dp", axis=1, tiled=True),
        lax.all_gather(again_parts[8], "dp", axis=1, tiled=True),
        lax.all_gather(again_parts[9], "dp", axis=1, tiled=True),
    )
    grad_top = cotangent.astype(jnp.float32)
    gate_three = grad_top * branch_three
    grad_three = (mod_terms[8] * grad_top).astype(jnp.bfloat16)
    down_grad = narrow_dot(active.T, grad_three)
    inner_grad = gelu_pull(narrow_dot(grad_three, back_set[9].T))[0].astype(jnp.bfloat16)
    up_grad = narrow_dot(normed_three.T, inner_grad)
    stream_back, offset_three, stretch_three = pull_three(narrow_dot(inner_grad, back_set[8].T))
    grad_middle = grad_top + stream_back
    gate_two = grad_middle * branch_two
    grad_two = (mod_terms[5] * grad_middle).astype(jnp.bfloat16)
    cross_out_grad = narrow_dot(crossed.T, grad_two)
    crossed_grad = narrow_dot(grad_two, back_set[7].T).astype(jnp.bfloat16)
    query_b_grad, key_b_grad, value_b_grad = attend_backward(
        query_b, key_b, value_b, text_mask, factor, total_two, crossed_grad
    )
    query_b_low = query_b_grad.astype(jnp.bfloat16)
    cross_query_grad = narrow_dot(normed_two.T, query_b_low)
    memory_grad = narrow_dot(
        text_flat.T, jnp.concatenate([key_b_grad, value_b_grad], axis=1).astype(jnp.bfloat16)
    )
    stream_back, offset_two, stretch_two = pull_two(narrow_dot(query_b_low, back_set[5].T))
    grad_lower = grad_middle + stream_back
    gate_one = grad_lower * branch_one
    grad_one = (mod_terms[2] * grad_lower).astype(jnp.bfloat16)
    self_out_grad = narrow_dot(attended.T, grad_one)
    attended_grad = narrow_dot(grad_one, back_set[4].T).astype(jnp.bfloat16)
    query_a_grad, key_a_grad, value_a_grad = attend_backward(
        query_a, key_a, value_a, same_item, factor, total_one, attended_grad
    )
    packed_grad = jnp.concatenate([query_a_grad, key_a_grad, value_a_grad], axis=1).astype(
        jnp.bfloat16
    )
    self_in_grad = narrow_dot(normed_one.T, packed_grad)
    stream_back, offset_one, stretch_one = pull_one(narrow_dot(packed_grad, back_set[3].T))
    stream_grad = grad_lower + stream_back
    latents_grad = keep_rows * stream_grad
    terms_grad = jnp.concatenate(
        [
            offset_one,
            stretch_one,
            gate_one,
            offset_two,
            stretch_two,
            gate_two,
            offset_three,
            stretch_three,
            gate_three,
        ],
        axis=1,
    )
    mod_grad = high_dot(member.T, terms_grad).astype(jnp.bfloat16)
    modulation_grad = narrow_dot(cond_low.T, mod_grad)
    cond_grad = narrow_dot(mod_grad, back_set[2].T)
    cond_again, time_pull = jax.vjp(
        time_path, embedding, back_set[0].astype(jnp.float32), back_set[1].astype(jnp.float32)
    )
    time_grads = time_pull(cond_grad)
    col_sums = (
        lax.psum_scatter(
            time_grads[1].astype(jnp.bfloat16), "dp", scatter_dimension=1, tiled=True
        ).astype(jnp.float32),
        lax.psum_scatter(
            time_grads[2].astype(jnp.bfloat16), "dp", scatter_dimension=1, tiled=True
        ).astype(jnp.float32),
        lax.psum_scatter(
            modulation_grad.astype(jnp.bfloat16), "dp", scatter_dimension=1, tiled=True
        ).astype(jnp.float32),
        lax.psum_scatter(
            self_in_grad.astype(jnp.bfloat16), "dp", scatter_dimension=1, tiled=True
        ).astype(jnp.float32),
        lax.psum_scatter(
            self_out_grad.astype(jnp.bfloat16), "dp", scatter_dimension=1, tiled=True
        ).astype(jnp.float32),
        lax.psum_scatter(
            cross_query_grad.astype(jnp.bfloat16), "dp", scatter_dimension=1, tiled=True
        ).astype(jnp.float32),
        lax.psum_scatter(
            memory_grad.astype(jnp.bfloat16), "dp", scatter_dimension=1, tiled=True
        ).astype(jnp.float32),
        lax.psum_scatter(
            cross_out_grad.astype(jnp.bfloat16), "dp", scatter_dimension=1, tiled=True
        ).astype(jnp.float32),
        lax.psum_scatter(
            up_grad.astype(jnp.bfloat16), "dp", scatter_dimension=1, tiled=True
        ).astype(jnp.float32),
        lax.psum_scatter(
            down_grad.astype(jnp.bfloat16), "dp", scatter_dimension=1, tiled=True
        ).astype(jnp.float32),
    )
    shares = (
        lax.psum_scatter(
            col_sums[0].astype(jnp.bfloat16), "fsdp", scatter_dimension=0, tiled=True
        ).astype(jnp.float32),
        lax.psum_scatter(
            col_sums[1].astype(jnp.bfloat16), "fsdp", scatter_dimension=0, tiled=True
        ).astype(jnp.float32),
        lax.psum_scatter(
            col_sums[2].astype(jnp.bfloat16), "fsdp", scatter_dimension=0, tiled=True
        ).astype(jnp.float32),
        lax.psum_scatter(
            col_sums[3].astype(jnp.bfloat16), "fsdp", scatter_dimension=0, tiled=True
        ).astype(jnp.float32),
        lax.psum_scatter(
            col_sums[4].astype(jnp.bfloat16), "fsdp", scatter_dimension=0, tiled=True
        ).astype(jnp.float32),
        lax.psum_scatter(
            col_sums[5].astype(jnp.bfloat16), "fsdp", scatter_dimension=0, tiled=True
        ).astype(jnp.float32),
        lax.psum_scatter(
            col_sums[6].astype(jnp.bfloat16), "fsdp", scatter_dimension=0, tiled=True
        ).astype(jnp.float32),
        lax.psum_scatter(
            col_sums[7].astype(jnp.bfloat16), "fsdp", scatter_dimension=0, tiled=True
        ).astype(jnp.float32),
        lax.psum_scatter(
            col_sums[8].astype(jnp.bfloat16), "fsdp", scatter_dimension=0, tiled=True
        ).astype(jnp.float32),
        lax.psum_scatter(
            col_sums[9].astype(jnp.bfloat16), "fsdp", scatter_dimension=0, tiled=True
        ).astype(jnp.float32),
    )
    return (
        block_out,
        latents_grad,
        shares[0],
        shares[1],
        shares[2],
        shares[3],
        shares[4],
        shares[5],
        shares[6],
        shares[7],
        shares[8],
        shares[9],
    )


def solution(mesh):
    return jax.shard_map(
        body,
        mesh=mesh,
        in_specs=(
            P(("dp", "fsdp"), None),
            P(("dp", "fsdp"), None),
            P(("dp", "fsdp"), None, None),
            P(("dp", "fsdp")),
            P(("dp", "fsdp"), None),
            P(("dp", "fsdp")),
            P(("dp", "fsdp"), None),
            P("fsdp", "dp"),
            P("fsdp", "dp"),
            P("fsdp", "dp"),
            P("fsdp", "dp"),
            P("fsdp", "dp"),
            P("fsdp", "dp"),
            P("fsdp", "dp"),
            P("fsdp", "dp"),
            P("fsdp", "dp"),
            P("fsdp", "dp"),
        ),
        out_specs=(
            P(("dp", "fsdp"), None),
            P(("dp", "fsdp"), None),
            P("fsdp", "dp"),
            P("fsdp", "dp"),
            P("fsdp", "dp"),
            P("fsdp", "dp"),
            P("fsdp", "dp"),
            P("fsdp", "dp"),
            P("fsdp", "dp"),
            P("fsdp", "dp"),
            P("fsdp", "dp"),
            P("fsdp", "dp"),
        ),
        check_vma=False,
    )
```

profile of v0, /device:TPU:0, one launch (start us, length us, event | category | flops | bytes accessed | tf_op | source)
XLA Modules:
  0.0 2082.7 jit_solution(3391863293492043227)
XLA Ops:
  88.9 32.7 %all_gather.79 = bf16[256,768]{0,1:T(8,128)(2,1)S(1)} all-gather(bf16[256,96]{0,1:T(8,128)(2,1)S(1)} %copy.199), channel_id=1, replica_groups=mesh['dp'=8,'fsdp'=4] {'dp'}, dimensions={1}, use_global_device_ids=true | all-gather | bytes 442368 | tf_op jit(solution)/shard_map/all_gather | solution.py:144
  142.4 144.8 %all-gather.15.cloned.1.call-done = bf16[768,6912]{0,1:T(8,128)(2,1)} async-done(((bf16[768,864]{0,1:T(8,128)(2,1)}), bf16[768,6912]{0,1:T(8,128)(2,1)}) %all-gather.15.cloned.1.call-update) | async-done | bytes 10616848 | tf_op jit(solution)/shard_map/all_gather | solution.py:146
  311.9 40.7 %all-gather.17.cloned.1.call-done = bf16[768,2304]{0,1:T(8,128)(2,1)} async-done(((bf16[768,288]{0,1:T(8,128)(2,1)}), bf16[768,2304]{0,1:T(8,128)(2,1)}) %all-gather.17.cloned.1.call-update) | async-done | bytes 3538960 | tf_op jit(solution)/shard_map/all_gather | solution.py:147
  375.7 48.4 %while.56 = (s32[]{:T(128)}, bf16[12,768,64]{1,2,0:T(8,128)(2,1)}, f32[12,768]{1,0:T(8,128)S(1)}, bf16[12,768,64]{2,1,0:T(8,128)(2,1)}, bf16[12,768,64]{2,1,0:T(...) while((s32[]{:T(128)}, bf16[12,768,64]{1,2,0:T(8,128)(2,1)}, ...), condition=%wide.region_7.8_spmd.clone, body=%wide.region_4.7_spmd.clone.sunk | while | flops 156351744 | bytes 7813225 | solution.py:81
  446.0 43.5 %while.57 = (s32[]{:T(128)}, bf16[12,768,64]{1,2,0:T(8,128)(2,1)}, f32[12,768]{1,0:T(8,128)S(1)}, bf16[12,768,64]{2,1,0:T(8,128)(2,1)}, bf16[12,384,64]{2,1,0:T(...) while((s32[]{:T(128)}, bf16[12,768,64]{1,2,0:T(8,128)(2,1)}, ...), condition=%wide.region_13.14_spmd.clone, body=%wide.region_10.13_spmd.clone.sunk | while | flops 78494976 | bytes 4074489 | solution.py:81
  500.0 61.4 %all-gather.27.cloned.1.call-done = bf16[768,3072]{1,0:T(8,128)(2,1)} async-done(((bf16[768,384]{1,0:T(8,128)(2,1)}), bf16[768,3072]{1,0:T(8,128)(2,1)}) %all-gather.27.cloned.1.call-update) | async-done | bytes 4718608 | tf_op jit(solution)/shard_map/all_gather | solution.py:152
  571.5 69.9 %all-gather.29.cloned.1.call-done = bf16[3072,768]{0,1:T(8,128)(2,1)} async-done(((bf16[3072,96]{0,1:T(8,128)(2,1)}), bf16[3072,768]{0,1:T(8,128)(2,1)}) %all-gather.29.cloned.1.call-update) | async-done | bytes 4718608 | tf_op jit(solution)/shard_map/all_gather | solution.py:153
  685.2 103.6 %while.58 = (s32[]{:T(128)}, bf16[12,768,64]{1,2,0:T(8,128)(2,1)}, bf16[12,384,64]{1,2,0:T(8,128)(2,1)}, bf16[12,384,64]{1,2,0:T(8,128)(2,1)}, bf16[12,768,64]{2...) while((s32[]{:T(128)}, bf16[12,768,64]{1,2,0:T(8,128)(2,1)}, ...), condition=%wide.region_20.21_spmd.clone, body=%wide.region_18.20_spmd.clone.sunk | while | flops 192281856 | bytes 10347529 | solution.py:99
  809.3 118.6 %while.59 = (s32[]{:T(128)}, bf16[12,768,64]{1,2,0:T(8,128)(2,1)}, bf16[12,768,64]{1,2,0:T(8,128)(2,1)}, bf16[12,768,64]{1,2,0:T(8,128)(2,1)}, bf16[12,768,64]{2...) while((s32[]{:T(128)}, bf16[12,768,64]{1,2,0:T(8,128)(2,1)}, ...), condition=%wide.region_25.26_spmd.clone, body=%wide.region_23.25_spmd.clone.sunk | while | flops 383974656 | bytes 19690616 | solution.py:99
  1036.6 64.7 %reduce-scatter.53.cloned.1.call-done = bf16[768,96]{0,1:T(8,128)(2,1)} async-done(((bf16[768,768]{0,1:T(8,128)(2,1)}), bf16[768,96]{0,1:T(8,128)(2,1)}) %reduce-scatter.53.cloned.1.call-update) | async-done | bytes 147472 | tf_op jit(solution)/shard_map/reduce_scatter | solution.py:297
  1103.2 64.7 %reduce-scatter.49.cloned.1.call-done = bf16[768,96]{0,1:T(8,128)(2,1)} async-done(((bf16[768,768]{0,1:T(8,128)(2,1)}), bf16[768,96]{0,1:T(8,128)(2,1)}) %reduce-scatter.49.cloned.1.call-update) | async-done | bytes 147472 | tf_op jit(solution)/shard_map/reduce_scatter | solution.py:291
  1169.7 64.4 %reduce-scatter.47.cloned.1.call-done = bf16[768,96]{0,1:T(8,128)(2,1)} async-done(((bf16[768,768]{0,1:T(8,128)(2,1)}), bf16[768,96]{0,1:T(8,128)(2,1)}) %reduce-scatter.47.cloned.1.call-update) | async-done | bytes 147472 | tf_op jit(solution)/shard_map/reduce_scatter | solution.py:288
  1235.9 64.5 %reduce-scatter.41.cloned.1.call-done = bf16[768,96]{0,1:T(8,128)(2,1)} async-done(((bf16[768,768]{0,1:T(8,128)(2,1)}), bf16[768,96]{0,1:T(8,128)(2,1)}) %reduce-scatter.41.cloned.1.call-update) | async-done | bytes 147472 | tf_op jit(solution)/shard_map/reduce_scatter | solution.py:279
  1302.2 69.8 %reduce-scatter.51.cloned.1.call-done = bf16[768,192]{0,1:T(8,128)(2,1)} async-done(((bf16[768,1536]{0,1:T(8,128)(2,1)}), bf16[768,192]{0,1:T(8,128)(2,1)}) %reduce-scatter.51.cloned.1.call-update) | async-done | bytes 294928 | tf_op jit(solution)/shard_map/reduce_scatter | solution.py:294
  1373.9 79.8 %reduce-scatter.45.cloned.1.call-done = bf16[768,288]{0,1:T(8,128)(2,1)} async-done(((bf16[768,2304]{0,1:T(8,128)(2,1)}), bf16[768,288]{0,1:T(8,128)(2,1)}) %reduce-scatter.45.cloned.1.call-update) | async-done | bytes 442384 | tf_op jit(solution)/shard_map/reduce_scatter | solution.py:285
  1455.9 96.2 %reduce-scatter.77.cloned.1.call-done = bf16[384,768]{1,0:T(8,128)(2,1)} async-done(((bf16[3072,768]{1,0:T(8,128)(2,1)}), bf16[384,768]{1,0:T(8,128)(2,1)}) %reduce-scatter.77.cloned.1.call-update) | async-done | bytes 589840
  1554.3 96.4 %reduce-scatter.57.cloned.1.call-done = bf16[3072,96]{0,1:T(8,128)(2,1)} async-done(((bf16[3072,768]{0,1:T(8,128)(2,1)}), bf16[3072,96]{0,1:T(8,128)(2,1)}) %reduce-scatter.57.cloned.1.call-update) | async-done | bytes 589840 | tf_op jit(solution)/shard_map/reduce_scatter | solution.py:303
  1650.8 182.9 %reduce-scatter.43.cloned.1.call-done = bf16[768,864]{0,1:T(8,128)(2,1)} async-done(((bf16[768,6912]{0,1:T(8,128)(2,1)}), bf16[768,864]{0,1:T(8,128)(2,1)}) %reduce-scatter.43.cloned.1.call-update) | async-done | bytes 1327120 | tf_op jit(solution)/shard_map/reduce_scatter | solution.py:282
  1857.0 21.3 %reduce-scatter.75.cloned.1.call-done = bf16[192,96]{1,0:T(8,128)(2,1)} async-done(((bf16[768,96]{1,0:T(8,128)(2,1)}), bf16[192,96]{1,0:T(8,128)(2,1)}) %reduce-scatter.75.cloned.1.call-update) | async-done | bytes 36880
  1948.0 21.6 %reduce-scatter.73.cloned.1.call-done = bf16[192,192]{1,0:T(8,128)(2,1)} async-done(((bf16[768,192]{1,0:T(8,128)(2,1)}), bf16[192,192]{1,0:T(8,128)(2,1)}) %reduce-scatter.73.cloned.1.call-update) | async-done | bytes 73744
  1971.4 23.2 %reduce-scatter.67.cloned.1.call-done = bf16[192,288]{1,0:T(8,128)(2,1)} async-done(((bf16[768,288]{1,0:T(8,128)(2,1)}), bf16[192,288]{1,0:T(8,128)(2,1)}) %reduce-scatter.67.cloned.1.call-update) | async-done | bytes 110608
  1996.5 22.8 %reduce-scatter.55.cloned.1.call-done = bf16[192,384]{1,0:T(8,128)(2,1)} async-done(((bf16[768,384]{1,0:T(8,128)(2,1)}), bf16[192,384]{1,0:T(8,128)(2,1)}) %reduce-scatter.55.cloned.1.call-update) | async-done | bytes 147472 | tf_op jit(solution)/shard_map/reduce_scatter | solution.py:332
  2020.9 22.9 %reduce-scatter.59.cloned.1.call-done = bf16[768,96]{0,1:T(8,128)(2,1)} async-done(((bf16[3072,96]{0,1:T(8,128)(2,1)}), bf16[768,96]{0,1:T(8,128)(2,1)}) %reduce-scatter.59.cloned.1.call-update) | async-done | bytes 147472 | tf_op jit(solution)/shard_map/reduce_scatter | solution.py:335
  2045.4 27.8 %reduce-scatter.65.cloned.1.call-done = bf16[192,864]{1,0:T(8,128)(2,1)} async-done(((bf16[768,864]{1,0:T(8,128)(2,1)}), bf16[192,864]{1,0:T(8,128)(2,1)}) %reduce-scatter.65.cloned.1.call-update) | async-done | bytes 331792
  (672 shorter events, 792.8 us)
Async XLA Ops:
  23.8 263.4 %all-gather.15.cloned.1.call-start = ((), (), s32[]{:S(2)}) async-start(), calls=%async_computation.22 | async-start | bytes 11943936 | tf_op jit(solution)/shard_map/all_gather | solution.py:146
  33.4 319.2 %all-gather.17.cloned.1.call-start = ((), (), s32[]{:S(2)}) async-start(), calls=%async_computation.23 | async-start | bytes 3981312 | tf_op jit(solution)/shard_map/all_gather | solution.py:147
  42.2 382.0 %all-gather.19.cloned.1.call-start = ((), (), s32[]{:S(2)}) async-start(), calls=%async_computation.24 | async-start | bytes 1327104 | tf_op jit(solution)/shard_map/all_gather | solution.py:148
  48.7 388.7 %all-gather.21.cloned.1.call-start = ((), (), s32[]{:S(2)}) async-start(), calls=%async_computation.25 | async-start | bytes 1327104 | tf_op jit(solution)/shard_map/all_gather | solution.py:149
  55.3 434.3 %all-gather.25.cloned.1.call-start = ((), (), s32[]{:S(2)}) async-start(), calls=%async_computation.27 | async-start | bytes 1327104 | tf_op jit(solution)/shard_map/all_gather | solution.py:151
  61.8 499.5 %all-gather.27.cloned.1.call-start = ((), (), s32[]{:S(2)}) async-start(), calls=%async_computation.28 | async-start | bytes 5308416 | tf_op jit(solution)/shard_map/all_gather | solution.py:152
  70.0 571.5 %all-gather.29.cloned.1.call-start = ((), (), s32[]{:S(2)}) async-start(), calls=%async_computation.29 | async-start | bytes 5308416 | tf_op jit(solution)/shard_map/all_gather | solution.py:153
  78.2 956.8 %reduce-scatter.39.cloned.1.call-start = ((), (), s32[]{:S(2)}) async-start(), calls=%async_computation.30 | async-start | bytes 442368 | tf_op jit(solution)/shard_map/reduce_scatter | solution.py:276
  986.1 314.3 %reduce-scatter.41.cloned.1.call-start = ((), (), s32[]{:S(2)}) async-start(), calls=%async_computation.31 | async-start | bytes 1327104 | tf_op jit(solution)/shard_map/reduce_scatter | solution.py:279
  989.2 382.7 %reduce-scatter.51.cloned.1.call-start = ((), (), s32[]{:S(2)}) async-start(), calls=%async_computation.36 | async-start | bytes 2654208 | tf_op jit(solution)/shard_map/reduce_scatter | solution.py:294
  992.1 461.6 %reduce-scatter.45.cloned.1.call-start = ((), (), s32[]{:S(2)}) async-start(), calls=%async_computation.33 | async-start | bytes 3981312 | tf_op jit(solution)/shard_map/reduce_scatter | solution.py:285
  1000.1 552.0 %reduce-scatter.77.cloned.1.call-start = ((), (), s32[]{:S(2)}) async-start(), calls=%async_computation.49 | async-start | bytes 5308416
  1016.2 634.6 %reduce-scatter.57.cloned.1.call-start = ((), (), s32[]{:S(2)}) async-start(), calls=%async_computation.39 | async-start | bytes 5308416 | tf_op jit(solution)/shard_map/reduce_scatter | solution.py:303
  1026.7 807.1 %reduce-scatter.43.cloned.1.call-start = ((), (), s32[]{:S(2)}) async-start(), calls=%async_computation.32 | async-start | bytes 11943936 | tf_op jit(solution)/shard_map/reduce_scatter | solution.py:282
  1032.5 822.9 %reduce-scatter.61.cloned.1.call-start = ((), (), s32[]{:S(2)}) async-start(), calls=%async_computation.41 | async-start | bytes 81920
  1036.6 841.7 %reduce-scatter.75.cloned.1.call-start = ((), (), s32[]{:S(2)}) async-start(), calls=%async_computation.48 | async-start | bytes 245760
  1103.1 797.9 %reduce-scatter.71.cloned.1.call-start = ((), (), s32[]{:S(2)}) async-start(), calls=%async_computation.46 | async-start | bytes 245760
  1169.6 754.0 %reduce-scatter.69.cloned.1.call-start = ((), (), s32[]{:S(2)}) async-start(), calls=%async_computation.45 | async-start | bytes 245760
  1235.9 710.5 %reduce-scatter.63.cloned.1.call-start = ((), (), s32[]{:S(2)}) async-start(), calls=%async_computation.42 | async-start | bytes 245760
  1302.1 667.5 %reduce-scatter.73.cloned.1.call-start = ((), (), s32[]{:S(2)}) async-start(), calls=%async_computation.47 | async-start | bytes 491520
  1373.9 620.7 %reduce-scatter.67.cloned.1.call-start = ((), (), s32[]{:S(2)}) async-start(), calls=%async_computation.44 | async-start | bytes 737280
  1455.8 563.4 %reduce-scatter.55.cloned.1.call-start = ((), (), s32[]{:S(2)}) async-start(), calls=%async_computation.38 | async-start | bytes 737280 | tf_op jit(solution)/shard_map/reduce_scatter | solution.py:332
  1554.3 489.5 %reduce-scatter.59.cloned.1.call-start = ((), (), s32[]{:S(2)}) async-start(), calls=%async_computation.40 | async-start | bytes 737280 | tf_op jit(solution)/shard_map/reduce_scatter | solution.py:335
  1650.8 422.4 %reduce-scatter.65.cloned.1.call-start = ((), (), s32[]{:S(2)}) async-start(), calls=%async_computation.43 | async-start | bytes 1720320
  (80 other events, 1727.4 us)
Sparse Core Ops, SparseCore 0:
  9.6 21.2 all-gather.12
  33.6 42.3 all-gather.10
  78.8 53.6 all-gather.22
  135.1 152.0 all-gather.14
  289.2 63.3 all-gather.16
  355.2 39.5 all-gather.18
  397.6 39.8 all-gather.20
  439.6 39.8 all-gather.24
  481.5 79.7 all-gather.26
  563.4 78.0 all-gather.28
  975.5 59.4 reduce-scatter.38
  1038.3 63.0 reduce-scatter.52
  1104.8 63.0 reduce-scatter.48
  1171.1 62.9 reduce-scatter.46
  1237.3 63.0 reduce-scatter.40
  1303.7 68.2 reduce-scatter.50
  1375.5 78.2 reduce-scatter.44
  1457.2 94.7 reduce-scatter.76
  1555.7 95.0 reduce-scatter.56
  1654.2 179.5 reduce-scatter.42
  1972.5 22.0 reduce-scatter.66
  1997.1 22.0 reduce-scatter.54
  2021.7 22.0 reduce-scatter.58
  2046.2 26.9 reduce-scatter.64
  (6 shorter events, 117.8 us)
where the time goes:
time: 2100 us; the launch traced here: 2080 us
  waiting for transfers between devices  1340 us (64%)
  matrix products  460 us (22%)
  local copies, waits for them, and re-layouts  111 us (5%)
  blocking collectives  92.9 us (4%)
  other arithmetic  58.3 us (3%)
    dot_general x191, matrix products, narrow_dot(): return jnp.dot(left, right, preferred_element_type=jnp.float32)  430 us
    unnamed x39, waiting for transfers between devices  274 us
    reduce_scatter x1, waiting for transfers between devices, body(): lax.psum_scatter(modulation_grad.astype(jnp.bfloat16), 'dp', scatter_dime...  183 us
    all_gather x1, waiting for transfers between devices, body(): lax.all_gather(row_parts[2], 'dp', axis=1, tiled=True)  145 us
    reduce_scatter x1, waiting for transfers between devices, body(): lax.psum_scatter(down_grad.astype(jnp.bfloat16), 'dp', scatter_dimension=...  96.4 us
    reduce_scatter x1, waiting for transfers between devices, body(): lax.psum_scatter(self_in_grad.astype(jnp.bfloat16), 'dp', scatter_dimensi...  79.8 us
    unnamed x181, local copies, waits for them, and re-layouts  72.3 us
    all_gather x1, waiting for transfers between devices, body(): lax.all_gather(row_parts[9], 'dp', axis=1, tiled=True)  69.9 us
  transfers between devices with their start and end apart: 30, of which 27 were waited for; matrix products, arithmetic and copies ran while one was open for 13% of the time, Pallas kernels for 0%

commit v1 on v0

v1 whole, which is shorter than its diff:
```python
from functools import partial
import math

import jax
import jax.numpy as jnp
from jax import lax
from jax.experimental import pallas as pl
from jax.experimental.pallas import tpu as pltpu
from jax.sharding import PartitionSpec as P

F32, BF16 = jnp.float32, jnp.bfloat16
HEADS = 12
FREQ = 256
HD = 64
FACTOR = float(HD) ** -0.5
PAIR = 2 * HD
PAIRS = HEADS // 2
BIG = 1e30
TILE = 256
MIB = 2**20


def dot(left, right, lc, rc):
    return lax.dot_general(left, right, (((lc,), (rc,)), ((), ())), preferred_element_type=F32)


def nt(left, right):
    return dot(left, right, 1, 1)


def nn(left, right):
    return dot(left, right, 1, 0)


def tn(left, right):
    return dot(left, right, 0, 0)


def owners_column(lens, first, rows):
    place = lax.broadcasted_iota(jnp.int32, (rows, 1), 0) + first
    end = lens[0, 0]
    return (place >= end).astype(jnp.int32) + (place >= end + lens[0, 1]).astype(jnp.int32)


def owners_row(lens, cols):
    place = lax.broadcasted_iota(jnp.int32, (1, cols), 1)
    end = lens[0, 0]
    return (place >= end).astype(jnp.int32) + (place >= end + lens[0, 1]).astype(jnp.int32)


def pick(own, a, b, c):
    return jnp.where(own == 0, a, jnp.where(own == 1, b, c))


def expand(own, mod, block, width):
    lo = block * width
    return pick(own, mod[0:1, lo : lo + width], mod[1:2, lo : lo + width], mod[2:3, lo : lo + width])


def item_sums(lens, first, rows, values):
    items = lax.broadcasted_iota(jnp.int32, (16, rows), 0)
    place = lax.broadcasted_iota(jnp.int32, (16, rows), 1) + first
    end = lens[0, 0]
    own = (place >= end).astype(jnp.int32) + (place >= end + lens[0, 1]).astype(jnp.int32)
    member = jnp.where(items == own, 1.0, 0.0).astype(BF16)
    return nn(member, values.astype(BF16))


def fill_masks(lens, tlens, aq, aks, akc):
    rows = aq.shape[0]
    lane = lax.broadcasted_iota(jnp.int32, (rows, PAIR), 1) % HD
    own = owners_column(lens, 0, rows)
    aq[...] = jnp.where(own == lane, 1.0, 0.0).astype(BF16)
    minus = jnp.where((lane >= 3) & (lane < 6), -1.0, 0.0)
    aks[...] = jnp.where((lane < 3) & (own != lane), -BIG, minus).astype(BF16)
    slots = akc.shape[0]
    text = slots // 3
    lane = lax.broadcasted_iota(jnp.int32, (slots, PAIR), 1) % HD
    minus = jnp.where((lane >= 3) & (lane < 6), -1.0, 0.0)
    slot = lax.broadcasted_iota(jnp.int32, (slots, 1), 0)
    item = (slot >= text).astype(jnp.int32) + (slot >= 2 * text).astype(jnp.int32)
    live = slot - item * text < pick(item, tlens[0], tlens[1], tlens[2])
    akc[...] = jnp.where((lane < 3) & ((item != lane) | ~live), -BIG, minus).astype(BF16)


def pieces(column):
    one = column.astype(BF16).astype(F32)
    two = (column - one).astype(BF16).astype(F32)
    return one, two, column - one - two


def attention_forward(q, k, k_at, v_at, ak, aq, out, qaug):
    frames = q.shape[0]

    def pair(p, carry):
        lanes = pl.ds(pl.multiple_of(p * PAIR, PAIR), PAIR)
        kp = k[:, pl.ds(pl.multiple_of(k_at + p * PAIR, PAIR), PAIR)]
        vp = k[:, pl.ds(pl.multiple_of(v_at + p * PAIR, PAIR), PAIR)]
        klow = lax.broadcasted_iota(jnp.int32, kp.shape, 1) < HD
        keys = (jnp.where(klow, kp, ak[...]), jnp.where(klow, ak[...], kp))
        one = jnp.ones_like(vp)
        values = (jnp.where(klow, vp, one), jnp.where(klow, one, vp))
        lane = lax.broadcasted_iota(jnp.int32, (TILE, PAIR), 1)
        low, inner = lane < HD, lane % HD
        for t in range(frames // TILE):
            rows = pl.ds(t * TILE, TILE)
            qp = q[rows, lanes] * jnp.asarray(FACTOR, BF16)
            mark = aq[rows, :]
            done = []
            for h in range(2):
                own = low if h == 0 else ~low
                qh = jnp.where(own, qp, mark)
                s = nt(qh, keys[h])
                top = jnp.max(s, axis=1, keepdims=True)
                e = jnp.exp(s - top).astype(BF16)
                o = nn(e, values[h])
                total = o[:, HD : HD + 1] if h == 0 else o[:, 0:1]
                done.append(o * (1.0 / total))
                a, b, c = pieces(top + jnp.log(total))
                extra = jnp.where(inner == 3, a, jnp.where(inner == 4, b, c))
                extra = jnp.where((inner >= 3) & (inner < 6), extra, mark.astype(F32)).astype(BF16)
                at = pl.ds(pl.multiple_of((2 * p + h) * PAIR, PAIR), PAIR)
                qaug[rows, at] = jnp.where(own, qp, extra)
            out[rows, lanes] = jnp.where(low, done[0], done[1]).astype(BF16)
        return carry

    lax.fori_loop(0, PAIRS, pair, 0)


def attention_backward(qaug, k, k_at, v_at, ak, att, datt, dq, dk, dk_at, dv_at, acc):
    frames = att.shape[0]
    tall = k.shape[0]
    step = TILE if tall % TILE == 0 else PAIR

    def pair(p, carry):
        lanes = pl.ds(pl.multiple_of(p * PAIR, PAIR), PAIR)
        lane = lax.broadcasted_iota(jnp.int32, (frames, PAIR), 1)
        low, inner = lane < HD, lane % HD
        do = datt[:, lanes]
        both = do.astype(F32) * att[:, lanes].astype(F32)
        outs, queries = [], []
        for h in range(2):
            own = low if h == 0 else ~low
            a, b, c = pieces(jnp.sum(jnp.where(own, both, 0.0), axis=1, keepdims=True))
            extra = jnp.where(inner == 3, a, jnp.where(inner == 4, b, c))
            extra = jnp.where((inner >= 3) & (inner < 6), extra, 0.0).astype(BF16)
            outs.append(jnp.where(own, do, extra))
            queries.append(qaug[:, pl.ds(pl.multiple_of((2 * p + h) * PAIR, PAIR), PAIR)])
        for t in range(tall // step):
            rows = pl.ds(t * step, step)
            kp = k[rows, pl.ds(pl.multiple_of(k_at + p * PAIR, PAIR), PAIR)]
            vp = k[rows, pl.ds(pl.multiple_of(v_at + p * PAIR, PAIR), PAIR)]
            mark = ak[rows, :]
            klow = lax.broadcasted_iota(jnp.int32, kp.shape, 1) < HD
            kt = kp.T
            dks, dvs = [], []
            for h in range(2):
                own = klow if h == 0 else ~klow
                pt = jnp.exp(nt(jnp.where(own, kp, mark), queries[h]))
                dpt = nt(jnp.where(own, vp, mark), outs[h])
                dst = (pt * dpt).astype(BF16)
                dvs.append(nn(pt.astype(BF16), do))
                dks.append(nn(dst, queries[h]))
                part = nn(kt[h * HD : (h + 1) * HD, :], dst)
                at = pl.ds(h * HD, HD)
                if t == 0:
                    acc[at, :] = part
                else:
                    acc[at, :] += part
            dk[rows, pl.ds(pl.multiple_of(dk_at + p * PAIR, PAIR), PAIR)] = jnp.where(klow, dks[0], dks[1]).astype(BF16)
            dk[rows, pl.ds(pl.multiple_of(dv_at + p * PAIR, PAIR), PAIR)] = jnp.where(klow, dvs[0], dvs[1]).astype(BF16)
        dq[:, lanes] = (acc[...].T * FACTOR).astype(BF16)
        return carry

    lax.fori_loop(0, PAIRS, pair, 0)


def norm_tile(s):
    width = s.shape[1]
    center = s - jnp.sum(s, axis=1, keepdims=True) * (1.0 / width)
    spread = jnp.sum(center * center, axis=1, keepdims=True) * (1.0 / width)
    rs = lax.rsqrt(spread + 1e-06)
    return center * rs, rs


def tiles(count, fn):
    def step(i, carry):
        fn(pl.multiple_of(i * TILE, TILE))
        return carry

    lax.fori_loop(0, count // TILE, step, 0)


def big_nt(left, right, out, width):
    def step(n, carry):
        cols = pl.ds(pl.multiple_of(n * width, width), width)
        out[:, cols] = nt(left[...], right[cols, :]).astype(BF16)
        return carry

    lax.fori_loop(0, right.shape[0] // width, step, 0)


def big_tn(left, right, out, width):
    def step(n, carry):
        cols = pl.ds(pl.multiple_of(n * width, width), width)
        out[cols, :] = tn(left[:, cols], right[...]).astype(BF16)
        return carry

    lax.fori_loop(0, left.shape[1] // width, step, 0)


def norm_into(s, rows, own, lens, mod, sub, xh, m, rs, width):
    hat, r = norm_tile(s)
    xh[rows, :] = hat.astype(BF16)
    base = 3 * sub
    m[rows, :] = (hat * (1.0 + expand(own, mod, base + 1, width)) + expand(own, mod, base, width)).astype(BF16)
    lane = lax.broadcasted_iota(jnp.int32, (TILE, 128), 1)
    rs[rows, :] = jnp.where(lane == sub, r, rs[rows, :])


def forward_attention(lens, tlens, keep, loud, mod, lat, noi, text, wsp, wso, wcq, wcm, wco,
                      stream, xh1, m1, packed, qa1, att1, br1, xh2, m2, mem, qa2, att2, br2, rs,
                      aq, aks, akc, qb, tmp):
    frames, width = lat.shape
    fill_masks(lens, tlens, aq, aks, akc)
    rs[...] = jnp.zeros_like(rs)

    def start(at):
        rows = pl.ds(at, TILE)
        own = owners_column(lens, at, TILE)
        s = pick(own, keep[0], keep[1], keep[2]) * lat[rows, :].astype(F32)
        s = s + pick(own, loud[0], loud[1], loud[2]) * noi[rows, :].astype(F32)
        stream[rows, :] = s
        norm_into(s, rows, own, lens, mod, 0, xh1, m1, rs, width)

    tiles(frames, start)
    big_nt(m1, wsp, packed, width)
    attention_forward(packed, packed, width, 2 * width, aks, aq, att1, qa1)
    tmp[...] = nt(att1[...], wso[...])

    def middle(at):
        rows = pl.ds(at, TILE)
        own = owners_column(lens, at, TILE)
        br = tmp[rows, :]
        br1[rows, :] = br.astype(BF16)
        s = stream[rows, :] + expand(own, mod, 2, width) * br
        stream[rows, :] = s
        norm_into(s, rows, own, lens, mod, 1, xh2, m2, rs, width)

    tiles(frames, middle)
    big_nt(m2, wcq, qb, width)
    big_nt(text, wcm, mem, width)
    attention_forward(qb, mem, 0, width, akc, aq, att2, qa2)
    tmp[...] = nt(att2[...], wco[...])

    def last(at):
        rows = pl.ds(at, TILE)
        own = owners_column(lens, at, TILE)
        br = tmp[rows, :]
        br2[rows, :] = br.astype(BF16)
        stream[rows, :] = stream[rows, :] + expand(own, mod, 5, width) * br

    tiles(frames, last)


GELU_A, GELU_B = math.sqrt(2.0 / math.pi), 0.044715


def forward_ff(lens, mod, stream, wup, wdn, xh3, m3, act, slope, br3, out, rs, tmp):
    frames, width = stream.shape
    rs[...] = jnp.zeros_like(rs)

    def start(at):
        rows = pl.ds(at, TILE)
        own = owners_column(lens, at, TILE)
        norm_into(stream[rows, :], rows, own, lens, mod, 2, xh3, m3, rs, width)

    tiles(frames, start)

    def chunk(n, carry):
        cols = pl.ds(pl.multiple_of(n * width, width), width)
        tmp[...] = nt(m3[...], wup[cols, :])

        def gelu(at):
            rows = pl.ds(at, TILE)
            x = tmp[rows, :]
            sq = x * x
            t = jnp.tanh(x * (GELU_A + GELU_A * GELU_B * sq))
            half = 0.5 + 0.5 * t
            act[rows, cols] = (x * half).astype(BF16)
            slope[rows, cols] = (half + half * (1.0 - t) * x * (GELU_A + 3.0 * GELU_A * GELU_B * sq)).astype(BF16)

        tiles(frames, gelu)
        return carry

    lax.fori_loop(0, wup.shape[0] // width, chunk, 0)
    tmp[...] = nt(act[...], wdn[...])

    def last(at):
        rows = pl.ds(at, TILE)
        own = owners_column(lens, at, TILE)
        br = tmp[rows, :]
        br3[rows, :] = br.astype(BF16)
        out[rows, :] = (stream[rows, :] + expand(own, mod, 8, width) * br).astype(BF16)

    tiles(frames, last)


def norm_back(dm, hat, r, stretch):
    width = dm.shape[1]
    dh = dm * (1.0 + stretch)
    a = jnp.sum(dh, axis=1, keepdims=True) * (1.0 / width)
    b = jnp.sum(dh * hat, axis=1, keepdims=True) * (1.0 / width)
    return r * (dh - a - hat * b)


def add_sums(lens, at, sums, cols, values):
    sums[:, cols] += item_sums(lens, at, TILE, values)


def gate_tile(lens, at, own, mod, g, br, sub, sums, b, width):
    rows = pl.ds(at, TILE)
    add_sums(lens, at, sums, pl.ds((3 * sub + 2) * width, width), g * br[rows, :].astype(F32))
    b[rows, :] = (expand(own, mod, 3 * sub + 2, width) * g).astype(BF16)


def norm_back_tile(lens, at, own, mod, dm, xh, rs, sub, sums, width):
    rows = pl.ds(at, TILE)
    hat = xh[rows, :].astype(F32)
    add_sums(lens, at, sums, pl.ds(3 * sub * width, width), dm)
    add_sums(lens, at, sums, pl.ds((3 * sub + 1) * width, width), dm * hat)
    return norm_back(dm, hat, rs[rows, sub : sub + 1], expand(own, mod, 3 * sub + 1, width))


def backward_ff(lens, mod, cot, br3, act, slope, xh3, m3, rs, wup, wdn, g, b2, br2, dwd, dwu, sums, b3, ig, tmp):
    frames, width = cot.shape
    sums[...] = jnp.zeros_like(sums)

    def start(at):
        rows = pl.ds(at, TILE)
        own = owners_column(lens, at, TILE)
        gate_tile(lens, at, own, mod, cot[rows, :].astype(F32), br3, 2, sums, b3, width)

    tiles(frames, start)

    def chunk(n, carry):
        cols = pl.ds(pl.multiple_of(n * width, width), width)
        dwd[:, cols] = tn(b3[...], act[:, cols]).astype(BF16)
        ig[:, cols] = (nn(b3[...], wdn[:, cols]) * slope[:, cols].astype(F32)).astype(BF16)
        dwu[cols, :] = tn(ig[:, cols], m3[...]).astype(BF16)
        return carry

    lax.fori_loop(0, wup.shape[0] // width, chunk, 0)
    tmp[...] = nn(ig[...], wup[...])

    def last(at):
        rows = pl.ds(at, TILE)
        own = owners_column(lens, at, TILE)
        s = cot[rows, :].astype(F32) + norm_back_tile(lens, at, own, mod, tmp[rows, :], xh3, rs, 2, sums, width)
        g[rows, :] = s
        gate_tile(lens, at, own, mod, s, br2, 1, sums, b2, width)

    tiles(frames, last)


def backward_attention(lens, tlens, keep, mod, text, g, b2, xh1, m1, packed, qa1, att1, br1, xh2, m2, mem, qa2, att2, rs,
                       wsp, wso, wcq, wcm, wco, sums_in,
                       lat_grad, dsp, dso, dcq, dcm, dco, sums,
                       aq, aks, akc, datt, dq, dmem, dpack, acc, tmp, stage):
    frames, width = g.shape
    fill_masks(lens, tlens, aq, aks, akc)
    sums[...] = sums_in[...]
    big_tn(b2, att2, dco, width)
    datt[...] = nn(b2[...], wco[...]).astype(BF16)
    attention_backward(qa2, mem, 0, width, akc, att2, datt, dq, dmem, 0, width, acc)
    big_tn(dq, m2, dcq, width)
    big_tn(dmem, text, dcm, width)
    tmp[...] = nn(dq[...], wcq[...])

    def middle(at):
        rows = pl.ds(at, TILE)
        own = owners_column(lens, at, TILE)
        s = g[rows, :] + norm_back_tile(lens, at, own, mod, tmp[rows, :], xh2, rs, 1, sums, width)
        stage[rows, :] = s
        gate_tile(lens, at, own, mod, s, br1, 0, sums, dq, width)

    tiles(frames, middle)
    big_tn(dq, att1, dso, width)
    datt[...] = nn(dq[...], wso[...]).astype(BF16)
    attention_backward(qa1, packed, width, 2 * width, aks, att1, datt, dpack, dpack, width, 2 * width, acc)
    big_tn(dpack, m1, dsp, width)
    tmp[...] = nn(dpack[...], wsp[...])

    def last(at):
        rows = pl.ds(at, TILE)
        own = owners_column(lens, at, TILE)
        s = stage[rows, :] + norm_back_tile(lens, at, own, mod, tmp[rows, :], xh1, rs, 0, sums, width)
        lat_grad[rows, :] = pick(own, keep[0], keep[1], keep[2]) * s

    tiles(frames, last)


def sds(shape, kind=BF16):
    return jax.ShapeDtypeStruct(shape, kind)


VM = pl.BlockSpec(memory_space=pltpu.VMEM)
SM = pl.BlockSpec(memory_space=pltpu.SMEM)


def call(body, scalars, ins, outs, scratch, flops):
    cost = pl.CostEstimate(flops=int(flops), bytes_accessed=int(3e7), transcendentals=0)
    return pl.pallas_call(
        body,
        out_shape=outs,
        in_specs=[SM] * len(scalars) + [VM] * len(ins),
        out_specs=[VM] * len(outs),
        scratch_shapes=scratch,
        cost_estimate=cost,
        compiler_params=pltpu.CompilerParams(vmem_limit_bytes=62 * MIB),
    )(*scalars, *ins)


def run_forward(lens, tlens, keep, loud, mod, lat, noi, text, wsp, wso, wcq, wcm, wco, wup, wdn):
    t, d = lat.shape
    x = text.shape[0]
    wide = HEADS * PAIR
    a = call(forward_attention, (lens, tlens, keep, loud), (mod, lat, noi, text, wsp, wso, wcq, wcm, wco),
             [sds((t, d), F32), sds((t, d)), sds((t, d)), sds((t, 3 * d)), sds((t, wide)), sds((t, d)), sds((t, d)),
              sds((t, d)), sds((t, d)), sds((x, 2 * d)), sds((t, wide)), sds((t, d)), sds((t, d)), sds((t, 128), F32)],
             [pltpu.VMEM((t, PAIR), BF16), pltpu.VMEM((t, PAIR), BF16), pltpu.VMEM((x, PAIR), BF16),
              pltpu.VMEM((t, d), BF16), pltpu.VMEM((t, d), F32)], 3e10)
    ff = wup.shape[0]
    b = call(forward_ff, (lens,), (mod, a[0], wup, wdn),
             [sds((t, d)), sds((t, d)), sds((t, ff)), sds((t, ff)), sds((t, d)), sds((t, d)), sds((t, 128), F32)],
             [pltpu.VMEM((t, d), F32)], 1e10)
    return a, b


def run_backward(lens, tlens, keep, mod, text, cot, a, b, wsp, wso, wcq, wcm, wco, wup, wdn):
    t, d = cot.shape
    x = text.shape[0]
    stream, xh1, m1, packed, qa1, att1, br1, xh2, m2, mem, qa2, att2, br2, rs = a
    xh3, m3, act, slope, br3, out, rs3 = b
    ff = wup.shape[0]
    g, b2, dwd, dwu, sums = call(
        partial(lambda lens, mod, cot, br3, act, slope, xh3, m3, rs, wup, wdn, br2, g, b2, dwd, dwu, sums, b3, ig, tmp:
                backward_ff(lens, mod, cot, br3, act, slope, xh3, m3, rs, wup, wdn, g, b2, br2, dwd, dwu, sums, b3, ig, tmp)),
        (lens,), (mod, cot, br3, act, slope, xh3, m3, rs3, wup, wdn, br2),
        [sds((t, d), F32), sds((t, d)), sds((d, ff)), sds((ff, d)), sds((16, 9 * d), F32)],
        [pltpu.VMEM((t, d), BF16), pltpu.VMEM((t, ff), BF16), pltpu.VMEM((t, d), F32)], 3e10)
    lat_grad, dsp, dso, dcq, dcm, dco, sums = call(
        backward_attention, (lens, tlens, keep),
        (mod, text, g, b2, xh1, m1, packed, qa1, att1, br1, xh2, m2, mem, qa2, att2, rs, wsp, wso, wcq, wcm, wco, sums),
        [sds((t, d), F32), sds((3 * d, d)), sds((d, d)), sds((d, d)), sds((2 * d, d)), sds((d, d)), sds((16, 9 * d), F32)],
        [pltpu.VMEM((t, PAIR), BF16), pltpu.VMEM((t, PAIR), BF16), pltpu.VMEM((x, PAIR), BF16),
         pltpu.VMEM((t, d), BF16), pltpu.VMEM((t, d), BF16), pltpu.VMEM((x, 2 * d), BF16), pltpu.VMEM((t, 3 * d), BF16),
         pltpu.VMEM((PAIR, t), F32), pltpu.VMEM((t, d), F32), pltpu.VMEM((t, d), F32)], 6e10)
    return out, lat_grad, dsp, dso, dcq, dcm, dco, dwu, dwd, sums

MESH = pl.DeviceIdType.MESH
ANY = pl.BlockSpec(memory_space=pl.ANY)
UNITS = (
    (0, 0, 1, 0, 2, 0), (1, 0, 1, 0, 2, 1),
    (2, 0, 2 / 3, 0, 2, 0), (2, 2 / 3, 1 / 3, 0, 2, 1),
    (3, 0, 1, 0, 2, 1), (4, 0, 1, 0, 2, 0),
    (5, 0, 1 / 2, 0, 2, 0), (5, 1 / 2, 1 / 2, 0, 2, 1),
    (6, 0, 1, 0, 2, 1),
    (7, 0, 1 / 2, 0, 2, 0), (7, 1 / 2, 1 / 2, 0, 2, 1),
    (8, 0, 1, 0, 1, 0), (8, 0, 1, 1, 1, 1),
)


class Place:
    def __init__(self, depth):
        dp, fsdp = lax.axis_index("dp"), lax.axis_index("fsdp")
        self.depth = depth
        self.z, self.y = dp // 2, dp % 2
        self.x, self.c = fsdp // 2, fsdp % 2

    def at(self, z=None, y=None, x=None, c=None):
        z = self.z if z is None else z
        y = self.y if y is None else y
        x = self.x if x is None else x
        c = self.c if c is None else c
        return (z * 2 + y, x * 2 + c)

    def other_z(self, k):
        return lax.rem(self.z + k, self.depth)

    def barrier(self):
        bar = pltpu.get_barrier_semaphore()
        ids = [self.at(z=self.other_z(k)) for k in range(1, self.depth)]
        ids += [self.at(y=1 - self.y), self.at(x=1 - self.x), self.at(c=1 - self.c)]
        for d in ids:
            pl.semaphore_signal(bar, inc=1, device_id=d, device_id_type=MESH)
        pl.semaphore_wait(bar, len(ids))


class Counter:
    def __init__(self, send, recv):
        self.send, self.recv, self.n = send, recv, 0

    def remote(self, src, dst, device):
        n, self.n = self.n, self.n + 1
        return pltpu.make_async_remote_copy(src_ref=src, dst_ref=dst, send_sem=self.send.at[n], recv_sem=self.recv.at[n],
                                            device_id=device, device_id_type=MESH)

    def local(self, src, dst):
        n, self.n = self.n, self.n + 1
        return pltpu.make_async_copy(src, dst, self.send.at[n])


def unit_shape(unit, shapes):
    w, r0, nr, l0, nl, route = unit
    c8, share = shapes[w]
    half = c8 // 2
    return w, int(round(half * r0)), int(round(half * nr)), l0 * share, nl * share, route, half


class GatherUnit:
    def __init__(self, unit, shapes, place, count, block, out):
        w, r0, n, l0, nl, route, half = unit_shape(unit, shapes)
        self.p, p = place, place
        self.route = route
        share = shapes[w][1]
        row = pl.ds(pl.multiple_of(p.c * half + r0, 16), n)
        other = pl.ds(pl.multiple_of((1 - p.c) * half + r0, 16), n)
        lane = lambda x: pl.ds(pl.multiple_of(x * (2 * share) + l0, 128), nl)
        own = block[w].at[pl.ds(r0, n), pl.ds(l0, nl)]
        o = out[w]
        mine, theirs = lane(p.x), lane(1 - p.x)
        D = p.depth
        dst = o.at[p.z, p.y, row, mine]
        self.local = count.local(own, dst)
        self.zs = [count.remote(own, dst, p.at(z=p.other_z(k))) for k in range(1, D)]
        self.second, self.third = [], []
        for k in range(D):
            zz = p.z if k == 0 else p.other_z(D - k)
            if route == 0:
                a = o.at[zz, p.y, row, mine]
                self.second.append(count.remote(own if k == 0 else a, a, p.at(y=1 - p.y)))
            else:
                a = o.at[zz, p.y, row, mine]
                self.second.append(count.remote(own if k == 0 else a, a, p.at(x=1 - p.x)))
        for k in range(D):
            zz = p.z if k == 0 else p.other_z(D - k)
            if route == 0:
                a = o.at[zz, :, row, mine]
                self.third.append(count.remote(a, a, p.at(x=1 - p.x)))
            else:
                lanes = pl.ds(l0, nl)
                a = [o.at[zz, p.y, row, lane(i)] for i in range(2)]
                self.third.append([count.remote(v, v, p.at(y=1 - p.y)) for v in a])
        sib = [o.at[:, :, row, lane(i)] for i in range(2)]
        self.sib = [count.remote(v, v, p.at(c=1 - p.c)) for v in sib]

    def flat(self, v):
        return v if isinstance(v, list) else [v]

    def begin(self):
        self.local.start()
        for cp in self.zs:
            cp.start()
        self.second[0].start()

    def step_z(self):
        for k, cp in enumerate(self.zs, 1):
            cp.wait_recv()
            self.second[k].start()
        self.local.wait()

    def step_second(self):
        for k, cp in enumerate(self.second):
            cp.wait_recv()
            for c in self.flat(self.third[k]):
                c.start()

    def step_third(self):
        for v in self.third:
            for c in self.flat(v):
                c.wait_recv()
        for c in self.sib:
            c.start()

    def finish(self):
        for c in self.sib:
            c.wait()
        for c in self.zs + self.second + [c for v in self.third for c in self.flat(v)]:
            c.wait_send()


def gather_body(depth, shapes, *refs):
    nw = len(shapes)
    ins, outs = refs[:nw], refs[nw : 2 * nw]
    rest = refs[2 * nw :]
    turned, landed, block = rest[:nw], rest[nw : 2 * nw], rest[2 * nw : 3 * nw]
    send, recv = rest[3 * nw :]
    p = Place(depth)
    count = Counter(send, recv)
    swaps = []
    for w, (c8, share) in enumerate(shapes):
        turned[w][...] = ins[w][...].T
    p.barrier()
    for w, (c8, share) in enumerate(shapes):
        half = c8 // 2
        theirs = turned[w].at[pl.ds(pl.multiple_of((1 - p.c) * half, 16), half), :]
        swaps.append(count.remote(theirs, landed[w], p.at(c=1 - p.c)))
        swaps[-1].start()
    for w, (c8, share) in enumerate(shapes):
        half = c8 // 2
        swaps[w].wait_recv()
        own = turned[w][pl.ds(pl.multiple_of(p.c * half, 16), half), :]
        got = landed[w][...]
        first = p.c == 0
        block[w][...] = jnp.concatenate([jnp.where(first, own, got), jnp.where(first, got, own)], axis=1)
    units = [GatherUnit(u, shapes, p, count, block, outs) for u in UNITS]
    n = len(units)
    ahead = 2
    begun = 0
    for t in range(n + 2):
        while begun < min(n, t + ahead):
            units[begun].begin()
            begun += 1
        if t < n:
            units[t].step_z()
        if 0 <= t - 1 < n:
            units[t - 1].step_second()
        if 0 <= t - 2 < n:
            units[t - 2].step_third()
    for u in units:
        u.finish()
    for s in swaps:
        s.wait_send()


def copies_of_gather(depth, nw):
    return nw + sum(1 + (depth - 1) + depth + depth * (1 if u[5] == 0 else 2) + 2 for u in UNITS)


def gather(mesh, weights):
    depth = mesh.shape["dp"] // 2
    nx = mesh.shape["fsdp"] // 2
    shapes = [(w.shape[1], w.shape[0]) for w in weights]
    ns = copies_of_gather(depth, len(weights))
    outs = [sds((depth, 2, c8, share * 2 * nx)) for c8, share in shapes]
    full = pl.pallas_call(
        partial(gather_body, depth, shapes),
        out_shape=outs,
        in_specs=[VM] * len(weights),
        out_specs=[ANY] * len(weights),
        scratch_shapes=[pltpu.VMEM((c8, share), BF16) for c8, share in shapes]
        + [pltpu.VMEM((c8 // 2, share), BF16) for c8, share in shapes]
        + [pltpu.VMEM((c8 // 2, 2 * share), BF16) for c8, share in shapes]
        + [pltpu.SemaphoreType.DMA((ns,)), pltpu.SemaphoreType.DMA((ns,))],
        compiler_params=pltpu.CompilerParams(collective_id=0, has_side_effects=True, vmem_limit_bytes=40 * MIB),
    )(*weights)
    return [f.reshape(-1, f.shape[-1]) for f in full]


SUM_UNITS = (
    (6, 0, 1, 0, 1, 0), (6, 0, 1, 1, 1, 1), (5, 0, 1 / 2, 0, 2, 0), (5, 1 / 2, 1 / 2, 0, 2, 1),
    (4, 0, 1, 0, 2, 0), (2, 0, 1, 0, 2, 1), (3, 0, 1 / 2, 0, 2, 0), (3, 1 / 2, 1 / 2, 0, 2, 1),
    (1, 0, 1, 0, 2, 1), (0, 0, 2 / 3, 0, 2, 0), (0, 2 / 3, 1 / 3, 0, 2, 1),
)


def each(count, fn):
    def step(i, carry):
        fn(i)
        return carry

    lax.fori_loop(0, count, step, 0)


def plus(a, b):
    return (a.astype(F32) + b.astype(F32)).astype(BF16)


class SumUnit:
    def __init__(self, unit, shapes, place, count, grads, held, cores, first, second, lasts, final):
        w, r0, n, l0, nl, route, half = unit_shape(unit, shapes)
        self.p, self.route, self.D = place, route, place.depth
        p, D = place, place.depth
        share = shapes[w][1]
        row = pl.ds(pl.multiple_of(p.c * half + r0, 16), n)
        other = pl.ds(pl.multiple_of((1 - p.c) * half + r0, 16), n)
        self.held, self.cores, self.first, self.second, self.lasts = held, cores, first, second, lasts
        self.final, self.at = final[w], (pl.ds(r0, n), pl.ds(l0, nl))
        self.loads, self.swaps = [], []
        for i in range(2):
            lane = pl.ds(i * 2 * share + l0, nl)
            self.loads.append(count.local(grads[w].at[:, :, row, lane], held.at[i]))
            self.swaps.append(count.remote(grads[w].at[:, :, other, lane], cores.at[i], p.at(c=1 - p.c)))
        x, y, z = p.x, p.y, p.z
        if route == 0:
            self.one = count.remote(held.at[1 - x], first, p.at(x=1 - x))
            self.two = count.remote(held.at[x, :, 1 - y], second, p.at(y=1 - y))
        else:
            self.one = count.remote(held.at[:, :, 1 - y], first, p.at(y=1 - y))
            self.two = count.remote(held.at[1 - x, :, y], second, p.at(x=1 - x))
        self.three = []
        for k in range(1, D):
            zz = p.other_z(k)
            self.three.append(count.remote(held.at[x, zz, y], lasts.at[k - 1], p.at(z=zz)))

    def begin(self):
        for c in self.loads + self.swaps:
            c.start()

    def step_core(self):
        for c in self.loads:
            c.wait()
        for c in self.swaps:
            c.wait_recv()
        x, y, D = self.p.x, self.p.y, self.D
        held, cores = self.held, self.cores
        if self.route == 0:
            def add(xx):
                def fn(i):
                    held[xx, i // 2, i % 2] = plus(held[xx, i // 2, i % 2], cores[xx, i // 2, i % 2])
                each(2 * D, fn)
            add(1 - x)
            self.one.start()
            add(x)
        else:
            def add(yy):
                def fn(i):
                    held[i // D, i % D, yy] = plus(held[i // D, i % D, yy], cores[i // D, i % D, yy])
                each(2 * D, fn)
            add(1 - y)
            self.one.start()
            add(y)

    def step_one(self):
        self.one.wait_recv()
        x, y, D = self.p.x, self.p.y, self.D
        held, got = self.held, self.first
        if self.route == 0:
            def add(yy):
                def fn(i):
                    held[x, i, yy] = plus(held[x, i, yy], got[i, yy])
                each(D, fn)
            add(1 - y)
            self.two.start()
            add(y)
        else:
            def add(xx):
                def fn(i):
                    held[xx, i, y] = plus(held[xx, i, y], got[xx, i])
                each(D, fn)
            add(1 - x)
            self.two.start()
            add(x)

    def step_two(self):
        self.two.wait_recv()
        x, y = self.p.x, self.p.y
        held, got = self.held, self.second
        for k in range(1, self.D):
            zz = self.p.other_z(k)
            held[x, zz, y] = plus(held[x, zz, y], got[zz])
            self.three[k - 1].start()

    def step_three(self):
        for c in self.three:
            c.wait_recv()
        x, y, z = self.p.x, self.p.y, self.p.z
        total = self.held[x, z, y].astype(F32) + self.second[z].astype(F32)
        for k in range(self.D - 1):
            total += self.lasts[k].astype(F32)
        self.final[self.at] = total

    def finish(self):
        for c in self.swaps + [self.one, self.two] + self.three:
            c.wait_send()


def sum_scratch(shapes, depth, units):
    scratch = []
    for u in units:
        w, r0, n, l0, nl, route, half = unit_shape(u, shapes)
        scratch.append(pltpu.VMEM((2, depth, 2, n, nl), BF16))
        scratch.append(pltpu.VMEM((2, depth, 2, n, nl), BF16))
        scratch.append(pltpu.VMEM((depth, 2, n, nl) if route == 0 else (2, depth, n, nl), BF16))
        scratch.append(pltpu.VMEM((depth, n, nl), BF16))
        scratch.append(pltpu.VMEM((depth - 1, n, nl), BF16))
    return scratch


class LastSwap:
    def __init__(self, w, shapes, place, count, final, part, out):
        self.c8, self.share = shapes[w]
        self.p, self.final, self.part, self.out = place, final[w], part[w], out[w]
        half = self.c8 // 2
        self.rows = pl.ds(pl.multiple_of(place.c * half, 16), half)
        self.copy = count.remote(self.part, self.out.at[self.rows, :], place.at(c=1 - place.c))

    def begin(self):
        total = self.final[...]
        low, high = total[:, : self.share], total[:, self.share :]
        first = self.p.c == 0
        self.part[...] = jnp.where(first, high, low)
        self.copy.start()
        self.out[self.rows, :] = jnp.where(first, low, high)

    def finish(self):
        self.copy.wait()


def reduce_body(depth, shapes, *refs):
    nw = len(shapes)
    grads, outs, rest = refs[:nw], refs[nw : 2 * nw], refs[2 * nw :]
    final, part, rest = rest[:nw], rest[nw : 2 * nw], rest[2 * nw :]
    send, recv = rest[-2:]
    p = Place(depth)
    count = Counter(send, recv)
    p.barrier()
    units = [SumUnit(u, shapes, p, count, grads, *rest[5 * i : 5 * i + 5], final) for i, u in enumerate(SUM_UNITS)]
    swaps = [LastSwap(w, shapes, p, count, final, part, outs) for w in range(nw)]
    n = len(units)
    last = {u[0]: i for i, u in enumerate(SUM_UNITS)}
    for u in units:
        u.begin()
    for t in range(n + 3):
        if t < n:
            units[t].step_core()
        if 0 <= t - 1 < n:
            units[t - 1].step_one()
        if 0 <= t - 2 < n:
            units[t - 2].step_two()
        if 0 <= t - 3 < n:
            units[t - 3].step_three()
            for w, i in last.items():
                if i == t - 3:
                    swaps[w].begin()
    for u in units:
        u.finish()
    for s in swaps:
        s.finish()


def turn_body(nw, *refs):
    for w in range(nw):
        refs[nw + w][...] = refs[w][...].T


def reduce(mesh, grads):
    depth, ncore = mesh.shape["dp"] // 2, mesh.shape["fsdp"]
    shapes = [(g.shape[0] // (2 * depth), g.shape[1] // ncore) for g in grads]
    ns = sum(4 + 2 + depth - 1 for _ in SUM_UNITS) + len(shapes)
    shares = pl.pallas_call(
        partial(reduce_body, depth, shapes),
        out_shape=[sds(s, F32) for s in shapes],
        in_specs=[ANY] * len(grads),
        out_specs=[VM] * len(grads),
        scratch_shapes=[pltpu.VMEM((c8 // 2, 2 * share), F32) for c8, share in shapes]
        + [pltpu.VMEM((c8 // 2, share), F32) for c8, share in shapes]
        + sum_scratch(shapes, depth, SUM_UNITS)
        + [pltpu.SemaphoreType.DMA((ns,)), pltpu.SemaphoreType.DMA((ns,))],
        compiler_params=pltpu.CompilerParams(collective_id=1, has_side_effects=True, vmem_limit_bytes=50 * MIB),
    )(*[g.reshape(depth, 2, c8, g.shape[1]) for g, (c8, _) in zip(grads, shapes)])
    return pl.pallas_call(
        partial(turn_body, len(shapes)),
        out_shape=[sds(s[::-1], F32) for s in shapes],
        in_specs=[VM] * len(grads),
        out_specs=[VM] * len(grads),
    )(*shares)


HIGHEST = lax.Precision.HIGHEST
BOTH = ("dp", "fsdp")


def high_dot(left, right, lc=1, rc=0):
    return lax.dot_general(left, right, (((lc,), (rc,)), ((), ())), precision=HIGHEST, preferred_element_type=F32)


def plan(step_row):
    levels = step_row.astype(F32)
    cumulative = jnp.cos(0.5 * math.pi * (levels / 1000.0 + 0.008) / 1.008) ** 2
    half_width = FREQ // 2
    frequency = jnp.exp(-math.log(10000.0) * jnp.arange(half_width, dtype=F32) / half_width)
    angles = levels[:, None] * frequency[None, :]
    embedding = jnp.concatenate([jnp.cos(angles), jnp.sin(angles)], axis=1)
    return jnp.sqrt(cumulative), jnp.sqrt(1.0 - cumulative), embedding


def silu_slope(v):
    s = jax.nn.sigmoid(v)
    return s * (1.0 + v * (1.0 - s))


def plain_gather(w):
    part = lax.all_gather(w, "fsdp", axis=0, tiled=True)
    return lax.all_gather(part, "dp", axis=1, tiled=True).T


def plain_reduce(g):
    part = lax.psum_scatter(g.T, "dp", scatter_dimension=1, tiled=True).astype(BF16)
    return lax.psum_scatter(part, "fsdp", scatter_dimension=0, tiled=True).astype(F32)


def fits(mesh, weights):
    if mesh.shape["fsdp"] != 4 or mesh.shape["dp"] % 2:
        return False
    return all(w.shape[0] * 2 % 128 == 0 and w.shape[1] % 32 == 0 for w in weights)


def columns(values, index, width):
    return lax.dynamic_slice_in_dim(values, index * width, width, axis=1)


def body(mesh, latents, noise_draw, text_states, time_steps, item_lengths, text_lengths, cotangent, time_in, time_out,
         modulation, *others):
    ndp, nfs = mesh.shape["dp"], mesh.shape["fsdp"]
    i, j = lax.axis_index("dp"), lax.axis_index("fsdp")
    width = latents.shape[1]
    items = time_steps.shape[0]
    sent = (time_in, time_out) + others
    direct = fits(mesh, sent)
    full = gather(mesh, sent) if direct else [plain_gather(w) for w in sent]
    t_in, t_out = full[0].astype(F32), full[1].astype(F32)
    weights = full[2:]

    all_steps = lax.all_gather(time_steps, BOTH, axis=0, tiled=True)
    keep, loud, _ = plan(time_steps)
    _, _, embedding = plan(all_steps)
    pre_one = high_dot(embedding, t_in, 1, 1)
    hidden = jax.nn.silu(pre_one)
    pre_two = high_dot(hidden, t_out, 1, 1)
    cond_low = jax.nn.silu(pre_two).astype(BF16)
    deep, wide = modulation.shape
    mine = columns(cond_low, j, deep)
    part = jnp.dot(mine, modulation, preferred_element_type=F32).reshape(ndp, nfs * items, wide)
    part = lax.psum_scatter(part, "fsdp", scatter_dimension=1, tiled=True)
    rows = lax.all_to_all(part, "dp", 0, 0, tiled=True)
    mod = jnp.pad(rows.transpose(1, 0, 2).reshape(items, -1), ((0, 8 - items), (0, 0)))

    text = text_states.reshape(-1, width)
    a, b = run_forward(item_lengths, text_lengths, keep, loud, mod, latents, noise_draw, text, *weights)
    out, lat_grad, *grads, sums = run_backward(item_lengths, text_lengths, keep, mod, text, cotangent, a, b, *weights)
    shares = reduce(mesh, grads) if direct else [plain_reduce(g) for g in grads]

    sent_sums = sums[:items].astype(BF16).reshape(items, ndp, wide).transpose(1, 0, 2)
    got = lax.all_to_all(sent_sums, "dp", 0, 0, tiled=True)
    got = lax.all_gather(got, "fsdp", axis=1, tiled=True).reshape(-1, wide)
    modulation_grad = lax.dot_general(mine, got, (((0,), (0,)), ((), ())), preferred_element_type=F32)
    back = lax.dot_general(got, modulation, (((1,), (1,)), ((), ())), preferred_element_type=F32)
    back = lax.all_gather(lax.psum(back, "dp"), "fsdp", axis=1, tiled=True)
    back_two = back * silu_slope(pre_two)
    back_one = high_dot(back_two, t_out) * silu_slope(pre_one)
    time_in_grad = high_dot(columns(embedding, j, time_in.shape[0]), columns(back_one, i, time_in.shape[1]), 0, 0)
    time_out_grad = high_dot(columns(hidden, j, time_out.shape[0]), columns(back_two, i, time_out.shape[1]), 0, 0)
    return (out, lat_grad, time_in_grad, time_out_grad, modulation_grad, *shares)


def solution(mesh):
    rows, weight = P(BOTH, None), P("fsdp", "dp")
    return jax.shard_map(
        partial(body, mesh),
        mesh=mesh,
        in_specs=(rows, rows, P(BOTH, None, None), P(BOTH), rows, P(BOTH), rows) + (weight,) * 10,
        out_specs=(rows, rows) + (weight,) * 10,
        check_vma=False,
    )
```

time: 2100 us -> 624 us (0.30)
  waiting for transfers between devices: 1340 us -> 93.7 us
  matrix products: 460 us -> 9.77 us
  Pallas kernels: 0 us -> 406 us
  local copies, waits for them, and re-layouts: 111 us -> 27.5 us
  other arithmetic: 58.3 us -> 1.08 us
  blocking collectives: 92.9 us -> 55.7 us
    reduce_scatter x11 -> x0, waiting for transfers between devices: 735 us -> none  [the longest x1 183 us: body(): lax.psum_scatter(modulation_grad.astype(jnp.bfloat16), 'dp', scatter_dime...]
    dot_general x200 -> x8, matrix products: 460 us -> 9.77 us  [the longest x5 7.55 us: high_dot(): lax.dot_general(left, right, (((lc,), (rc,)), ((), ())), precision=HIGHES...]
    pallas_call x0 -> x7, Pallas kernels: none -> 406 us  [the longest x4 182 us: call(): pl.pallas_call(body, out_shape=outs, in_specs=[SM] * len(scalars) + [VM]...]
    all_gather x10 -> x0, waiting for transfers between devices: 333 us -> none  [the longest x1 145 us: body(): lax.all_gather(row_parts[2], 'dp', axis=1, tiled=True)]
    unnamed x39 -> x3, waiting for transfers between devices: 274 us -> 19 us
    all_gather x10 -> x2, blocking collectives: 92.9 us -> 13.7 us  [the longest x1 7.28 us: body(): got = lax.all_gather(got, 'fsdp', axis=1, tiled=True).reshape(-1, wide)]
    psum x0 -> x1, waiting for transfers between devices: none -> 68.1 us  [body(): back = lax.all_gather(lax.psum(back, 'dp'), 'fsdp', axis=1, tiled=True)]
    unnamed x181 -> x54, local copies, waits for them, and re-layouts: 72.3 us -> 21.2 us
  transfers between devices with their start and end apart: 30 -> 4, of which waited for: 27 -> 3; matrix products, arithmetic and copies ran while one was open for 13% -> 1% of each run, Pallas kernels for 0% -> 18%
where the time goes in v1:
time: 624 us; the launch traced here: 618 us
  Pallas kernels  406 us (65%)
  waiting for transfers between devices  93.7 us (15%)
  blocking collectives  55.7 us (9%)
  local copies, waits for them, and re-layouts  27.5 us (4%)
  between operations  14.8 us (2%)
  matrix products  9.77 us (2%)
  starting transfers between devices  9.46 us (2%)
    pallas_call x4, Pallas kernels, call(): pl.pallas_call(body, out_shape=outs, in_specs=[SM] * len(scalars) + [VM]...  182 us
    pallas_call x1, Pallas kernels, gather(): pl.pallas_call(partial(gather_body, depth, shapes), out_shape=outs, in_sp...  112 us
    pallas_call x1, Pallas kernels, reduce(): pl.pallas_call(partial(reduce_body, depth, shapes), out_shape=[sds(s, F32...  109 us
    psum x1, waiting for transfers between devices, body(): back = lax.all_gather(lax.psum(back, 'dp'), 'fsdp', axis=1, tiled=True)  68.1 us
    unnamed x1, blocking collectives  42 us
    unnamed x54, local copies, waits for them, and re-layouts  21.2 us
    unnamed x3, waiting for transfers between devices  19 us
  transfers between devices with their start and end apart: 4, of which 3 were waited for; matrix products, arithmetic and copies ran while one was open for 1% of the time, Pallas kernels for 18%

profile of v1, /device:TPU:0, one launch (start us, length us, event | category | flops | bytes accessed | tf_op | source)
XLA Modules:
  0.0 618.1 jit_solution(3109183709227996606)
XLA Ops:
  8.1 42.0 %all-reduce.1 = s32[96]{0:T(128)S(1)} all-reduce(s32[96]{0:T(128)S(1)} %dynamic-update-slice), channel_id=1, replica_groups=mesh['dp'=8,'fsdp'=4] {'dp','fsdp'}, use_global_device_ids=true, to_apply=%add.1 | all-reduce | flops 96 | bytes 768
  58.1 111.6 %shard_map.256 = (bf16[4,2,96,256]{3,2,1,0:T(8,128)(2,1)S(1)}, bf16[4,2,96,768]{3,2,1,0:T(8,128)(2,1)S(1)}, bf16[4,2,288,768]{3,2,1,0:T(8,128)(2,1)S(1)}, bf16[4...) custom-call(bf16[64,96]{1,0:T(8,128)(2,1)S(1)} %copy-done.17, ...), custom_call_target="tpu_custom_call" | custom-call | tf_op jit(solution)/shard_map/pallas_call | solution.py:647
  169.7 1.4 copy-done.19
  173.2 1.8 fusion.20
  175.0 1.2 add_divide_fusion
  177.5 19.0 %reduce-scatter.4.cloned.1.call-done = f32[8,3,864]{2,0,1:T(8,128)} async-done(((f32[8,12,864]{2,0,1:T(8,128)}), f32[8,3,864]{2,0,1:T(8,128)}) %reduce-scatter.4.cloned.1.call-update) | async-done | bytes 82960
  196.5 1.6 copy.44
  198.0 6.0 all-to-all-start
  204.6 6.6 %all-to-all-done = f32[8,3,864]{2,1,0:T(4,128)S(1)} async-done(((f32[8,3,864]{2,1,0:T(4,128)}), f32[8,3,864]{2,1,0:T(4,128)S(1)}, u32[]{:S(2)}, u32[]{:S(2)}) %all-to-all-start) | async-done | bytes 82976 | tf_op jit(solution)/shard_map/all_to_all | solution.py:937
  212.1 57.0 %shard_map.257 = (f32[768,768]{1,0:T(8,128)}, bf16[768,768]{1,0:T(8,128)(2,1)}, bf16[768,768]{1,0:T(8,128)(2,1)}, bf16[768,2304]{1,0:T(8,128)(2,1)}, bf16[768,15...) custom-call(s32[1,3]{1,0:T(1,128)} %lens.7, ...), custom_call_target="tpu_custom_call" | custom-call | flops 30000001024 | bytes 30000000 | tf_op jit(solution)/shard_map/pallas_call | solution.py:413
  269.1 25.1 %shard_map.258 = (bf16[768,768]{1,0:T(8,128)(2,1)}, bf16[768,768]{1,0:T(8,128)(2,1)}, bf16[768,3072]{1,0:T(8,128)(2,1)}, bf16[768,3072]{1,0:T(8,128)(2,1)}, bf16...) custom-call(s32[1,3]{1,0:T(1,128)} %lens.7, f32[8,6912]{1,0:T(8,128)} %pad.4.mod, ...), custom_call_target="tpu_custom_call" | custom-call | flops 10000000000 | bytes 30000000 | tf_op jit(solution)/shard_map/pallas_call | solution.py:413
  294.2 33.7 %shard_map.259 = (f32[768,768]{1,0:T(8,128)}, bf16[768,768]{1,0:T(8,128)(2,1)}, bf16[768,3072]{1,0:T(8,128)(2,1)}, bf16[3072,768]{1,0:T(8,128)(2,1)}, f32[16,6912]{1,0:T(8,128)}) custom-call(s32[1,3]{1,0:T(1,128)} %lens.7, f32[8,6912]{1,0:T(8,128)} %pad.4.mod, bf16[768,768]{1,0:T(8,128)(2,1)} %cot.1, bf16[768,768]{1,0:T(8,128)(2,1)} %get-tuple-element.79.br3, ...), custom_call_target="tpu_custom_call" | custom-call | flops 30000001024 | bytes 30000000 | tf_op jit(solution)/shard_map/pallas_call | solution.py:413
  327.9 66.7 %shard_map.260 = (f32[768,768]{1,0:T(8,128)}, bf16[2304,768]{1,0:T(8,128)(2,1)}, bf16[768,768]{1,0:T(8,128)(2,1)}, bf16[768,768]{1,0:T(8,128)(2,1)}, bf16[1536,7...) custom-call(s32[1,3]{1,0:T(1,128)} %lens.7, s32[3]{0:T(128)} %tlens.3, f32[3]{0:T(128)} %get-tuple-element.177.keep, ...), custom_call_target="tpu_custom_call" | custom-call | flops 60000002048 | bytes 30000000 | tf_op jit(solution)/shard_map/pallas_call | solution.py:413
  396.3 3.3 all-to-all-start.1
  399.8 1.3 copy-done.1
  401.0 1.3 copy-done.2
  402.3 109.4 %shard_map.261 = (f32[288,192]{1,0:T(8,128)S(1)}, f32[96,192]{1,0:T(8,128)S(1)}, f32[96,192]{1,0:T(8,128)S(1)}, f32[192,192]{1,0:T(8,128)S(1)}, f32[96,192]{1,0:...) custom-call(bf16[4,2,288,768]{3,2,1,0:T(8,128)(2,1)} %bitcast.49, bf16[4,2,96,768]{3,2,1,0:T(8,128)(2,1)S(1)} %bitcast.32, ...), custom_call_target="tpu_custom_call" | custom-call | tf_op jit(solution)/shard_map/pallas_call | solution.py:852
  516.4 2.7 shard_map.262
  519.1 1.9 copy.51
  521.0 7.3 %all_gather.10 = bf16[8,12,864]{2,0,1:T(8,128)(2,1)S(1)} all-gather(bf16[8,3,864]{2,0,1:T(8,128)(2,1)S(1)} %copy.47), channel_id=1, replica_groups=mesh['dp'=8,'fsdp'=4] {'fsdp'}, dimensions={1}, use_global_device_ids=true | all-gather | bytes 207360 | tf_op jit(solution)/shard_map/all_gather | solution.py:947
  530.4 68.1 %all-reduce.5.cloned.1.call-done = f32[96,192]{1,0:T(8,128)} async-done(((f32[96,192]{1,0:T(8,128)}), f32[96,192]{1,0:T(8,128)}) %all-reduce.5.cloned.1.call-update) | async-done | bytes 73744 | tf_op jit(solution)/shard_map/psum | solution.py:950
  599.6 6.4 %all_gather.11 = f32[96,768]{0,1:T(8,128)S(1)} all-gather(f32[96,192]{0,1:T(8,128)S(1)} %copy.49), channel_id=1, replica_groups=mesh['dp'=8,'fsdp'=4] {'fsdp'}, dimensions={1}, use_global_device_ids=true | all-gather | bytes 368640 | tf_op jit(solution)/shard_map/all_gather | solution.py:950
  607.0 2.0 fusion.2
  609.0 1.9 fusion.5
  (78 shorter events, 24.2 us)
Async XLA Ops:
  7.2 169.2 %copy-start = (bf16[192,864]{1,0:T(8,128)(2,1)S(1)}, bf16[192,864]{1,0:T(8,128)(2,1)}, u32[]{:S(2)}) copy-start(bf16[192,864]{1,0:T(8,128)(2,1)} %param.26) | copy-start | bytes 995332
  7.2 189.3 %reduce-scatter.4.cloned.1.call-start = ((), (), s32[]{:S(2)}) async-start(), calls=%async_computation.4 | async-start | bytes 430080
  51.5 0.9 copy-start.7
  52.4 0.9 copy-start.8
  53.3 0.9 copy-start.9
  54.2 0.8 copy-start.13
  55.0 0.8 copy-start.14
  55.8 0.8 copy-start.15
  56.6 0.8 copy-start.16
  57.4 0.7 copy-start.17
  169.7 1.4 copy-start.19
  171.2 1.1 copy-start.21
  172.2 1.0 copy-start.22
  173.2 3.0 copy-start.18
  173.2 3.0 copy-start.20
  175.0 1.4 copy-start.23
  176.6 27.5 %copy-start.24 = (s32[3]{0:T(128)S(1)}, s32[3]{0:T(128)}, u32[]{:S(2)}) copy-start(s32[3]{0:T(128)} %param.20) | copy-start | bytes 40
  198.0 13.2 %all-to-all-start = ((f32[8,3,864]{2,1,0:T(4,128)}), f32[8,3,864]{2,1,0:T(4,128)S(1)}, u32[]{:S(2)}, u32[]{:S(2)}) async-start(f32[8,3,864]{2,1,0:T(4,128)} %copy.44), calls=%async_computation | async-start | bytes 229376 | tf_op jit(solution)/shard_map/all_to_all | solution.py:937
  396.3 124.7 %all-to-all-start.1 = ((bf16[8,3,864]{2,1,0:T(4,128)(2,1)}), bf16[8,3,864]{2,1,0:T(4,128)(2,1)S(1)}, u32[]{:S(2)}, u32[]{:S(2)}) async-start(bf16[8,3,864]{2,1,0:T(4,128)(2,1)} %bitcast.31), calls=%async_computation.1 | async-start | bytes 114688 | tf_op jit(solution)/shard_map/all_to_all | solution.py:946
  399.7 198.9 %all-reduce.5.cloned.1.call-start = ((), (), s32[]{:S(2)}) async-start(), calls=%async_computation.3 | async-start | bytes 196608 | tf_op jit(solution)/shard_map/psum | solution.py:950
  399.7 1.3 copy-start.1
  401.0 1.3 copy-start.2
  511.7 0.7 copy-start.3
  513.1 0.7 copy-start.5
  (5 other events, 3.3 us)
Sparse Core Ops, SparseCore 0:
  177.6 18.7 reduce-scatter.3
  529.4 69.0 all-reduce.4

commit v2 on v1

--- a/solution.py
+++ b/solution.py
@@ -89,7 +89,16 @@
     return one, two, column - one - two
 
 
-def attention_forward(q, k, k_at, v_at, ak, aq, out, qaug):
+def in_parts(pair, pump, step=2):
+    if pump is None:
+        lax.fori_loop(0, PAIRS, pair, 0)
+        return
+    for first in range(0, PAIRS, step):
+        lax.fori_loop(first, first + step, pair, 0)
+        pump()
+
+
+def attention_forward(q, k, k_at, v_at, ak, aq, out, qaug, pump=None):
     frames = q.shape[0]
 
     def pair(p, carry):
@@ -124,10 +133,10 @@
             out[rows, lanes] = jnp.where(low, done[0], done[1]).astype(BF16)
         return carry
 
-    lax.fori_loop(0, PAIRS, pair, 0)
-
-
-def attention_backward(qaug, k, k_at, v_at, ak, att, datt, dq, dk, dk_at, dv_at, acc):
+    in_parts(pair, pump)
+
+
+def attention_backward(qaug, k, k_at, v_at, ak, att, datt, dq, dk, dk_at, dv_at, acc, pump=None):
     frames = att.shape[0]
     tall = k.shape[0]
     step = TILE if tall % TILE == 0 else PAIR
@@ -172,7 +181,7 @@
         dq[:, lanes] = (acc[...].T * FACTOR).astype(BF16)
         return carry
 
-    lax.fori_loop(0, PAIRS, pair, 0)
+    in_parts(pair, pump)
 
 
 def norm_tile(s):
@@ -218,12 +227,32 @@
     rs[rows, :] = jnp.where(lane == sub, r, rs[rows, :])
 
 
-def forward_attention(lens, tlens, keep, loud, mod, lat, noi, text, wsp, wso, wcq, wcm, wco,
+class NoLinks:
+    pump = None
+
+    def use(self, *names):
+        pass
+
+    def fetch(self, *names):
+        pass
+
+    def tick(self, n=1):
+        pass
+
+    def modulation(self):
+        pass
+
+    def done(self, *names):
+        pass
+
+
+def forward_attention(links, lens, tlens, keep, loud, mod, lat, noi, text, wsp, wso, wcq, wcm, wco,
                       stream, xh1, m1, packed, qa1, att1, br1, xh2, m2, mem, qa2, att2, br2, rs,
                       aq, aks, akc, qb, tmp):
     frames, width = lat.shape
     fill_masks(lens, tlens, aq, aks, akc)
     rs[...] = jnp.zeros_like(rs)
+    links.modulation()
 
     def start(at):
         rows = pl.ds(at, TILE)
@@ -234,8 +263,14 @@
         norm_into(s, rows, own, lens, mod, 0, xh1, m1, rs, width)
 
     tiles(frames, start)
+    links.done("xh1", "m1")
+    links.use("wsp")
     big_nt(m1, wsp, packed, width)
-    attention_forward(packed, packed, width, 2 * width, aks, aq, att1, qa1)
+    links.done("packed")
+    links.tick()
+    attention_forward(packed, packed, width, 2 * width, aks, aq, att1, qa1, links.pump)
+    links.done("att1", "qa1")
+    links.use("wso")
     tmp[...] = nt(att1[...], wso[...])
 
     def middle(at):
@@ -248,9 +283,15 @@
         norm_into(s, rows, own, lens, mod, 1, xh2, m2, rs, width)
 
     tiles(frames, middle)
+    links.done("br1", "xh2", "m2", "rs")
+    links.tick()
+    links.use("wcq", "wcm")
     big_nt(m2, wcq, qb, width)
     big_nt(text, wcm, mem, width)
-    attention_forward(qb, mem, 0, width, akc, aq, att2, qa2)
+    links.done("mem")
+    attention_forward(qb, mem, 0, width, akc, aq, att2, qa2, links.pump)
+    links.done("att2", "qa2")
+    links.use("wco")
     tmp[...] = nt(att2[...], wco[...])
 
     def last(at):
@@ -261,6 +302,7 @@
         stream[rows, :] = stream[rows, :] + expand(own, mod, 5, width) * br
 
     tiles(frames, last)
+    links.done("br2", "stream")
 
 
 GELU_A, GELU_B = math.sqrt(2.0 / math.pi), 0.044715
@@ -421,20 +463,24 @@
     )(*scalars, *ins)
 
 
-def run_forward(lens, tlens, keep, loud, mod, lat, noi, text, wsp, wso, wcq, wcm, wco, wup, wdn):
+def run_attention(lens, tlens, keep, loud, mod, lat, noi, text, wsp, wso, wcq, wcm, wco):
     t, d = lat.shape
     x = text.shape[0]
     wide = HEADS * PAIR
-    a = call(forward_attention, (lens, tlens, keep, loud), (mod, lat, noi, text, wsp, wso, wcq, wcm, wco),
-             [sds((t, d), F32), sds((t, d)), sds((t, d)), sds((t, 3 * d)), sds((t, wide)), sds((t, d)), sds((t, d)),
-              sds((t, d)), sds((t, d)), sds((x, 2 * d)), sds((t, wide)), sds((t, d)), sds((t, d)), sds((t, 128), F32)],
-             [pltpu.VMEM((t, PAIR), BF16), pltpu.VMEM((t, PAIR), BF16), pltpu.VMEM((x, PAIR), BF16),
-              pltpu.VMEM((t, d), BF16), pltpu.VMEM((t, d), F32)], 3e10)
+    return call(partial(forward_attention, NoLinks()), (lens, tlens, keep, loud),
+                (mod, lat, noi, text, wsp, wso, wcq, wcm, wco),
+                [sds((t, d), F32), sds((t, d)), sds((t, d)), sds((t, 3 * d)), sds((t, wide)), sds((t, d)), sds((t, d)),
+                 sds((t, d)), sds((t, d)), sds((x, 2 * d)), sds((t, wide)), sds((t, d)), sds((t, d)), sds((t, 128), F32)],
+                [pltpu.VMEM((t, PAIR), BF16), pltpu.VMEM((t, PAIR), BF16), pltpu.VMEM((x, PAIR), BF16),
+                 pltpu.VMEM((t, d), BF16), pltpu.VMEM((t, d), F32)], 3e10)
+
+
+def run_ff(lens, mod, stream, wup, wdn):
+    t, d = stream.shape
     ff = wup.shape[0]
-    b = call(forward_ff, (lens,), (mod, a[0], wup, wdn),
-             [sds((t, d)), sds((t, d)), sds((t, ff)), sds((t, ff)), sds((t, d)), sds((t, d)), sds((t, 128), F32)],
-             [pltpu.VMEM((t, d), F32)], 1e10)
-    return a, b
+    return call(forward_ff, (lens,), (mod, stream, wup, wdn),
+                [sds((t, d)), sds((t, d)), sds((t, ff)), sds((t, ff)), sds((t, d)), sds((t, d)), sds((t, 128), F32)],
+                [pltpu.VMEM((t, d), F32)], 1e10)
 
 
 def run_backward(lens, tlens, keep, mod, text, cot, a, b, wsp, wso, wcq, wcm, wco, wup, wdn):
@@ -485,11 +531,19 @@
         c = self.c if c is None else c
         return (z * 2 + y, x * 2 + c)
 
+    def flat(self, ncore):
+        return (self.z * 2 + self.y) * ncore + self.x * 2 + self.c
+
     def other_z(self, k):
         return lax.rem(self.z + k, self.depth)
 
-    def barrier(self):
+    def barrier(self, every=None):
         bar = pltpu.get_barrier_semaphore()
+        if every is not None:
+            for d in every:
+                pl.semaphore_signal(bar, inc=1, device_id=d, device_id_type=MESH)
+            pl.semaphore_wait(bar, len(every))
+            return
         ids = [self.at(z=self.other_z(k)) for k in range(1, self.depth)]
         ids += [self.at(y=1 - self.y), self.at(x=1 - self.x), self.at(c=1 - self.c)]
         for d in ids:
@@ -583,79 +637,260 @@
         for c in self.sib:
             c.start()
 
+    def settled(self):
+        for c in self.sib:
+            c.wait_recv()
+
     def finish(self):
-        for c in self.sib:
+        for c in self.sib + self.zs + self.second + [c for v in self.third for c in self.flat(v)]:
+            c.wait_send()
+
+
+def others(place, ndp, ncore):
+    total = ndp * ncore
+    me = place.flat(ncore)
+    found = []
+    for k in range(1, total):
+        t = lax.rem(me + k, total)
+        found.append((k, t, (t // ncore, t % ncore)))
+    return found
+
+
+def split_columns(values, index, parts, width):
+    picked = values[:, :width]
+    for i in range(1, parts):
+        picked = jnp.where(index == i, values[:, i * width : (i + 1) * width], picked)
+    return picked
+
+
+def three(value):
+    one = value.astype(BF16)
+    rest = value - one.astype(F32)
+    two = rest.astype(BF16)
+    return one, two, (rest - two.astype(F32)).astype(BF16)
+
+
+def fine_nt(left, right):
+    a, b, c = three(left)
+    return nt(a, right) + (nt(b, right) + nt(c, right))
+
+
+def fine_nn(left, right):
+    a, b, c = three(left)
+    return nn(a, right) + (nn(b, right) + nn(c, right))
+
+
+def silu(v):
+    return v / (1.0 + jnp.exp(-v))
+
+
+class ForwardLinks:
+    NAMES = ("tin", "tout", "wsp", "wso", "wcq", "wcm", "wco", "wup", "wdn")
+
+    def __init__(self, mesh, shapes, r):
+        self.ndp, self.ncore = mesh.shape["dp"], mesh.shape["fsdp"]
+        self.shapes, self.r = shapes, r
+        depth = self.ndp // 2
+        self.p = p = Place(depth)
+        self.count = count = Counter(r["send"], r["recv"])
+        self.every = others(p, self.ndp, self.ncore)
+        nw = len(shapes)
+        turned, landed, block = r["turned"], r["landed"], r["block"]
+        for w in range(nw):
+            turned[w][...] = r["shards"][w][...].T
+        me = p.flat(self.ncore)
+        r["eall"][me] = r["emb"][...]
+        p.barrier([d for _, _, d in self.every])
+        self.spread = []
+        swaps = []
+        for w, (c8, share) in enumerate(shapes):
+            half = c8 // 2
+            theirs = turned[w].at[pl.ds(pl.multiple_of((1 - p.c) * half, 16), half), :]
+            swaps.append(count.remote(theirs, landed[w], p.at(c=1 - p.c)))
+            swaps[-1].start()
+        for k, t, d in self.every:
+            c = count.remote(r["eall"].at[me], r["eall"].at[me], d)
+            c.start()
+            self.spread.append(c)
+        self.units = []
+        for w, (c8, share) in enumerate(shapes):
+            half = c8 // 2
+            swaps[w].wait_recv()
+            own = turned[w][pl.ds(pl.multiple_of(p.c * half, 16), half), :]
+            got = landed[w][...]
+            first = p.c == 0
+            block[w][...] = jnp.concatenate([jnp.where(first, own, got), jnp.where(first, got, own)], axis=1)
+            for u in UNITS:
+                if u[0] == w:
+                    self.units.append(GatherUnit(u, shapes, p, count, block, r["full"]))
+                    self.units[-1].begin()
+        self.swaps = swaps
+        self.now, self.fetched, self.waiting, self.saves = 0, {}, {}, []
+        self.pump = self.tick
+
+    def tick(self, n=1):
+        for _ in range(n):
+            t, self.now = self.now, self.now + 1
+            if t < len(self.units):
+                self.units[t].step_z()
+            if 0 <= t - 1 < len(self.units):
+                self.units[t - 1].step_second()
+            if 0 <= t - 2 < len(self.units):
+                self.units[t - 2].step_third()
+
+    def fetch(self, *names):
+        for name in names:
+            if name in self.fetched:
+                continue
+            w = self.NAMES.index(name)
+            mine = [i for i, u in enumerate(UNITS) if u[0] == w]
+            while self.now - 3 < mine[-1]:
+                self.tick()
+            for i in mine:
+                self.units[i].settled()
+            c8 = self.shapes[w][0]
+            self.fetched[name] = []
+            for z in range(self.p.depth):
+                for y in range(2):
+                    c = self.count.local(self.r["full"][w].at[z, y], self.r[name].at[pl.ds((2 * z + y) * c8, c8), :])
+                    c.start()
+                    self.fetched[name].append(c)
+
+    def use(self, *names):
+        self.fetch(*names)
+        for name in names:
+            for c in self.fetched[name]:
+                c.wait()
+
+    def modulation(self):
+        r, p = self.r, self.p
+        self.fetch("tin", "tout")
+        self.tick(2)
+        for c in self.spread:
+            c.wait_recv()
+        self.use("tin", "tout")
+        total = self.ndp * self.ncore
+        rows = total * 8
+        one = fine_nt(r["eall"][...].reshape(rows, FREQ), r["tin"][...])
+        hidden = silu(one)
+        two = fine_nt(hidden, r["tout"][...])
+        r["pre1"][...] = one
+        r["pre2"][...] = two
+        cond = silu(two)
+        deep, wide = r["modw"].shape
+        part = wide // 2
+        mine = split_columns(cond, p.x * 2 + p.c, self.ncore, deep)
+        low = mine.astype(BF16)
+        high = pltpu.roll(mine, 4, 0).astype(BF16)
+        ready = nn(low, r["modw"][:, :part]) + nn(high, r["modw"][:, part:])
+        pad = r["psend"].shape[2] - part
+        r["psend"][...] = jnp.concatenate([ready, jnp.zeros((rows, pad), F32)], axis=1).reshape(total, 8, part + pad)
+        me = p.flat(self.ncore)
+        self.parts = []
+        for k, t, d in self.every:
+            c = self.count.remote(r["psend"].at[t], r["pgot"].at[me], d)
+            c.start()
+            self.parts.append(c)
+        r["pgot"][me] = r["psend"][me]
+        self.done("pre1", "pre2", "eall")
+        self.tick(1)
+        for c in self.parts:
+            c.wait_recv()
+        found = []
+        for i in range(self.ndp):
+            s = r["pgot"][i * self.ncore]
+            for j in range(1, self.ncore):
+                s = s + r["pgot"][i * self.ncore + j]
+            found += [s[:4, :part], s[4:, :part]]
+        rows = jnp.concatenate(found, axis=1)
+        r["mod"][...] = jnp.concatenate([rows, jnp.zeros_like(rows)], axis=0)
+        self.done("mod")
+
+    def done(self, *names):
+        for name in names:
+            c = self.count.local(self.r[name], self.r["out_" + name])
+            c.start()
+            self.saves.append(c)
+
+    def finish(self):
+        while self.now < len(self.units) + 2:
+            self.tick()
+        for i, u in enumerate(self.units):
+            if self.NAMES[UNITS[i][0]] not in self.fetched:
+                u.settled()
+            u.finish()
+        for c in self.swaps + self.spread + self.parts:
+            c.wait_send()
+        for c in self.saves:
             c.wait()
-        for c in self.zs + self.second + [c for v in self.third for c in self.flat(v)]:
-            c.wait_send()
-
-
-def gather_body(depth, shapes, *refs):
+
+
+SAVED = ("mod", "pre1", "pre2", "eall", "stream", "xh1", "m1", "packed", "qa1", "att1", "br1", "xh2", "m2", "mem", "qa2",
+         "att2", "br2", "rs")
+
+
+def gather_forward(mesh, lens, tlens, keep, loud, emb, lat, noi, text, modw, shards):
+    ndp, ncore = mesh.shape["dp"], mesh.shape["fsdp"]
+    depth, total = ndp // 2, ndp * ncore
+    shapes = [(w.shape[1], w.shape[0]) for w in shards]
     nw = len(shapes)
-    ins, outs = refs[:nw], refs[nw : 2 * nw]
-    rest = refs[2 * nw :]
-    turned, landed, block = rest[:nw], rest[nw : 2 * nw], rest[2 * nw : 3 * nw]
-    send, recv = rest[3 * nw :]
-    p = Place(depth)
-    count = Counter(send, recv)
-    swaps = []
+    t, d = lat.shape
+    x, wide = text.shape[0], HEADS * PAIR
+    vm = lambda shape, kind=BF16: pltpu.VMEM(shape, kind)
+    part = modw.shape[1] // 2
+    padded = -(-part // 128) * 128
+    kept = {
+        "mod": ((8, 9 * d), F32), "pre1": ((total * 8, d), F32), "pre2": ((total * 8, d), F32),
+        "eall": ((total, 8, FREQ), F32), "stream": ((t, d), F32), "xh1": ((t, d), BF16), "m1": ((t, d), BF16),
+        "packed": ((t, 3 * d), BF16), "qa1": ((t, wide), BF16), "att1": ((t, d), BF16), "br1": ((t, d), BF16),
+        "xh2": ((t, d), BF16), "m2": ((t, d), BF16), "mem": ((x, 2 * d), BF16), "qa2": ((t, wide), BF16),
+        "att2": ((t, d), BF16), "br2": ((t, d), BF16), "rs": ((t, 128), F32),
+    }
+    full = [(c8 * ndp, share * ncore) for c8, share in shapes]
+    scratch = {name: vm(*kept[name]) for name in SAVED}
+    for w, name in enumerate(ForwardLinks.NAMES[:7]):
+        scratch[name] = vm(full[w])
+    scratch.update(aq=vm((t, PAIR)), aks=vm((t, PAIR)), akc=vm((x, PAIR)), qb=vm((t, d)), tmp=vm((t, d), F32))
+    scratch.update(psend=vm((total, 8, padded), F32), pgot=vm((total, 8, padded), F32))
     for w, (c8, share) in enumerate(shapes):
-        turned[w][...] = ins[w][...].T
-    p.barrier()
-    for w, (c8, share) in enumerate(shapes):
-        half = c8 // 2
-        theirs = turned[w].at[pl.ds(pl.multiple_of((1 - p.c) * half, 16), half), :]
-        swaps.append(count.remote(theirs, landed[w], p.at(c=1 - p.c)))
-        swaps[-1].start()
-    for w, (c8, share) in enumerate(shapes):
-        half = c8 // 2
-        swaps[w].wait_recv()
-        own = turned[w][pl.ds(pl.multiple_of(p.c * half, 16), half), :]
-        got = landed[w][...]
-        first = p.c == 0
-        block[w][...] = jnp.concatenate([jnp.where(first, own, got), jnp.where(first, got, own)], axis=1)
-    units = [GatherUnit(u, shapes, p, count, block, outs) for u in UNITS]
-    n = len(units)
-    ahead = 2
-    begun = 0
-    for t in range(n + 2):
-        while begun < min(n, t + ahead):
-            units[begun].begin()
-            begun += 1
-        if t < n:
-            units[t].step_z()
-        if 0 <= t - 1 < n:
-            units[t - 1].step_second()
-        if 0 <= t - 2 < n:
-            units[t - 2].step_third()
-    for u in units:
-        u.finish()
-    for s in swaps:
-        s.wait_send()
-
-
-def copies_of_gather(depth, nw):
-    return nw + sum(1 + (depth - 1) + depth + depth * (1 if u[5] == 0 else 2) + 2 for u in UNITS)
-
-
-def gather(mesh, weights):
-    depth = mesh.shape["dp"] // 2
-    nx = mesh.shape["fsdp"] // 2
-    shapes = [(w.shape[1], w.shape[0]) for w in weights]
-    ns = copies_of_gather(depth, len(weights))
-    outs = [sds((depth, 2, c8, share * 2 * nx)) for c8, share in shapes]
-    full = pl.pallas_call(
-        partial(gather_body, depth, shapes),
-        out_shape=outs,
-        in_specs=[VM] * len(weights),
-        out_specs=[ANY] * len(weights),
-        scratch_shapes=[pltpu.VMEM((c8, share), BF16) for c8, share in shapes]
-        + [pltpu.VMEM((c8 // 2, share), BF16) for c8, share in shapes]
-        + [pltpu.VMEM((c8 // 2, 2 * share), BF16) for c8, share in shapes]
-        + [pltpu.SemaphoreType.DMA((ns,)), pltpu.SemaphoreType.DMA((ns,))],
-        compiler_params=pltpu.CompilerParams(collective_id=0, has_side_effects=True, vmem_limit_bytes=40 * MIB),
-    )(*weights)
-    return [f.reshape(-1, f.shape[-1]) for f in full]
+        scratch[f"turned{w}"] = vm((c8, share))
+        scratch[f"landed{w}"] = vm((c8 // 2, share))
+        scratch[f"block{w}"] = vm((c8 // 2, 2 * share))
+    ns = 9 + 2 * (total - 1) + len(SAVED) + 7 * ndp
+    ns += sum(1 + (depth - 1) + depth + depth * (1 if u[5] == 0 else 2) + 2 for u in UNITS)
+    scratch.update(send=pltpu.SemaphoreType.DMA((ns,)), recv=pltpu.SemaphoreType.DMA((ns,)))
+    names = list(scratch)
+
+    def kernel(*refs):
+        lens, tlens, keep, loud, emb, lat, noi, text, modw = refs[:9]
+        r = dict(emb=emb, modw=modw, shards=refs[9 : 9 + nw])
+        at = 9 + nw
+        r["full"] = refs[at : at + nw]
+        at += nw
+        for name in SAVED:
+            r["out_" + name] = refs[at]
+            at += 1
+        r.update(zip(names, refs[at:]))
+        for kind in ("turned", "landed", "block"):
+            r[kind] = [r[f"{kind}{w}"] for w in range(nw)]
+        links = ForwardLinks(mesh, shapes, r)
+        forward_attention(links, lens, tlens, keep, loud, r["mod"], lat, noi, text,
+                          *[r[n] for n in ("wsp", "wso", "wcq", "wcm", "wco", "stream", "xh1", "m1", "packed", "qa1",
+                                           "att1", "br1", "xh2", "m2", "mem", "qa2", "att2", "br2", "rs", "aq", "aks",
+                                           "akc", "qb", "tmp")])
+        links.finish()
+
+    got = pl.pallas_call(
+        kernel,
+        out_shape=[sds((depth, 2, c8, share * ncore)) for c8, share in shapes] + [sds(*kept[n]) for n in SAVED],
+        in_specs=[SM] * 4 + [VM] * (5 + nw),
+        out_specs=[ANY] * (nw + len(SAVED)),
+        scratch_shapes=list(scratch.values()),
+        cost_estimate=pl.CostEstimate(flops=int(3e10), bytes_accessed=int(6e7), transcendentals=0),
+        compiler_params=pltpu.CompilerParams(collective_id=0, has_side_effects=True, vmem_limit_bytes=60 * MIB),
+    )(lens, tlens, keep, loud, emb, lat, noi, text, modw, *shards)
+    weights = [f.reshape(-1, f.shape[-1]) for f in got[:nw]]
+    return weights, dict(zip(SAVED, got[nw:]))
 
 
 SUM_UNITS = (
@@ -919,27 +1154,36 @@
     items = time_steps.shape[0]
     sent = (time_in, time_out) + others
     direct = fits(mesh, sent)
-    full = gather(mesh, sent) if direct else [plain_gather(w) for w in sent]
-    t_in, t_out = full[0].astype(F32), full[1].astype(F32)
+    text = text_states.reshape(-1, width)
+    keep, loud, embedding = plan(time_steps)
+    deep, wide = modulation.shape
+    if direct:
+        embedding = jnp.pad(embedding, ((0, 8 - items), (0, 0)))
+        full, saved = gather_forward(mesh, item_lengths, text_lengths, keep, loud, embedding, latents, noise_draw, text,
+                                     modulation, sent)
+        mod = saved["mod"]
+        first = [saved[n] for n in SAVED[4:]]
+        embedding = saved["eall"][:, :items].reshape(-1, FREQ)
+        pre_one, pre_two = [saved[n].reshape(-1, 8, width)[:, :items].reshape(-1, width) for n in ("pre1", "pre2")]
+        t_out = full[1].astype(F32)
+        hidden = jax.nn.silu(pre_one)
+        mine = columns(jax.nn.silu(pre_two).astype(BF16), j, deep)
+    else:
+        full = [plain_gather(w) for w in sent]
+        t_in, t_out = full[0].astype(F32), full[1].astype(F32)
+        embedding = lax.all_gather(embedding, BOTH, axis=0, tiled=True)
+        pre_one = high_dot(embedding, t_in, 1, 1)
+        hidden = jax.nn.silu(pre_one)
+        pre_two = high_dot(hidden, t_out, 1, 1)
+        mine = columns(jax.nn.silu(pre_two).astype(BF16), j, deep)
+        part = jnp.dot(mine, modulation, preferred_element_type=F32).reshape(ndp, nfs * items, wide)
+        part = lax.psum_scatter(part, "fsdp", scatter_dimension=1, tiled=True)
+        rows = lax.all_to_all(part, "dp", 0, 0, tiled=True)
+        mod = jnp.pad(rows.transpose(1, 0, 2).reshape(items, -1), ((0, 8 - items), (0, 0)))
+        first = run_attention(item_lengths, text_lengths, keep, loud, mod, latents, noise_draw, text, *full[2:7])
     weights = full[2:]
-
-    all_steps = lax.all_gather(time_steps, BOTH, axis=0, tiled=True)
-    keep, loud, _ = plan(time_steps)
-    _, _, embedding = plan(all_steps)
-    pre_one = high_dot(embedding, t_in, 1, 1)
-    hidden = jax.nn.silu(pre_one)
-    pre_two = high_dot(hidden, t_out, 1, 1)
-    cond_low = jax.nn.silu(pre_two).astype(BF16)
-    deep, wide = modulation.shape
-    mine = columns(cond_low, j, deep)
-    part = jnp.dot(mine, modulation, preferred_element_type=F32).reshape(ndp, nfs * items, wide)
-    part = lax.psum_scatter(part, "fsdp", scatter_dimension=1, tiled=True)
-    rows = lax.all_to_all(part, "dp", 0, 0, tiled=True)
-    mod = jnp.pad(rows.transpose(1, 0, 2).reshape(items, -1), ((0, 8 - items), (0, 0)))
-
-    text = text_states.reshape(-1, width)
-    a, b = run_forward(item_lengths, text_lengths, keep, loud, mod, latents, noise_draw, text, *weights)
-    out, lat_grad, *grads, sums = run_backward(item_lengths, text_lengths, keep, mod, text, cotangent, a, b, *weights)
+    second = run_ff(item_lengths, mod, first[0], *weights[5:])
+    out, lat_grad, *grads, sums = run_backward(item_lengths, text_lengths, keep, mod, text, cotangent, first, second, *weights)
     shares = reduce(mesh, grads) if direct else [plain_reduce(g) for g in grads]
 
     sent_sums = sums[:items].astype(BF16).reshape(items, ndp, wide).transpose(1, 0, 2)

time: 624 us -> 480 us (0.77)
  waiting for transfers between devices: 93.7 us -> 6.58 us
  blocking collectives: 55.7 us -> 12.4 us
  local copies, waits for them, and re-layouts: 27.5 us -> 13.6 us
    psum x1, waiting for transfers between devices: 68.1 us -> 0.01 us  [body(): back = lax.all_gather(lax.psum(back, 'dp'), 'fsdp', axis=1, tiled=True)]
    pallas_call x1, Pallas kernels: 112 us -> 174 us  [gather_forward(): pl.pallas_call(kernel, out_shape=[sds((depth, 2, c8, share * ncore)) for...]
    pallas_call x4 -> x3, Pallas kernels: 182 us -> 126 us  [call(): pl.pallas_call(body, out_shape=outs, in_specs=[SM] * len(scalars) + [VM]...]
    unnamed x1 -> x0, blocking collectives: 42 us -> none
    unnamed x3 -> x1, waiting for transfers between devices: 19 us -> 0.02 us
    unnamed x54 -> x32, local copies, waits for them, and re-layouts: 21.2 us -> 8.38 us
    all_to_all x1 -> x0, waiting for transfers between devices: 6.61 us -> none  [body(): rows = lax.all_to_all(part, 'dp', 0, 0, tiled=True)]
    all_to_all x1, waiting for transfers between devices: 0.01 us -> 6.57 us  [body(): got = lax.all_to_all(sent_sums, 'dp', 0, 0, tiled=True)]
  transfers between devices with their start and end apart: 4 -> 2, of which waited for: 3 -> 1; matrix products, arithmetic and copies ran while one was open for 1% -> 1% of each run, Pallas kernels for 18% -> 24%
where the time goes in v2:
time: 480 us; the launch traced here: 476 us
  Pallas kernels  412 us (86%)
  between operations  14.7 us (3%)
  local copies, waits for them, and re-layouts  13.6 us (3%)
  blocking collectives  12.4 us (3%)
  starting transfers between devices  8.37 us (2%)
  waiting for transfers between devices  6.58 us (1%)
  matrix products  4.9 us (1%)
    pallas_call x1, Pallas kernels, gather_forward(): pl.pallas_call(kernel, out_shape=[sds((depth, 2, c8, share * ncore)) for...  174 us
    pallas_call x3, Pallas kernels, call(): pl.pallas_call(body, out_shape=outs, in_specs=[SM] * len(scalars) + [VM]...  126 us
    pallas_call x1, Pallas kernels, reduce(): pl.pallas_call(partial(reduce_body, depth, shapes), out_shape=[sds(s, F32...  109 us
  transfers between devices with their start and end apart: 2, of which 1 were waited for; matrix products, arithmetic and copies ran while one was open for 1% of the time, Pallas kernels for 24%

profile of v2, /device:TPU:0, one launch (start us, length us, event | category | flops | bytes accessed | tf_op | source)
XLA Modules:
  0.0 475.7 jit_solution(9860288472927701949)
XLA Ops:
  7.9 1.2 subtract_sqrt_fusion
  9.1 1.7 copy.39.refs_17_
  11.5 174.0 %shard_map.256 = (bf16[4,2,96,256]{3,2,1,0:T(8,128)(2,1)}, bf16[4,2,96,768]{3,2,1,0:T(8,128)(2,1)}, bf16[4,2,288,768]{3,2,1,0:T(8,128)(2,1)}, bf16[4,2,96,768]{3...) custom-call(s32[1,3]{1,0:T(1,128)} %lens.5, ...), custom_call_target="tpu_custom_call" | custom-call | flops 30000001024 | bytes 60000000 | tf_op jit(solution)/shard_map/pallas_call | solution.py:883
  185.5 25.1 %shard_map.257 = (bf16[768,768]{1,0:T(8,128)(2,1)}, bf16[768,768]{1,0:T(8,128)(2,1)}, bf16[768,3072]{1,0:T(8,128)(2,1)}, bf16[768,3072]{1,0:T(8,128)(2,1)}, bf16...) custom-call(s32[1,3]{1,0:T(1,128)} %lens.5, f32[8,6912]{1,0:T(8,128)} %get-tuple-element.71.mod, ...), custom_call_target="tpu_custom_call" | custom-call | flops 10000000000 | bytes 30000000 | tf_op jit(solution)/shard_map/pallas_call | solution.py:455
  210.7 33.7 %shard_map.258 = (f32[768,768]{1,0:T(8,128)}, bf16[768,768]{1,0:T(8,128)(2,1)}, bf16[768,3072]{1,0:T(8,128)(2,1)}, bf16[3072,768]{1,0:T(8,128)(2,1)}, f32[16,6912]{1,0:T(8,128)}) custom-call(s32[1,3]{1,0:T(1,128)} %lens.5, f32[8,6912]{1,0:T(8,128)} %get-tuple-element.71.mod, bf16[768,768]{1,0:T(8,128)(2,1)} %cot.1, bf16[768,768]{1,0:T(8,128)(2,1)} %get-tuple-element.76.br3, ...), custom_call_target="tpu_custom_call" | custom-call | flops 30000001024 | bytes 30000000 | tf_op jit(solution)/shard_map/pallas_call | solution.py:455
  244.4 66.7 %shard_map.259 = (f32[768,768]{1,0:T(8,128)}, bf16[2304,768]{1,0:T(8,128)(2,1)}, bf16[768,768]{1,0:T(8,128)(2,1)}, bf16[768,768]{1,0:T(8,128)(2,1)}, bf16[1536,7...) custom-call(s32[1,3]{1,0:T(1,128)} %lens.5, s32[3]{0:T(128)} %tlens.1, ...), custom_call_target="tpu_custom_call" | custom-call | flops 60000002048 | bytes 30000000 | tf_op jit(solution)/shard_map/pallas_call | solution.py:455
  311.1 1.0 slice.21
  312.9 8.3 %all-to-all-start = ((bf16[8,3,864]{2,1,0:T(4,128)(2,1)}), bf16[8,3,864]{2,1,0:T(4,128)(2,1)S(1)}, u32[]{:S(2)}, u32[]{:S(2)}) async-start(bf16[8,3,864]{2,1,0:T(4,128)(2,1)} %bitcast.25), calls=%async_computation | async-start | bytes 114688 | tf_op jit(solution)/shard_map/all_to_all | solution.py:1190
  321.5 6.6 %all-to-all-done = bf16[8,3,864]{2,1,0:T(4,128)(2,1)S(1)} async-done(((bf16[8,3,864]{2,1,0:T(4,128)(2,1)}), bf16[8,3,864]{2,1,0:T(4,128)(2,1)S(1)}, u32[]{:S(2)}, u32[]{:S(2)}) %all-to-all-start) | async-done | bytes 41504 | tf_op jit(solution)/shard_map/all_to_all | solution.py:1190
  328.1 5.7 %all_gather.6 = bf16[8,12,864]{2,0,1:T(8,128)(2,1)S(1)} all-gather(bf16[8,3,864]{2,0,1:T(8,128)(2,1)S(1)} %copy.41), channel_id=1, replica_groups=mesh['dp'=8,'fsdp'=4] {'fsdp'}, dimensions={1}, use_global_device_ids=true | all-gather | bytes 207360 | tf_op jit(solution)/shard_map/all_gather | solution.py:1191
  333.9 0.9 fusion.19
  334.8 0.8 add_divide_fusion
  336.3 1.2 slice.18
  337.7 109.4 %shard_map.260 = (f32[288,192]{1,0:T(8,128)S(1)}, f32[96,192]{1,0:T(8,128)S(1)}, f32[96,192]{1,0:T(8,128)S(1)}, f32[192,192]{1,0:T(8,128)S(1)}, f32[96,192]{1,0:...) custom-call(bf16[4,2,288,768]{3,2,1,0:T(8,128)(2,1)} %bitcast.30, bf16[4,2,96,768]{3,2,1,0:T(8,128)(2,1)S(1)} %bitcast.26, ...), custom_call_target="tpu_custom_call" | custom-call | tf_op jit(solution)/shard_map/pallas_call | solution.py:1087
  447.1 0.7 copy-done.2
  447.8 0.7 copy-done.3
  448.5 0.7 copy-done.4
  451.8 2.7 shard_map.261
  454.5 1.9 copy.45
  456.4 1.0 copy.43
  457.4 6.7 %all_gather.7 = f32[96,768]{0,1:T(8,128)S(1)} all-gather(f32[96,192]{0,1:T(8,128)S(1)} %copy.43), channel_id=1, replica_groups=mesh['dp'=8,'fsdp'=4] {'fsdp'}, dimensions={1}, use_global_device_ids=true | all-gather | bytes 368640 | tf_op jit(solution)/shard_map/all_gather | solution.py:1194
  465.1 1.2 fusion.3
  466.4 1.1 fusion.1
  467.5 0.9 fusion.5
  (47 shorter events, 7.0 us)
Async XLA Ops:
  244.4 76.9 %copy-start.13 = (f32[256,768]{1,0:T(8,128)S(1)}, f32[256,768]{1,0:T(8,128)}, u32[]{:S(2)}) copy-start(f32[256,768]{1,0:T(8,128)} %get-tuple-element.108) | copy-start | bytes 2359300
  312.9 15.2 %all-to-all-start = ((bf16[8,3,864]{2,1,0:T(4,128)(2,1)}), bf16[8,3,864]{2,1,0:T(4,128)(2,1)S(1)}, u32[]{:S(2)}, u32[]{:S(2)}) async-start(bf16[8,3,864]{2,1,0:T(4,128)(2,1)} %bitcast.25), calls=%async_computation | async-start | bytes 114688 | tf_op jit(solution)/shard_map/all_to_all | solution.py:1190
  321.2 135.2 %all-reduce.3.cloned.1.call-start = ((), (), s32[]{:S(2)}) async-start(), calls=%async_computation.1 | async-start | bytes 196608 | tf_op jit(solution)/shard_map/psum | solution.py:1194
  321.3 12.6 %copy-start.11 = (bf16[192,864]{1,0:T(8,128)(2,1)S(1)}, bf16[192,864]{1,0:T(8,128)(2,1)}, u32[]{:S(2)}) copy-start(bf16[192,864]{1,0:T(8,128)(2,1)} %refs_8_.1) | copy-start | bytes 995332
  328.1 7.5 %copy-start.14 = (f32[32,8,256]{2,1,0:T(8,128)S(1)}, f32[32,8,256]{2,1,0:T(8,128)}, u32[]{:S(2)}) copy-start(f32[32,8,256]{2,1,0:T(8,128)} %get-tuple-element.104) | copy-start | bytes 786436
  334.8 2.9 copy-start
  334.8 2.9 copy-start.1
  447.1 0.7 copy-start.2
  447.8 0.7 copy-start.3
  448.5 0.7 copy-start.4
  449.3 0.7 copy-start.5
  449.9 0.6 copy-start.6
  450.6 0.6 copy-start.7
  451.2 0.6 copy-start.8
  457.4 7.0 %copy-start.9 = (bf16[4,2,96,768]{3,2,1,0:T(8,128)(2,1)S(1)}, bf16[4,2,96,768]{3,2,1,0:T(8,128)(2,1)}, u32[]{:S(2)}) copy-start(bf16[4,2,96,768]{3,2,1,0:T(8,128)(2,1)} %get-tuple-element.107) | copy-start | bytes 3538948
  464.4 2.0 copy-start.10
  464.4 3.1 copy-start.12
Sparse Core Ops, SparseCore 0:
  334.9 67.5 all-reduce.2

commit v3 on v2

--- a/solution.py
+++ b/solution.py
@@ -89,7 +89,7 @@
     return one, two, column - one - two
 
 
-def in_parts(pair, pump, step=2):
+def in_parts(pair, pump, step=3):
     if pump is None:
         lax.fori_loop(0, PAIRS, pair, 0)
         return
@@ -284,7 +284,6 @@
 
     tiles(frames, middle)
     links.done("br1", "xh2", "m2", "rs")
-    links.tick()
     links.use("wcq", "wcm")
     big_nt(m2, wcq, qb, width)
     big_nt(text, wcm, mem, width)
@@ -483,18 +482,25 @@
                 [pltpu.VMEM((t, d), F32)], 1e10)
 
 
+def run_ff_back(lens, mod, cot, br2, kept, wup, wdn):
+    t, d = cot.shape
+    xh3, m3, act, slope, br3, out, rs3 = kept
+    ff = wup.shape[0]
+
+    def kernel(lens, mod, cot, br3, act, slope, xh3, m3, rs, wup, wdn, br2, g, b2, dwd, dwu, sums, b3, ig, tmp):
+        backward_ff(lens, mod, cot, br3, act, slope, xh3, m3, rs, wup, wdn, g, b2, br2, dwd, dwu, sums, b3, ig, tmp)
+
+    return call(kernel, (lens,), (mod, cot, br3, act, slope, xh3, m3, rs3, wup, wdn, br2),
+                [sds((t, d), F32), sds((t, d)), sds((d, ff)), sds((ff, d)), sds((16, 9 * d), F32)],
+                [pltpu.VMEM((t, d), BF16), pltpu.VMEM((t, ff), BF16), pltpu.VMEM((t, d), F32)], 3e10)
+
+
 def run_backward(lens, tlens, keep, mod, text, cot, a, b, wsp, wso, wcq, wcm, wco, wup, wdn):
     t, d = cot.shape
     x = text.shape[0]
     stream, xh1, m1, packed, qa1, att1, br1, xh2, m2, mem, qa2, att2, br2, rs = a
-    xh3, m3, act, slope, br3, out, rs3 = b
-    ff = wup.shape[0]
-    g, b2, dwd, dwu, sums = call(
-        partial(lambda lens, mod, cot, br3, act, slope, xh3, m3, rs, wup, wdn, br2, g, b2, dwd, dwu, sums, b3, ig, tmp:
-                backward_ff(lens, mod, cot, br3, act, slope, xh3, m3, rs, wup, wdn, g, b2, br2, dwd, dwu, sums, b3, ig, tmp)),
-        (lens,), (mod, cot, br3, act, slope, xh3, m3, rs3, wup, wdn, br2),
-        [sds((t, d), F32), sds((t, d)), sds((d, ff)), sds((ff, d)), sds((16, 9 * d), F32)],
-        [pltpu.VMEM((t, d), BF16), pltpu.VMEM((t, ff), BF16), pltpu.VMEM((t, d), F32)], 3e10)
+    out = b[5]
+    g, b2, dwd, dwu, sums = run_ff_back(lens, mod, cot, br2, b, wup, wdn)
     lat_grad, dsp, dso, dcq, dcm, dco, sums = call(
         backward_attention, (lens, tlens, keep),
         (mod, text, g, b2, xh1, m1, packed, qa1, att1, br1, xh2, m2, mem, qa2, att2, rs, wsp, wso, wcq, wcm, wco, sums),
@@ -506,15 +512,18 @@
 
 MESH = pl.DeviceIdType.MESH
 ANY = pl.BlockSpec(memory_space=pl.ANY)
-UNITS = (
-    (0, 0, 1, 0, 2, 0), (1, 0, 1, 0, 2, 1),
-    (2, 0, 2 / 3, 0, 2, 0), (2, 2 / 3, 1 / 3, 0, 2, 1),
-    (3, 0, 1, 0, 2, 1), (4, 0, 1, 0, 2, 0),
-    (5, 0, 1 / 2, 0, 2, 0), (5, 1 / 2, 1 / 2, 0, 2, 1),
-    (6, 0, 1, 0, 2, 1),
-    (7, 0, 1 / 2, 0, 2, 0), (7, 1 / 2, 1 / 2, 0, 2, 1),
-    (8, 0, 1, 0, 1, 0), (8, 0, 1, 1, 1, 1),
+GROUPS = (
+    ((0, 0, 1, 0, 2, 0), (1, 0, 1 / 3, 0, 2, 0), (1, 1 / 3, 2 / 3, 0, 2, 1)),
+    ((2, 0, 5 / 9, 0, 2, 0), (2, 5 / 9, 4 / 9, 0, 2, 1)),
+    ((3, 0, 1, 0, 2, 1), (4, 0, 1, 0, 2, 0)),
+    ((5, 0, 1 / 2, 0, 2, 0), (5, 1 / 2, 1 / 2, 0, 2, 1)),
+    ((6, 0, 1 / 3, 0, 2, 0), (6, 1 / 3, 2 / 3, 0, 2, 1)),
+    ((7, 0, 1 / 4, 0, 2, 0), (7, 1 / 4, 1 / 4, 0, 2, 1)),
+    ((7, 1 / 2, 1 / 4, 0, 2, 0), (7, 3 / 4, 1 / 4, 0, 2, 1)),
+    ((8, 0, 1 / 3, 0, 2, 0), (8, 1 / 3, 1 / 3, 0, 2, 1)),
+    ((8, 2 / 3, 1 / 3, 0, 1, 0), (8, 2 / 3, 1 / 3, 1, 1, 1)),
 )
+UNITS = tuple(u for g in GROUPS for u in g)
 
 
 class Place:
@@ -569,7 +578,7 @@
     w, r0, nr, l0, nl, route = unit
     c8, share = shapes[w]
     half = c8 // 2
-    return w, int(round(half * r0)), int(round(half * nr)), l0 * share, nl * share, route, half
+    return w, round(half * r0), round(half * nr), round(l0 * share), round(nl * share), route, half
 
 
 class GatherUnit:
@@ -684,6 +693,9 @@
     return v / (1.0 + jnp.exp(-v))
 
 
+AHEAD = 2
+
+
 class ForwardLinks:
     NAMES = ("tin", "tout", "wsp", "wso", "wcq", "wcm", "wco", "wup", "wdn")
 
@@ -720,34 +732,43 @@
             got = landed[w][...]
             first = p.c == 0
             block[w][...] = jnp.concatenate([jnp.where(first, own, got), jnp.where(first, got, own)], axis=1)
-            for u in UNITS:
-                if u[0] == w:
-                    self.units.append(GatherUnit(u, shapes, p, count, block, r["full"]))
-                    self.units[-1].begin()
-        self.swaps = swaps
+        self.units = [[GatherUnit(u, shapes, p, count, block, r["full"]) for u in g] for g in GROUPS]
+        self.swaps, self.begun = swaps, 0
+        self.start(AHEAD)
         self.now, self.fetched, self.waiting, self.saves = 0, {}, {}, []
         self.pump = self.tick
+
+    def start(self, upto):
+        while self.begun < min(upto, len(self.units)):
+            for u in self.units[self.begun]:
+                u.begin()
+            self.begun += 1
 
     def tick(self, n=1):
         for _ in range(n):
             t, self.now = self.now, self.now + 1
-            if t < len(self.units):
-                self.units[t].step_z()
-            if 0 <= t - 1 < len(self.units):
-                self.units[t - 1].step_second()
-            if 0 <= t - 2 < len(self.units):
-                self.units[t - 2].step_third()
+            n = len(self.units)
+            self.start(t + AHEAD)
+            if t < n:
+                for u in self.units[t]:
+                    u.step_z()
+            if 0 <= t - 1 < n:
+                for u in self.units[t - 1]:
+                    u.step_second()
+            if 0 <= t - 2 < n:
+                for u in self.units[t - 2]:
+                    u.step_third()
 
     def fetch(self, *names):
         for name in names:
             if name in self.fetched:
                 continue
             w = self.NAMES.index(name)
-            mine = [i for i, u in enumerate(UNITS) if u[0] == w]
-            while self.now - 3 < mine[-1]:
+            mine = [(i, k) for i, g in enumerate(GROUPS) for k, u in enumerate(g) if u[0] == w]
+            while self.now - 3 < mine[-1][0]:
                 self.tick()
-            for i in mine:
-                self.units[i].settled()
+            for i, k in mine:
+                self.units[i][k].settled()
             c8 = self.shapes[w][0]
             self.fetched[name] = []
             for z in range(self.p.depth):
@@ -765,7 +786,6 @@
     def modulation(self):
         r, p = self.r, self.p
         self.fetch("tin", "tout")
-        self.tick(2)
         for c in self.spread:
             c.wait_recv()
         self.use("tin", "tout")
@@ -815,10 +835,11 @@
     def finish(self):
         while self.now < len(self.units) + 2:
             self.tick()
-        for i, u in enumerate(self.units):
-            if self.NAMES[UNITS[i][0]] not in self.fetched:
-                u.settled()
-            u.finish()
+        for g, units in zip(GROUPS, self.units):
+            for u, unit in zip(g, units):
+                if self.NAMES[u[0]] not in self.fetched:
+                    unit.settled()
+                unit.finish()
         for c in self.swaps + self.spread + self.parts:
             c.wait_send()
         for c in self.saves:
@@ -893,11 +914,17 @@
     return weights, dict(zip(SAVED, got[nw:]))
 
 
-SUM_UNITS = (
-    (6, 0, 1, 0, 1, 0), (6, 0, 1, 1, 1, 1), (5, 0, 1 / 2, 0, 2, 0), (5, 1 / 2, 1 / 2, 0, 2, 1),
-    (4, 0, 1, 0, 2, 0), (2, 0, 1, 0, 2, 1), (3, 0, 1 / 2, 0, 2, 0), (3, 1 / 2, 1 / 2, 0, 2, 1),
-    (1, 0, 1, 0, 2, 1), (0, 0, 2 / 3, 0, 2, 0), (0, 2 / 3, 1 / 3, 0, 2, 1),
+SUM_GROUPS = (
+    ((6, 0, 1, 0, 1 / 2, 0), (6, 0, 1, 1 / 2, 1 / 2, 1)),
+    ((6, 0, 1, 1, 1 / 2, 0), (6, 0, 1, 3 / 2, 1 / 2, 1)),
+    ((5, 0, 1 / 4, 0, 2, 0), (5, 1 / 4, 1 / 4, 0, 2, 1)),
+    ((5, 1 / 2, 1 / 4, 0, 2, 0), (5, 3 / 4, 1 / 4, 0, 2, 1)),
+    ((4, 0, 1, 0, 2, 0), (2, 0, 1, 0, 2, 1)),
+    ((3, 0, 1 / 2, 0, 2, 0), (3, 1 / 2, 1 / 2, 0, 2, 1)),
+    ((1, 0, 1, 0, 2, 0), (0, 0, 1 / 3, 0, 2, 1)),
+    ((0, 1 / 3, 1 / 3, 0, 2, 0), (0, 2 / 3, 1 / 3, 0, 2, 1)),
 )
+EARLY = 4
 
 
 def each(count, fn):
@@ -913,35 +940,55 @@
 
 
 class SumUnit:
-    def __init__(self, unit, shapes, place, count, grads, held, cores, first, second, lasts, final):
+    def __init__(self, unit, shapes, place, count, grads, own, bufs, final):
         w, r0, n, l0, nl, route, half = unit_shape(unit, shapes)
         self.p, self.route, self.D = place, route, place.depth
         p, D = place, place.depth
         share = shapes[w][1]
         row = pl.ds(pl.multiple_of(p.c * half + r0, 16), n)
         other = pl.ds(pl.multiple_of((1 - p.c) * half + r0, 16), n)
-        self.held, self.cores, self.first, self.second, self.lasts = held, cores, first, second, lasts
+        self.total, self.first, self.second, self.lasts = bufs
         self.final, self.at = final[w], (pl.ds(r0, n), pl.ds(l0, nl))
-        self.loads, self.swaps = [], []
+        self.loads, self.swaps, self.lanes = [], [], []
+        self.row, self.grad, self.own = row, grads[w], own
         for i in range(2):
             lane = pl.ds(i * 2 * share + l0, nl)
-            self.loads.append(count.local(grads[w].at[:, :, row, lane], held.at[i]))
-            self.swaps.append(count.remote(grads[w].at[:, :, other, lane], cores.at[i], p.at(c=1 - p.c)))
+            self.lanes.append(lane)
+            if own is not None:
+                self.loads.append(count.local(grads[w].at[:, :, row, lane], own.at[i]))
+            self.swaps.append(count.remote(grads[w].at[:, :, other, lane], self.total.at[i], p.at(c=1 - p.c)))
         x, y, z = p.x, p.y, p.z
+        total = self.total
         if route == 0:
-            self.one = count.remote(held.at[1 - x], first, p.at(x=1 - x))
-            self.two = count.remote(held.at[x, :, 1 - y], second, p.at(y=1 - y))
+            self.one = count.remote(total.at[1 - x], self.first, p.at(x=1 - x))
+            self.two = count.remote(total.at[x, :, 1 - y], self.second, p.at(y=1 - y))
         else:
-            self.one = count.remote(held.at[:, :, 1 - y], first, p.at(y=1 - y))
-            self.two = count.remote(held.at[1 - x, :, y], second, p.at(x=1 - x))
+            self.one = count.remote(total.at[:, :, 1 - y], self.first, p.at(y=1 - y))
+            self.two = count.remote(total.at[1 - x, :, y], self.second, p.at(x=1 - x))
         self.three = []
         for k in range(1, D):
             zz = p.other_z(k)
-            self.three.append(count.remote(held.at[x, zz, y], lasts.at[k - 1], p.at(z=zz)))
-
-    def begin(self):
-        for c in self.loads + self.swaps:
+            self.three.append(count.remote(total.at[x, zz, y], self.lasts.at[k - 1], p.at(z=zz)))
+
+    def load(self):
+        for c in self.loads:
             c.start()
+
+    def swap(self):
+        for c in self.swaps:
+            c.start()
+
+    def add_own(self, x, z, y):
+        if self.own is not None:
+            v = self.own[x, z, y]
+        else:
+            if isinstance(x, int):
+                v = self.grad[z, y, self.row, self.lanes[x]]
+            else:
+                width = self.lanes[1].start - self.lanes[0].start
+                lane = pl.ds(pl.multiple_of(x * width + self.lanes[0].start, 128), self.lanes[0].size)
+                v = self.grad[z, y, self.row, lane]
+        self.total[x, z, y] = plus(self.total[x, z, y], v)
 
     def step_core(self):
         for c in self.loads:
@@ -949,32 +996,23 @@
         for c in self.swaps:
             c.wait_recv()
         x, y, D = self.p.x, self.p.y, self.D
-        held, cores = self.held, self.cores
         if self.route == 0:
-            def add(xx):
-                def fn(i):
-                    held[xx, i // 2, i % 2] = plus(held[xx, i // 2, i % 2], cores[xx, i // 2, i % 2])
-                each(2 * D, fn)
-            add(1 - x)
+            each(2 * D, lambda i: self.add_own(1 - x, i // 2, i % 2))
             self.one.start()
-            add(x)
+            each(2 * D, lambda i: self.add_own(x, i // 2, i % 2))
         else:
-            def add(yy):
-                def fn(i):
-                    held[i // D, i % D, yy] = plus(held[i // D, i % D, yy], cores[i // D, i % D, yy])
-                each(2 * D, fn)
-            add(1 - y)
+            each(2 * D, lambda i: self.add_own(i // D, i % D, 1 - y))
             self.one.start()
-            add(y)
+            each(2 * D, lambda i: self.add_own(i // D, i % D, y))
 
     def step_one(self):
         self.one.wait_recv()
         x, y, D = self.p.x, self.p.y, self.D
-        held, got = self.held, self.first
+        total, got = self.total, self.first
         if self.route == 0:
             def add(yy):
                 def fn(i):
-                    held[x, i, yy] = plus(held[x, i, yy], got[i, yy])
+                    total[x, i, yy] = plus(total[x, i, yy], got[i, yy])
                 each(D, fn)
             add(1 - y)
             self.two.start()
@@ -982,7 +1020,7 @@
         else:
             def add(xx):
                 def fn(i):
-                    held[xx, i, y] = plus(held[xx, i, y], got[xx, i])
+                    total[xx, i, y] = plus(total[xx, i, y], got[xx, i])
                 each(D, fn)
             add(1 - x)
             self.two.start()
@@ -991,36 +1029,24 @@
     def step_two(self):
         self.two.wait_recv()
         x, y = self.p.x, self.p.y
-        held, got = self.held, self.second
+        total, got = self.total, self.second
         for k in range(1, self.D):
             zz = self.p.other_z(k)
-            held[x, zz, y] = plus(held[x, zz, y], got[zz])
+            total[x, zz, y] = plus(total[x, zz, y], got[zz])
             self.three[k - 1].start()
 
     def step_three(self):
         for c in self.three:
             c.wait_recv()
         x, y, z = self.p.x, self.p.y, self.p.z
-        total = self.held[x, z, y].astype(F32) + self.second[z].astype(F32)
+        value = self.total[x, z, y].astype(F32) + self.second[z].astype(F32)
         for k in range(self.D - 1):
-            total += self.lasts[k].astype(F32)
-        self.final[self.at] = total
-
-    def finish(self):
+            value += self.lasts[k].astype(F32)
+        self.final[self.at] = value
+
+    def sent(self):
         for c in self.swaps + [self.one, self.two] + self.three:
             c.wait_send()
-
-
-def sum_scratch(shapes, depth, units):
-    scratch = []
-    for u in units:
-        w, r0, n, l0, nl, route, half = unit_shape(u, shapes)
-        scratch.append(pltpu.VMEM((2, depth, 2, n, nl), BF16))
-        scratch.append(pltpu.VMEM((2, depth, 2, n, nl), BF16))
-        scratch.append(pltpu.VMEM((depth, 2, n, nl) if route == 0 else (2, depth, n, nl), BF16))
-        scratch.append(pltpu.VMEM((depth, n, nl), BF16))
-        scratch.append(pltpu.VMEM((depth - 1, n, nl), BF16))
-    return scratch
 
 
 class LastSwap:
@@ -1043,64 +1069,423 @@
         self.copy.wait()
 
 
-def reduce_body(depth, shapes, *refs):
-    nw = len(shapes)
-    grads, outs, rest = refs[:nw], refs[nw : 2 * nw], refs[2 * nw :]
-    final, part, rest = rest[:nw], rest[nw : 2 * nw], rest[2 * nw :]
-    send, recv = rest[-2:]
-    p = Place(depth)
-    count = Counter(send, recv)
-    p.barrier()
-    units = [SumUnit(u, shapes, p, count, grads, *rest[5 * i : 5 * i + 5], final) for i, u in enumerate(SUM_UNITS)]
-    swaps = [LastSwap(w, shapes, p, count, final, part, outs) for w in range(nw)]
-    n = len(units)
-    last = {u[0]: i for i, u in enumerate(SUM_UNITS)}
-    for u in units:
-        u.begin()
-    for t in range(n + 3):
-        if t < n:
-            units[t].step_core()
-        if 0 <= t - 1 < n:
-            units[t - 1].step_one()
-        if 0 <= t - 2 < n:
-            units[t - 2].step_two()
-        if 0 <= t - 3 < n:
-            units[t - 3].step_three()
-            for w, i in last.items():
-                if i == t - 3:
-                    swaps[w].begin()
-    for u in units:
-        u.finish()
-    for s in swaps:
-        s.finish()
+class BackwardLinks:
+    def __init__(self, mesh, shapes, r):
+        self.ndp, self.ncore = mesh.shape["dp"], mesh.shape["fsdp"]
+        self.shapes, self.r = shapes, r
+        self.p = p = Place(self.ndp // 2)
+        self.count = count = Counter(r["send"], r["recv"])
+        self.every = others(p, self.ndp, self.ncore)
+        p.barrier([d for _, _, d in self.every])
+        self.groups, self.now = [], 0
+        for gi, g in enumerate(SUM_GROUPS):
+            early = gi < EARLY
+            units = []
+            for k, u in enumerate(g):
+                own = r[f"own{gi % 2}_{k}"] if early else None
+                units.append(SumUnit(u, shapes, p, count, r["grads"], own, r["slot_of"][(gi, k)], r["final"]))
+            self.groups.append(units)
+        self.swaps = [LastSwap(w, shapes, p, count, r["final"], r["part"], r["shares"]) for w in range(len(shapes))]
+        last = {u[0]: gi for gi, g in enumerate(SUM_GROUPS) for u in g}
+        self.closing = {gi: [w for w, l in last.items() if l == gi] for gi in range(len(SUM_GROUPS))}
+        for units in self.groups[:EARLY]:
+            for u in units:
+                u.swap()
+        for units in self.groups[:2]:
+            for u in units:
+                u.load()
+        self.moves, self.saves = {}, []
+
+    def load(self, name, src=None, to=None):
+        to = self.r[name] if to is None else to
+        c = self.count.local(self.r["in_" + (src or name)], to)
+        c.start()
+        self.moves[src or name] = c
+
+    def ready(self, *names):
+        for name in names:
+            self.moves.pop(name).wait()
+
+    def step(self, t, first, upto):
+        for back, name in ((0, "step_core"), (1, "step_one"), (2, "step_two"), (3, "step_three")):
+            g = first + t - back
+            if first <= g < upto:
+                for u in self.groups[g]:
+                    getattr(u, name)()
+                if back == 0 and g + 2 < EARLY:
+                    for u in self.groups[g + 2]:
+                        u.load()
+                if back == 3:
+                    for w in self.closing[g]:
+                        self.swaps[w].begin()
+
+    def tick(self):
+        self.step(self.now, 0, EARLY)
+        self.now += 1
+
+    def drain_early(self):
+        p = self.p
+        while self.now < EARLY + 3:
+            self.tick()
+        for units in self.groups[:EARLY]:
+            for u in units:
+                u.sent()
+        ids = [p.at(z=p.other_z(k)) for k in range(1, p.depth)] + [p.at(y=1 - p.y), p.at(x=1 - p.x), p.at(c=1 - p.c)]
+        for d in ids:
+            pl.semaphore_signal(self.r["free"], inc=1, device_id=d, device_id_type=MESH)
+        self.partners, self.open = len(ids), False
+
+    def swap(self, *groups):
+        if not self.open:
+            pl.semaphore_wait(self.r["free"], self.partners)
+            self.open = True
+        for gi in groups:
+            for u in self.groups[gi]:
+                u.swap()
+
+    def late(self, t):
+        self.step(t, EARLY, len(self.groups))
+
+    def save(self, value, name):
+        c = self.count.local(value, self.r["out_" + name])
+        c.start()
+        self.saves.append(c)
+
+    def send_sums(self, sums):
+        r, p = self.r, self.p
+        total = self.ndp * self.ncore
+        wide = sums.shape[1] // self.ndp
+        part = wide // 2
+        pad = r["gs"].shape[2] - part
+        value = sums[...].astype(BF16).astype(F32)
+        blank = jnp.zeros((8, pad), F32)
+        for i in range(self.ndp):
+            low = value[:4, i * wide : i * wide + part]
+            high = value[:4, i * wide + part : (i + 1) * wide]
+            r["gs"][i] = jnp.concatenate([jnp.concatenate([low, high], axis=0), blank], axis=1)
+        me = p.flat(self.ncore)
+        self.spread = []
+        for k, t, d in self.every:
+            c = self.count.remote(r["gs"].at[t // self.ncore], r["ggot"].at[me], d)
+            c.start()
+            self.spread.append(c)
+        r["ggot"][me] = r["gs"][me // self.ncore]
+
+    def condition_back(self, pre2):
+        r, p = self.r, self.p
+        total = self.ndp * self.ncore
+        rows = total * 8
+        for c in self.spread:
+            c.wait_recv()
+        modw = r["modw"]
+        deep, wide = modw.shape
+        part = wide // 2
+        got = r["ggot"][...].reshape(rows, r["ggot"].shape[2])[:, :part].astype(BF16)
+        mine = split_columns(silu(pre2[...]), p.x * 2 + p.c, self.ncore, deep)
+        high = pltpu.roll(mine, 4, 0).astype(BF16)
+        r["mg"][...] = jnp.concatenate([tn(mine.astype(BF16), got), tn(high, got)], axis=1)
+        back = nt(got, modw[:, :part]) + pltpu.roll(nt(got, modw[:, part:]), rows - 4, 0)
+        live = lax.broadcasted_iota(jnp.int32, (rows, 1), 0) % 8 < 4
+        back = jnp.where(live, back, 0.0)
+        pad = r["ds"].shape[2] - deep
+        block = self.ncore * 8
+        r["ds"][...] = jnp.concatenate([back, jnp.zeros((rows, pad), F32)], axis=1).reshape(self.ndp, block, deep + pad)
+        dp, fsdp = p.z * 2 + p.y, p.x * 2 + p.c
+        self.sums = []
+        for k in range(1, self.ndp):
+            i = lax.rem(dp + k, self.ndp)
+            c = self.count.remote(r["ds"].at[i], r["dgot"].at[dp], (i, fsdp))
+            c.start()
+            self.sums.append(c)
+        r["dgot"][dp] = r["ds"][dp]
+
+    def condition_spread(self):
+        r, p = self.r, self.p
+        for c in self.sums:
+            c.wait_recv()
+        value = r["dgot"][0]
+        for i in range(1, self.ndp):
+            value = value + r["dgot"][i]
+        block = self.ncore * 8
+        at = lax.broadcasted_iota(jnp.int32, (self.ncore * 4, block), 0)
+        of = lax.broadcasted_iota(jnp.int32, (self.ncore * 4, block), 1)
+        pick_rows = jnp.where(of == (at // 4) * 8 + at % 4, 1.0, 0.0).astype(BF16)
+        me = p.flat(self.ncore)
+        r["cgot"][me] = nn(pick_rows, value.astype(BF16)).astype(BF16)
+        self.last = []
+        for k, t, d in self.every:
+            c = self.count.remote(r["cgot"].at[me], r["cgot"].at[me], d)
+            c.start()
+            self.last.append(c)
+
+    def time_back(self, pre1, pre2, tout):
+        r, p = self.r, self.p
+        total = self.ndp * self.ncore
+        rows = total * 8
+        deep = r["modw"].shape[0]
+        for c in self.last:
+            c.wait_recv()
+        small = self.ncore * 4
+        cols = []
+        for j in range(self.ncore):
+            cols.append(jnp.concatenate([r["cgot"][i * self.ncore + j][:, :deep] for i in range(self.ndp)], axis=0))
+        dense = jnp.concatenate(cols, axis=1)
+        count = self.ndp * small
+        at = lax.broadcasted_iota(jnp.int32, (rows, count), 0)
+        of = lax.broadcasted_iota(jnp.int32, (rows, count), 1)
+        spread = jnp.where((at % 8 < 4) & (of == (at // 8) * 4 + at % 8), 1.0, 0.0).astype(BF16)
+        one, two = pre1[...], pre2[...]
+        back_two = nn(spread, dense) * silu_back(two)
+        back_one = fine_nn(back_two, tout[...]) * silu_back(one)
+        hidden = silu(one)
+        dp, fsdp = p.z * 2 + p.y, p.x * 2 + p.c
+        wide = r["tog"].shape[1]
+        left = split_columns(hidden, fsdp, self.ncore, r["tog"].shape[0])
+        r["tog"][...] = fine_tn(left, split_columns(back_two, dp, self.ndp, wide))
+        emb = r["eall"][...].reshape(rows, FREQ)
+        left = split_columns(emb, fsdp, self.ncore, r["tig"].shape[0])
+        r["tig"][...] = fine_tn(left, split_columns(back_one, dp, self.ndp, wide))
+
+    def finish(self):
+        for units in self.groups[EARLY:]:
+            for u in units:
+                u.sent()
+        for s in self.swaps:
+            s.finish()
+        for c in self.spread + self.sums + self.last:
+            c.wait_send()
+        for c in self.saves:
+            c.wait()
+
+
+def silu_back(v):
+    s = 1.0 / (1.0 + jnp.exp(-v))
+    return s * (1.0 + v * (1.0 - s))
+
+
+def fine_tn(left, right):
+    a, b, c = three(left)
+    d, e, f = three(right)
+    return tn(a, d) + (tn(a, e) + tn(b, d)) + (tn(b, e) + tn(a, f) + tn(c, d))
+
+
+def backward_linked(links, r, lens, tlens, keep, mod, text, rs, sums):
+    frames, width = r["stage"].shape
+    slots = text.shape[0]
+    qa, att, m, xh, wo, dq, datt, stage, tmp = [r[n] for n in ("qa", "att", "m", "xh", "wo", "dq", "datt", "stage", "tmp")]
+    packed, dpack, acc = r["packed"], r["dpack"], r["acc"]
+    mem = packed.at[pl.ds(0, slots), pl.ds(0, 2 * width)]
+    dmem = dpack.at[pl.ds(0, slots), pl.ds(0, 2 * width)]
+    grads = r["flat"]
+    links.load("dq", "b2")
+    links.load("att", "att2")
+    links.load("wo", "wco")
+    links.load("qa", "qa2")
+    links.load("mem", to=mem)
+    links.load("m", "m2")
+    links.load("xh", "xh2")
+    links.load("stage", "g")
+    links.load("wsp")
+    fill_masks(lens, tlens, r["aq"], r["aks"], r["akc"])
+    links.ready("b2", "att2", "wco")
+    grads(4, dq, att, width)
+    datt[...] = nn(dq[...], wo[...]).astype(BF16)
+    links.load("wo", "wcq")
+    links.ready("qa2", "mem")
+    links.tick()
+    attention_backward(qa, mem, 0, width, r["akc"], att, datt, dq, dmem, 0, width, acc, links.tick)
+    links.load("qa", "qa1")
+    links.load("att", "att1")
+    links.load("packed")
+    links.load("datt", "br1")
+    links.ready("m2")
+    grads(2, dq, m, width)
+    links.load("m", "m1")
+    grads(3, dmem, text, width)
+    links.ready("wcq")
+    tmp[...] = nn(dq[...], wo[...])
+    links.load("wo", "wso")
+    links.ready("xh2", "g", "br1")
+
+    def middle(at):
+        rows = pl.ds(at, TILE)
+        own = owners_column(lens, at, TILE)
+        s = stage[rows, :] + norm_back_tile(lens, at, own, mod, tmp[rows, :], xh, rs, 1, sums, width)
+        stage[rows, :] = s
+        gate_tile(lens, at, own, mod, s, datt, 0, sums, dq, width)
+
+    tiles(frames, middle)
+    links.load("xh", "xh1")
+    links.ready("att1", "wso")
+    links.tick()
+    grads(1, dq, att, width)
+    datt[...] = nn(dq[...], wo[...]).astype(BF16)
+    links.load("wo", "tout")
+    links.ready("qa1", "packed")
+    links.drain_early()
+    links.swap(4, 5)
+    steps = iter((0, 1))
+    attention_backward(qa, packed, width, 2 * width, r["aks"], att, datt, dpack, dpack, width, 2 * width, acc,
+                       lambda: links.late(next(steps)))
+    links.ready("m1", "wsp")
+    grads(0, dpack, m, width)
+    links.swap(6, 7)
+    tmp[...] = nn(dpack[...], r["wsp"][...])
+    links.late(2)
+    links.ready("xh1")
+
+    def last(at):
+        rows = pl.ds(at, TILE)
+        own = owners_column(lens, at, TILE)
+        s = stage[rows, :] + norm_back_tile(lens, at, own, mod, tmp[rows, :], xh, rs, 0, sums, width)
+        stage[rows, :] = pick(own, keep[0], keep[1], keep[2]) * s
+
+    tiles(frames, last)
+    links.send_sums(sums)
+    links.save(stage, "latents")
+    pre1, pre2 = tmp.at[pl.ds(0, r["in_pre1"].shape[0])], tmp.at[pl.ds(r["in_pre1"].shape[0], r["in_pre1"].shape[0])]
+    links.load("pre2", to=pre2)
+    links.load("pre1", to=pre1)
+    links.late(3)
+    links.ready("pre2")
+    links.condition_back(pre2)
+    links.late(4)
+    links.condition_spread()
+    links.late(5)
+    links.ready("pre1", "tout")
+    links.time_back(pre1, pre2, wo)
+    for t in range(6, len(SUM_GROUPS) - EARLY + 3):
+        links.late(t)
+
+
+def reduce_backward(mesh, lens, tlens, keep, small, big, grads_ff, tables):
+    ndp, ncore = mesh.shape["dp"], mesh.shape["fsdp"]
+    depth, total = ndp // 2, ndp * ncore
+    d = big["wso"].shape[0]
+    t = big["g"].shape[0]
+    x = small["text"].shape[0]
+    cols = (3 * d, d, d, 2 * d, d, grads_ff[0].shape[0], grads_ff[1].shape[0])
+    rows_of = (d, d, d, d, d, grads_ff[0].shape[1], grads_ff[1].shape[1])
+    shapes = [(c // ndp, rw // ncore) for c, rw in zip(cols, rows_of)]
+    vm = lambda shape, kind=BF16: pltpu.VMEM(shape, kind)
+    wide = HEADS * PAIR
+    deep, mcols = small["modw"].shape
+    padded = -(-(mcols // 2) // 128) * 128
+    dpad = -(-deep // 128) * 128
+    tin_rows, t_cols = FREQ // ncore, d // ndp
+    scratch = dict(
+        qa=vm((t, wide)), att=vm((t, d)), m=vm((t, d)), xh=vm((t, d)), wo=vm((d, d)), dq=vm((t, d)), datt=vm((t, d)),
+        stage=vm((t, d), F32), tmp=vm((t, d), F32), packed=vm((t, 3 * d)), dpack=vm((t, 3 * d)), wsp=vm((3 * d, d)),
+        acc=vm((PAIR, t), F32), aq=vm((t, PAIR)), aks=vm((t, PAIR)), akc=vm((x, PAIR)), sums=vm((16, 9 * d), F32),
+        gs=vm((ndp, 8, padded), F32), ggot=vm((total, 8, padded), F32), ds=vm((ndp, ncore * 8, dpad), F32),
+        dgot=vm((ndp, ncore * 8, dpad), F32), cgot=vm((total, ncore * 4, dpad)),
+    )
+    for w in range(5):
+        c8, share = shapes[w]
+        scratch[f"grad{w}"] = vm((depth, 2, c8, share * ncore))
+    for w, (c8, share) in enumerate(shapes):
+        scratch[f"final{w}"] = vm((c8 // 2, 2 * share), F32)
+        scratch[f"part{w}"] = vm((c8 // 2, share), F32)
+    dims = lambda u: unit_shape(u, shapes)
+    size = {}
+    for gi, g in enumerate(SUM_GROUPS):
+        early = gi < EARLY
+        for k, u in enumerate(g):
+            _, _, n, _, nl, route, _ = dims(u)
+            key = (gi - (0 if early else EARLY), k)
+            size.setdefault(key, {})[early] = (n, nl, route)
+    slot_names = {}
+    for (gi, k), kinds in size.items():
+        same = len(kinds) == 2 and kinds[True] == kinds[False]
+        for early, (n, nl, route) in kinds.items():
+            tag = f"slot{gi}_{k}" + ("" if same else ("e" if early else "l"))
+            slot_names[(gi + (0 if early else EARLY), k)] = tag
+            if tag + "a" not in scratch:
+                scratch[tag + "a"] = vm((2, depth, 2, n, nl))
+                scratch[tag + "b"] = vm((depth, 2, n, nl) if route == 0 else (2, depth, n, nl))
+                scratch[tag + "c"] = vm((depth, n, nl))
+                scratch[tag + "d"] = vm((depth - 1, n, nl))
+    for gi in range(EARLY):
+        for k, u in enumerate(SUM_GROUPS[gi]):
+            _, _, n, _, nl, _, _ = dims(u)
+            scratch[f"own{gi % 2}_{k}"] = vm((2, depth, 2, n, nl))
+    ns = sum(len(g) * (4 + 2 + depth - 1) for g in SUM_GROUPS) + len(shapes) + 2 * (total - 1) + ndp + 40
+    scratch.update(send=pltpu.SemaphoreType.DMA((ns,)), recv=pltpu.SemaphoreType.DMA((ns,)), free=pltpu.SemaphoreType.REGULAR)
+    names = list(scratch)
+    small_names, big_names = list(small), list(big)
+    outs = dict(latents=((t, d), F32), mg=((deep, mcols), F32), tig=((tin_rows, t_cols), F32), tog=((d // ncore, t_cols), F32))
+
+    def kernel(*refs):
+        lens, tlens, keep = refs[:3]
+        at = 3
+        r = {}
+        for n in small_names:
+            r["sums_in" if n == "sums" else n] = refs[at]
+            at += 1
+        for n in big_names:
+            r["in_" + n] = refs[at]
+            at += 1
+        ff = refs[at : at + 2]
+        at += 2
+        r["out_latents"] = refs[at]
+        r["mg"], r["tig"], r["tog"] = refs[at + 1 : at + 4]
+        at += 4
+        r["shares"] = refs[at : at + len(shapes)]
+        at += len(shapes)
+        r.update(zip(names, refs[at:]))
+        r["grads"] = [r[f"grad{w}"] for w in range(5)] + list(ff)
+        r["final"] = [r[f"final{w}"] for w in range(len(shapes))]
+        r["part"] = [r[f"part{w}"] for w in range(len(shapes))]
+        r["sums"][...] = r["sums_in"][...]
+
+        def flat(w, left, right, width):
+            out = r[f"grad{w}"]
+            c8 = shapes[w][0]
+            per = ndp
+            while per % 2 == 0 and per // 2 * c8 >= width and per // 2 * c8 % 128 == 0:
+                per //= 2
+
+            def step(i, carry):
+                cols = pl.ds(pl.multiple_of(i * per * c8, per * c8), per * c8)
+                value = tn(left[:, cols], right[...]).astype(BF16)
+                for k in range(per):
+                    b = i * per + k
+                    out[b // 2, b % 2] = value[k * c8 : (k + 1) * c8, :]
+                return carry
+
+            lax.fori_loop(0, ndp // per, step, 0)
+
+        r["flat"] = flat
+        tagged = {}
+        for (gi, k), tag in slot_names.items():
+            tagged[(gi, k)] = [r[tag + e] for e in "abcd"]
+        r["slot_of"] = tagged
+        links = BackwardLinks(mesh, shapes, r)
+        backward_linked(links, r, lens, tlens, keep, r["mod"], r["text"], r["rs"], r["sums"])
+        links.finish()
+
+    got = pl.pallas_call(
+        kernel,
+        out_shape=[sds(*outs[n]) for n in outs] + [sds(s, F32) for s in shapes],
+        in_specs=[SM] * 3 + [VM] * len(small) + [ANY] * (len(big) + 2),
+        out_specs=[ANY] + [VM] * (3 + len(shapes)),
+        scratch_shapes=list(scratch.values()),
+        cost_estimate=pl.CostEstimate(flops=int(6e10), bytes_accessed=int(8e7), transcendentals=0),
+        compiler_params=pltpu.CompilerParams(collective_id=1, has_side_effects=True, vmem_limit_bytes=63 * MIB),
+    )(lens, tlens, keep, *small.values(), *big.values(),
+      *[g.reshape(depth, 2, shapes[5 + k][0], g.shape[1]) for k, g in enumerate(grads_ff)])
+    turned = pl.pallas_call(
+        partial(turn_body, len(shapes)),
+        out_shape=[sds(s[::-1], F32) for s in shapes],
+        in_specs=[VM] * len(shapes),
+        out_specs=[VM] * len(shapes),
+    )(*got[4:])
+    return got[:4], turned
 
 
 def turn_body(nw, *refs):
     for w in range(nw):
         refs[nw + w][...] = refs[w][...].T
-
-
-def reduce(mesh, grads):
-    depth, ncore = mesh.shape["dp"] // 2, mesh.shape["fsdp"]
-    shapes = [(g.shape[0] // (2 * depth), g.shape[1] // ncore) for g in grads]
-    ns = sum(4 + 2 + depth - 1 for _ in SUM_UNITS) + len(shapes)
-    shares = pl.pallas_call(
-        partial(reduce_body, depth, shapes),
-        out_shape=[sds(s, F32) for s in shapes],
-        in_specs=[ANY] * len(grads),
-        out_specs=[VM] * len(grads),
-        scratch_shapes=[pltpu.VMEM((c8 // 2, 2 * share), F32) for c8, share in shapes]
-        + [pltpu.VMEM((c8 // 2, share), F32) for c8, share in shapes]
-        + sum_scratch(shapes, depth, SUM_UNITS)
-        + [pltpu.SemaphoreType.DMA((ns,)), pltpu.SemaphoreType.DMA((ns,))],
-        compiler_params=pltpu.CompilerParams(collective_id=1, has_side_effects=True, vmem_limit_bytes=50 * MIB),
-    )(*[g.reshape(depth, 2, c8, g.shape[1]) for g, (c8, _) in zip(grads, shapes)])
-    return pl.pallas_call(
-        partial(turn_body, len(shapes)),
-        out_shape=[sds(s[::-1], F32) for s in shapes],
-        in_specs=[VM] * len(grads),
-        out_specs=[VM] * len(grads),
-    )(*shares)
 
 
 HIGHEST = lax.Precision.HIGHEST
@@ -1136,8 +1521,10 @@
     return lax.psum_scatter(part, "fsdp", scatter_dimension=0, tiled=True).astype(F32)
 
 
-def fits(mesh, weights):
+def fits(mesh, frames, weights):
     if mesh.shape["fsdp"] != 4 or mesh.shape["dp"] % 2:
+        return False
+    if mesh.shape["dp"] * mesh.shape["fsdp"] * 16 > frames:
         return False
     return all(w.shape[0] * 2 % 128 == 0 and w.shape[1] % 32 == 0 for w in weights)
 
@@ -1153,7 +1540,7 @@
     width = latents.shape[1]
     items = time_steps.shape[0]
     sent = (time_in, time_out) + others
-    direct = fits(mesh, sent)
+    direct = fits(mesh, latents.shape[0], sent)
     text = text_states.reshape(-1, width)
     keep, loud, embedding = plan(time_steps)
     deep, wide = modulation.shape
@@ -1163,28 +1550,31 @@
                                      modulation, sent)
         mod = saved["mod"]
         first = [saved[n] for n in SAVED[4:]]
-        embedding = saved["eall"][:, :items].reshape(-1, FREQ)
-        pre_one, pre_two = [saved[n].reshape(-1, 8, width)[:, :items].reshape(-1, width) for n in ("pre1", "pre2")]
-        t_out = full[1].astype(F32)
-        hidden = jax.nn.silu(pre_one)
-        mine = columns(jax.nn.silu(pre_two).astype(BF16), j, deep)
-    else:
-        full = [plain_gather(w) for w in sent]
-        t_in, t_out = full[0].astype(F32), full[1].astype(F32)
-        embedding = lax.all_gather(embedding, BOTH, axis=0, tiled=True)
-        pre_one = high_dot(embedding, t_in, 1, 1)
-        hidden = jax.nn.silu(pre_one)
-        pre_two = high_dot(hidden, t_out, 1, 1)
-        mine = columns(jax.nn.silu(pre_two).astype(BF16), j, deep)
-        part = jnp.dot(mine, modulation, preferred_element_type=F32).reshape(ndp, nfs * items, wide)
-        part = lax.psum_scatter(part, "fsdp", scatter_dimension=1, tiled=True)
-        rows = lax.all_to_all(part, "dp", 0, 0, tiled=True)
-        mod = jnp.pad(rows.transpose(1, 0, 2).reshape(items, -1), ((0, 8 - items), (0, 0)))
-        first = run_attention(item_lengths, text_lengths, keep, loud, mod, latents, noise_draw, text, *full[2:7])
+        weights = full[2:]
+        second = run_ff(item_lengths, mod, first[0], *weights[5:])
+        g, b2, dwd, dwu, sums = run_ff_back(item_lengths, mod, cotangent, saved["br2"], second, *weights[5:])
+        small = dict(mod=mod, text=text, rs=saved["rs"], sums=sums, modw=modulation, eall=saved["eall"])
+        big = {n: saved[n] for n in ("att2", "qa2", "mem", "m2", "xh2", "qa1", "att1", "packed", "br1", "m1", "xh1", "pre1", "pre2")}
+        big.update(b2=b2, g=g, wsp=weights[0], wso=weights[1], wcq=weights[2], wco=weights[4], tout=full[1])
+        (lat_grad, modulation_grad, time_in_grad, time_out_grad), shares = reduce_backward(
+            mesh, item_lengths, text_lengths, keep, small, big, (dwu, dwd), None)
+        return (second[5], lat_grad, time_in_grad, time_out_grad, modulation_grad, *shares)
+    full = [plain_gather(w) for w in sent]
+    t_in, t_out = full[0].astype(F32), full[1].astype(F32)
+    embedding = lax.all_gather(embedding, BOTH, axis=0, tiled=True)
+    pre_one = high_dot(embedding, t_in, 1, 1)
+    hidden = jax.nn.silu(pre_one)
+    pre_two = high_dot(hidden, t_out, 1, 1)
+    mine = columns(jax.nn.silu(pre_two).astype(BF16), j, deep)
+    part = jnp.dot(mine, modulation, preferred_element_type=F32).reshape(ndp, nfs * items, wide)
+    part = lax.psum_scatter(part, "fsdp", scatter_dimension=1, tiled=True)
+    rows = lax.all_to_all(part, "dp", 0, 0, tiled=True)
+    mod = jnp.pad(rows.transpose(1, 0, 2).reshape(items, -1), ((0, 8 - items), (0, 0)))
+    first = run_attention(item_lengths, text_lengths, keep, loud, mod, latents, noise_draw, text, *full[2:7])
     weights = full[2:]
     second = run_ff(item_lengths, mod, first[0], *weights[5:])
     out, lat_grad, *grads, sums = run_backward(item_lengths, text_lengths, keep, mod, text, cotangent, first, second, *weights)
-    shares = reduce(mesh, grads) if direct else [plain_reduce(g) for g in grads]
+    shares = [plain_reduce(g) for g in grads]
 
     sent_sums = sums[:items].astype(BF16).reshape(items, ndp, wide).transpose(1, 0, 2)
     got = lax.all_to_all(sent_sums, "dp", 0, 0, tiled=True)

time: 480 us -> 375 us (0.78)
  Pallas kernels: 412 us -> 358 us
  between operations: 14.7 us -> 1.17 us
  blocking collectives: 12.4 us -> 0 us
  starting transfers between devices: 8.37 us -> 0 us
  waiting for transfers between devices: 6.58 us -> 0 us
  matrix products: 4.9 us -> 0 us
    pallas_call x3 -> x2, Pallas kernels: 126 us -> 58.8 us  [call(): pl.pallas_call(body, out_shape=outs, in_specs=[SM] * len(scalars) + [VM]...]
    pallas_call x2, Pallas kernels: 112 us -> 154 us  [the longest x1 152 us: reduce_backward(): pl.pallas_call(kernel, out_shape=[sds(*outs[n]) for n in outs] + [sds(s,...]
    pallas_call x1, Pallas kernels: 174 us -> 145 us  [gather_forward(): pl.pallas_call(kernel, out_shape=[sds((depth, 2, c8, share * ncore)) for...]
    all_gather x2 -> x0, blocking collectives: 12.4 us -> none  [the longest x1 6.73 us: body(): back = lax.all_gather(lax.psum(back, 'dp'), 'fsdp', axis=1, tiled=True)]
    all_to_all x1 -> x0, starting transfers between devices: 8.34 us -> none  [body(): got = lax.all_to_all(sent_sums, 'dp', 0, 0, tiled=True)]
    all_to_all x1 -> x0, waiting for transfers between devices: 6.57 us -> none  [body(): got = lax.all_to_all(sent_sums, 'dp', 0, 0, tiled=True)]
    dot_general x5 -> x0, matrix products: 4.9 us -> none  [the longest x3 2.75 us: high_dot(): lax.dot_general(left, right, (((lc,), (rc,)), ((), ())), precision=HIGHES...]
  transfers between devices with their start and end apart: 2 -> 0, of which waited for: 1 -> 0; matrix products, arithmetic and copies ran while one was open for 1% -> 0% of each run, Pallas kernels for 24% -> 0%
where the time goes in v3:
time: 375 us; the launch traced here: 371 us
  Pallas kernels  358 us (95%)
  local copies, waits for them, and re-layouts  9 us (2%)
    pallas_call x1, Pallas kernels, reduce_backward(): pl.pallas_call(kernel, out_shape=[sds(*outs[n]) for n in outs] + [sds(s,...  152 us
    pallas_call x1, Pallas kernels, gather_forward(): pl.pallas_call(kernel, out_shape=[sds((depth, 2, c8, share * ncore)) for...  145 us
    pallas_call x2, Pallas kernels, call(): pl.pallas_call(body, out_shape=outs, in_specs=[SM] * len(scalars) + [VM]...  58.8 us
    unnamed x12, local copies, waits for them, and re-layouts  9 us

profile of v3, /device:TPU:0, one launch (start us, length us, event | category | flops | bytes accessed | tf_op | source)
XLA Modules:
  0.0 370.6 jit_solution(5825257471331549972)
XLA Ops:
  0.6 0.7 convert_element_type.5
  1.3 1.2 subtract_sqrt_fusion
  2.5 0.1 multiply_cosine_fusion
  2.7 0.6 select_maximum_fusion.refs_4_
  3.3 1.7 copy.29.refs_17_
  5.0 144.6 %shard_map.256 = (bf16[4,2,96,256]{3,2,1,0:T(8,128)(2,1)}, bf16[4,2,96,768]{3,2,1,0:T(8,128)(2,1)}, bf16[4,2,288,768]{3,2,1,0:T(8,128)(2,1)}, bf16[4,2,96,768]{3...) custom-call(s32[1,3]{1,0:T(1,128)} %refs_0_.3, ...), custom_call_target="tpu_custom_call" | custom-call | flops 30000001024 | bytes 60000000 | tf_op jit(solution)/shard_map/pallas_call | solution.py:904
  149.6 25.0 %shard_map.257 = (bf16[768,768]{1,0:T(8,128)(2,1)}, bf16[768,768]{1,0:T(8,128)(2,1)}, bf16[768,3072]{1,0:T(8,128)(2,1)}, bf16[768,3072]{1,0:T(8,128)(2,1)}, bf16...) custom-call(s32[1,3]{1,0:T(1,128)} %refs_0_.3, f32[8,6912]{1,0:T(8,128)} %get-tuple-element.67.mod.refs_3_, ...), custom_call_target="tpu_custom_call" | custom-call | flops 10000000000 | bytes 30000000 | tf_op jit(solution)/shard_map/pallas_call | solution.py:454
  174.6 33.9 %shard_map.258 = (f32[768,768]{1,0:T(8,128)}, bf16[768,768]{1,0:T(8,128)(2,1)}, bf16[768,3072]{1,0:T(8,128)(2,1)}, bf16[3072,768]{1,0:T(8,128)(2,1)}, f32[16,6912]{1,0:T(8,128)}) custom-call(s32[1,3]{1,0:T(1,128)} %refs_0_.3, f32[8,6912]{1,0:T(8,128)} %get-tuple-element.67.mod.refs_3_, bf16[768,768]{1,0:T(8,128)(2,1)} %cot.1, ...), custom_call_target="tpu_custom_call" | custom-call | flops 30000001024 | bytes 30000000 | tf_op jit(solution)/shard_map/pallas_call | solution.py:454
  208.5 151.7 %shard_map.259 = (f32[768,768]{1,0:T(8,128)}, f32[192,864]{1,0:T(8,128)}, f32[64,96]{1,0:T(8,128)}, f32[192,96]{1,0:T(8,128)}, f32[288,192]{1,0:T(8,128)}, /*ind...) custom-call(s32[1,3]{1,0:T(1,128)} %refs_0_.3, ...), custom_call_target="tpu_custom_call" | custom-call | flops 60000002048 | bytes 80000000 | tf_op jit(solution)/shard_map/pallas_call | solution.py:1467
  360.2 2.7 shard_map.260
  362.9 1.9 copy.30
  364.7 0.0 copy-start.2
  364.7 0.0 copy-start.1
  364.7 0.0 copy-start
  364.7 3.3 copy.35
  368.0 0.0 copy-done.2
  368.0 0.6 copy.36
  368.6 0.0 copy-done.1
  368.7 0.6 copy.37
  369.3 0.0 copy-done
  369.3 0.8 copy.38
  (1 shorter events, 0.0 us)
Async XLA Ops:
  364.7 3.3 copy-start.2
  364.7 3.9 %copy-start.1 = (f32[192,96]{1,0:T(8,128)S(1)}, f32[192,96]{1,0:T(8,128)}, u32[]{:S(2)}) copy-start(f32[192,96]{1,0:T(8,128)} %get-tuple-element.153) | copy-start | bytes 221188
  364.7 4.6 %copy-start = (f32[192,864]{1,0:T(8,128)S(1)}, f32[192,864]{1,0:T(8,128)}, u32[]{:S(2)}) copy-start(f32[192,864]{1,0:T(8,128)} %get-tuple-element.154) | copy-start | bytes 1990660

commit v4 on v3

--- a/solution.py
+++ b/solution.py
@@ -136,7 +136,7 @@
     in_parts(pair, pump)
 
 
-def attention_backward(qaug, k, k_at, v_at, ak, att, datt, dq, dk, dk_at, dv_at, acc, pump=None):
+def attention_backward(qaug, k, k_at, v_at, ak, att, datt, dq, dk, dk_at, dv_at, acc, pump=None, step_pairs=3):
     frames = att.shape[0]
     tall = k.shape[0]
     step = TILE if tall % TILE == 0 else PAIR
@@ -181,7 +181,7 @@
         dq[:, lanes] = (acc[...].T * FACTOR).astype(BF16)
         return carry
 
-    in_parts(pair, pump)
+    in_parts(pair, pump, step_pairs)
 
 
 def norm_tile(s):
@@ -283,7 +283,7 @@
         norm_into(s, rows, own, lens, mod, 1, xh2, m2, rs, width)
 
     tiles(frames, middle)
-    links.done("br1", "xh2", "m2", "rs")
+    links.done("br1", "xh2", "m2")
     links.use("wcq", "wcm")
     big_nt(m2, wcq, qb, width)
     big_nt(text, wcm, mem, width)
@@ -301,10 +301,18 @@
         stream[rows, :] = stream[rows, :] + expand(own, mod, 5, width) * br
 
     tiles(frames, last)
-    links.done("br2", "stream")
+    links.done("br2")
 
 
 GELU_A, GELU_B = math.sqrt(2.0 / math.pi), 0.044715
+
+
+def gelu_tile(x, rows, act, slope):
+    sq = x * x
+    t = jnp.tanh(x * (GELU_A + GELU_A * GELU_B * sq))
+    half = 0.5 + 0.5 * t
+    act[rows, :] = (x * half).astype(BF16)
+    slope[rows, :] = (half + half * (1.0 - t) * x * (GELU_A + 3.0 * GELU_A * GELU_B * sq)).astype(BF16)
 
 
 def forward_ff(lens, mod, stream, wup, wdn, xh3, m3, act, slope, br3, out, rs, tmp):
@@ -324,12 +332,7 @@
 
         def gelu(at):
             rows = pl.ds(at, TILE)
-            x = tmp[rows, :]
-            sq = x * x
-            t = jnp.tanh(x * (GELU_A + GELU_A * GELU_B * sq))
-            half = 0.5 + 0.5 * t
-            act[rows, cols] = (x * half).astype(BF16)
-            slope[rows, cols] = (half + half * (1.0 - t) * x * (GELU_A + 3.0 * GELU_A * GELU_B * sq)).astype(BF16)
+            gelu_tile(tmp[rows, :], rows, act.at[:, cols], slope.at[:, cols])
 
         tiles(frames, gelu)
         return carry
@@ -546,18 +549,13 @@
     def other_z(self, k):
         return lax.rem(self.z + k, self.depth)
 
-    def barrier(self, every=None):
+    def greet(self, every):
         bar = pltpu.get_barrier_semaphore()
-        if every is not None:
-            for d in every:
-                pl.semaphore_signal(bar, inc=1, device_id=d, device_id_type=MESH)
-            pl.semaphore_wait(bar, len(every))
-            return
-        ids = [self.at(z=self.other_z(k)) for k in range(1, self.depth)]
-        ids += [self.at(y=1 - self.y), self.at(x=1 - self.x), self.at(c=1 - self.c)]
-        for d in ids:
+        for d in every:
             pl.semaphore_signal(bar, inc=1, device_id=d, device_id_type=MESH)
-        pl.semaphore_wait(bar, len(ids))
+
+    def meet(self, count):
+        pl.semaphore_wait(pltpu.get_barrier_semaphore(), count)
 
 
 class Counter:
@@ -708,11 +706,12 @@
         self.every = others(p, self.ndp, self.ncore)
         nw = len(shapes)
         turned, landed, block = r["turned"], r["landed"], r["block"]
+        p.greet([d for _, _, d in self.every])
         for w in range(nw):
             turned[w][...] = r["shards"][w][...].T
         me = p.flat(self.ncore)
         r["eall"][me] = r["emb"][...]
-        p.barrier([d for _, _, d in self.every])
+        p.meet(len(self.every))
         self.spread = []
         swaps = []
         for w, (c8, share) in enumerate(shapes):
@@ -735,7 +734,7 @@
         self.units = [[GatherUnit(u, shapes, p, count, block, r["full"]) for u in g] for g in GROUPS]
         self.swaps, self.begun = swaps, 0
         self.start(AHEAD)
-        self.now, self.fetched, self.waiting, self.saves = 0, {}, {}, []
+        self.now, self.fetched, self.saves = 0, {}, {}
         self.pump = self.tick
 
     def start(self, upto):
@@ -769,13 +768,29 @@
                 self.tick()
             for i, k in mine:
                 self.units[i][k].settled()
-            c8 = self.shapes[w][0]
             self.fetched[name] = []
-            for z in range(self.p.depth):
-                for y in range(2):
-                    c = self.count.local(self.r["full"][w].at[z, y], self.r[name].at[pl.ds((2 * z + y) * c8, c8), :])
-                    c.start()
-                    self.fetched[name].append(c)
+            for src, dst in self.places(name, w):
+                c = self.count.local(src, dst)
+                c.start()
+                self.fetched[name].append(c)
+
+    def places(self, name, w):
+        r, c8 = self.r, self.shapes[w][0]
+        found = []
+        for z in range(self.p.depth):
+            for y in range(2):
+                b, src = 2 * z + y, r["full"][w].at[z, y]
+                if name == "wup":
+                    width = src.shape[1]
+                    n, at = b * c8 // width, b * c8 % width
+                    found.append((src, self.ups[n].at[pl.ds(at, c8), :]))
+                elif name == "wdn":
+                    for n, down in enumerate(self.downs):
+                        width = down.shape[1]
+                        found.append((src.at[:, pl.ds(n * width, width)], down.at[pl.ds(b * c8, c8), :]))
+                else:
+                    found.append((src, r[name].at[pl.ds(b * c8, c8), :]))
+        return found
 
     def use(self, *names):
         self.fetch(*names)
@@ -828,9 +843,16 @@
 
     def done(self, *names):
         for name in names:
-            c = self.count.local(self.r[name], self.r["out_" + name])
-            c.start()
-            self.saves.append(c)
+            self.save(name, self.r[name], self.r["out_" + name])
+
+    def save(self, name, value, to):
+        c = self.count.local(value, to)
+        c.start()
+        self.saves[name] = c
+
+    def saved(self, *names):
+        for name in names:
+            self.saves.pop(name).wait()
 
     def finish(self):
         while self.now < len(self.units) + 2:
@@ -842,12 +864,64 @@
                 unit.finish()
         for c in self.swaps + self.spread + self.parts:
             c.wait_send()
-        for c in self.saves:
+        for c in self.saves.values():
             c.wait()
 
 
-SAVED = ("mod", "pre1", "pre2", "eall", "stream", "xh1", "m1", "packed", "qa1", "att1", "br1", "xh2", "m2", "mem", "qa2",
-         "att2", "br2", "rs")
+def forward_ff_linked(links, r, lens, mod):
+    stream, tmp = r["stream"], r["tmp"]
+    frames, width = stream.shape
+    block = lambda ref, k: ref.at[:, pl.ds(k * width, width)]
+    links.ups = [r["wsp"].at[pl.ds(k * width, width)] for k in range(3)] + [r["wso"]]
+    links.downs = [r["wcq"], r["wcm"].at[pl.ds(0, width)], r["wcm"].at[pl.ds(width, width)], r["wco"]]
+    acts = [block(r["packed"], k) for k in range(3)] + [r["qb"]]
+    slopes = [block(r[q], k) for q in ("qa1", "qa2") for k in range(2)]
+    links.fetch("wup")
+    links.saved("xh1", "m1", "packed", "qa1", "qa2", "att1", "br1")
+
+    def start(at):
+        rows = pl.ds(at, TILE)
+        own = owners_column(lens, at, TILE)
+        norm_into(stream[rows, :], rows, own, lens, mod, 2, r["xh1"], r["m1"], r["rs"], width)
+
+    tiles(frames, start)
+    links.save("xh3", r["xh1"], r["out_xh3"])
+    links.save("m3", r["m1"], r["out_m3"])
+    links.done("rs")
+    links.use("wup")
+    for n in range(len(acts)):
+        act, slope = acts[n], slopes[n]
+        tmp[...] = nt(r["m1"][...], links.ups[n][...])
+
+        def gelu(at):
+            rows = pl.ds(at, TILE)
+            gelu_tile(tmp[rows, :], rows, act, slope)
+
+        tiles(frames, gelu)
+        cols = pl.ds(n * width, width)
+        links.save(f"act{n}", act, r["out_act"].at[:, cols])
+        links.save(f"slope{n}", slope, r["out_slope"].at[:, cols])
+        if n % 2 == 1:
+            links.tick()
+    links.use("wdn")
+    tmp[...] = nt(acts[0][...], links.downs[0][...])
+    for n in range(1, len(acts)):
+        tmp[...] += nt(acts[n][...], links.downs[n][...])
+
+    def last(at):
+        rows = pl.ds(at, TILE)
+        own = owners_column(lens, at, TILE)
+        br = tmp[rows, :]
+        r["br1"][rows, :] = br.astype(BF16)
+        r["att1"][rows, :] = (stream[rows, :] + expand(own, mod, 8, width) * br).astype(BF16)
+
+    tiles(frames, last)
+    links.save("br3", r["br1"], r["out_br3"])
+    links.save("out", r["att1"], r["out_out"])
+
+
+SAVED = ("mod", "pre1", "pre2", "eall", "xh1", "m1", "packed", "qa1", "att1", "br1", "xh2", "m2", "mem", "qa2",
+         "att2", "br2", "rs", "xh3", "m3", "act", "slope", "br3", "out")
 
 
 def gather_forward(mesh, lens, tlens, keep, loud, emb, lat, noi, text, modw, shards):
@@ -856,19 +930,22 @@
     shapes = [(w.shape[1], w.shape[0]) for w in shards]
     nw = len(shapes)
     t, d = lat.shape
+    ff = shards[7].shape[1] * ndp
     x, wide = text.shape[0], HEADS * PAIR
     vm = lambda shape, kind=BF16: pltpu.VMEM(shape, kind)
     part = modw.shape[1] // 2
     padded = -(-part // 128) * 128
     kept = {
         "mod": ((8, 9 * d), F32), "pre1": ((total * 8, d), F32), "pre2": ((total * 8, d), F32),
-        "eall": ((total, 8, FREQ), F32), "stream": ((t, d), F32), "xh1": ((t, d), BF16), "m1": ((t, d), BF16),
+        "eall": ((total, 8, FREQ), F32), "xh1": ((t, d), BF16), "m1": ((t, d), BF16),
         "packed": ((t, 3 * d), BF16), "qa1": ((t, wide), BF16), "att1": ((t, d), BF16), "br1": ((t, d), BF16),
         "xh2": ((t, d), BF16), "m2": ((t, d), BF16), "mem": ((x, 2 * d), BF16), "qa2": ((t, wide), BF16),
-        "att2": ((t, d), BF16), "br2": ((t, d), BF16), "rs": ((t, 128), F32),
+        "att2": ((t, d), BF16), "br2": ((t, d), BF16), "rs": ((t, 128), F32), "xh3": ((t, d), BF16), "m3": ((t, d), BF16),
+        "act": ((t, ff), BF16), "slope": ((t, ff), BF16), "br3": ((t, d), BF16), "out": ((t, d), BF16),
     }
     full = [(c8 * ndp, share * ncore) for c8, share in shapes]
-    scratch = {name: vm(*kept[name]) for name in SAVED}
+    scratch = {name: vm(*kept[name]) for name in SAVED[: SAVED.index("xh3")] if name != "stream"}
+    scratch["stream"] = vm((t, d), F32)
     for w, name in enumerate(ForwardLinks.NAMES[:7]):
         scratch[name] = vm(full[w])
     scratch.update(aq=vm((t, PAIR)), aks=vm((t, PAIR)), akc=vm((x, PAIR)), qb=vm((t, d)), tmp=vm((t, d), F32))
@@ -877,7 +954,7 @@
         scratch[f"turned{w}"] = vm((c8, share))
         scratch[f"landed{w}"] = vm((c8 // 2, share))
         scratch[f"block{w}"] = vm((c8 // 2, 2 * share))
-    ns = 9 + 2 * (total - 1) + len(SAVED) + 7 * ndp
+    ns = 9 + 2 * (total - 1) + 2 * len(SAVED) + 12 * ndp
     ns += sum(1 + (depth - 1) + depth + depth * (1 if u[5] == 0 else 2) + 2 for u in UNITS)
     scratch.update(send=pltpu.SemaphoreType.DMA((ns,)), recv=pltpu.SemaphoreType.DMA((ns,)))
     names = list(scratch)
@@ -899,6 +976,7 @@
                           *[r[n] for n in ("wsp", "wso", "wcq", "wcm", "wco", "stream", "xh1", "m1", "packed", "qa1",
                                            "att1", "br1", "xh2", "m2", "mem", "qa2", "att2", "br2", "rs", "aq", "aks",
                                            "akc", "qb", "tmp")])
+        forward_ff_linked(links, r, lens, r["mod"])
         links.finish()
 
     got = pl.pallas_call(
@@ -921,10 +999,13 @@
     ((5, 1 / 2, 1 / 4, 0, 2, 0), (5, 3 / 4, 1 / 4, 0, 2, 1)),
     ((4, 0, 1, 0, 2, 0), (2, 0, 1, 0, 2, 1)),
     ((3, 0, 1 / 2, 0, 2, 0), (3, 1 / 2, 1 / 2, 0, 2, 1)),
-    ((1, 0, 1, 0, 2, 0), (0, 0, 1 / 3, 0, 2, 1)),
-    ((0, 1 / 3, 1 / 3, 0, 2, 0), (0, 2 / 3, 1 / 3, 0, 2, 1)),
+    ((1, 0, 1, 0, 2, 0),),
+    ((0, 0, 1 / 3, 0, 2, 0), (0, 1 / 3, 1 / 3, 0, 2, 1)),
+    ((0, 2 / 3, 1 / 3, 0, 2, 1),),
 )
 EARLY = 4
+SLOTS = (((0, 0), (0, 1)), ((1, 0), (1, 1)), ((2, 0),), ((3, 0), (3, 1)), ((2, 1),))
+ORDER = (0, 1, 2, 3, 4, 5, 6, None, 7, 8, None, None, None)
 
 
 def each(count, fn):
@@ -936,7 +1017,7 @@
 
 
 def plus(a, b):
-    return (a.astype(F32) + b.astype(F32)).astype(BF16)
+    return a + b
 
 
 class SumUnit:
@@ -1076,25 +1157,46 @@
         self.p = p = Place(self.ndp // 2)
         self.count = count = Counter(r["send"], r["recv"])
         self.every = others(p, self.ndp, self.ncore)
-        p.barrier([d for _, _, d in self.every])
-        self.groups, self.now = [], 0
+        p.greet([d for _, _, d in self.every])
+        self.groups, self.now, self.opened, self.given, self.through = [], 0, set(), set(), set()
         for gi, g in enumerate(SUM_GROUPS):
             early = gi < EARLY
             units = []
             for k, u in enumerate(g):
                 own = r[f"own{gi % 2}_{k}"] if early else None
-                units.append(SumUnit(u, shapes, p, count, r["grads"], own, r["slot_of"][(gi, k)], r["final"]))
+                units.append(SumUnit(u, shapes, p, count, r["grads"], own, r["slot_of"][(gi, k) if early else SLOTS[gi - EARLY][k]], r["final"]))
             self.groups.append(units)
         self.swaps = [LastSwap(w, shapes, p, count, r["final"], r["part"], r["shares"]) for w in range(len(shapes))]
         last = {u[0]: gi for gi, g in enumerate(SUM_GROUPS) for u in g}
         self.closing = {gi: [w for w, l in last.items() if l == gi] for gi in range(len(SUM_GROUPS))}
-        for units in self.groups[:EARLY]:
-            for u in units:
+        self.moves, self.saves, self.writes = {}, [], []
+
+    def met(self):
+        self.p.meet(len(self.every))
+
+    def write(self, value, to):
+        c = self.count.local(value, to)
+        c.start()
+        self.writes.append(c)
+
+    def written(self):
+        for c in self.writes:
+            c.wait()
+        self.writes = []
+
+    def early(self, *groups):
+        for gi in groups:
+            for u in self.groups[gi]:
                 u.swap()
-        for units in self.groups[:2]:
-            for u in units:
-                u.load()
-        self.moves, self.saves = {}, []
+            self.given.add(gi)
+        self.load_own()
+
+    def load_own(self):
+        for gi in sorted(self.given):
+            if gi < 2 or gi - 2 in self.through:
+                for u in self.groups[gi]:
+                    u.load()
+                self.given.remove(gi)
 
     def load(self, name, src=None, to=None):
         to = self.r[name] if to is None else to
@@ -1102,49 +1204,47 @@
         c.start()
         self.moves[src or name] = c
 
+    def load_part(self, name, src, to):
+        c = self.count.local(src, to)
+        c.start()
+        self.moves[name] = c
+
     def ready(self, *names):
         for name in names:
             self.moves.pop(name).wait()
 
-    def step(self, t, first, upto):
+    def tick(self):
+        t, self.now = self.now, self.now + 1
         for back, name in ((0, "step_core"), (1, "step_one"), (2, "step_two"), (3, "step_three")):
-            g = first + t - back
-            if first <= g < upto:
-                for u in self.groups[g]:
-                    getattr(u, name)()
-                if back == 0 and g + 2 < EARLY:
-                    for u in self.groups[g + 2]:
-                        u.load()
-                if back == 3:
-                    for w in self.closing[g]:
-                        self.swaps[w].begin()
-
-    def tick(self):
-        self.step(self.now, 0, EARLY)
-        self.now += 1
-
-    def drain_early(self):
+            g = ORDER[t - back] if 0 <= t - back < len(ORDER) else None
+            if g is None:
+                continue
+            for u in self.groups[g]:
+                getattr(u, name)()
+            if back == 0:
+                self.through.add(g)
+                self.load_own()
+            if back == 3:
+                for w in self.closing[g]:
+                    self.swaps[w].begin()
+                if g < EARLY:
+                    self.release(g)
+
+    def release(self, g):
         p = self.p
-        while self.now < EARLY + 3:
-            self.tick()
-        for units in self.groups[:EARLY]:
-            for u in units:
-                u.sent()
+        for u in self.groups[g]:
+            u.sent()
         ids = [p.at(z=p.other_z(k)) for k in range(1, p.depth)] + [p.at(y=1 - p.y), p.at(x=1 - p.x), p.at(c=1 - p.c)]
         for d in ids:
-            pl.semaphore_signal(self.r["free"], inc=1, device_id=d, device_id_type=MESH)
-        self.partners, self.open = len(ids), False
-
-    def swap(self, *groups):
-        if not self.open:
-            pl.semaphore_wait(self.r["free"], self.partners)
-            self.open = True
-        for gi in groups:
-            for u in self.groups[gi]:
-                u.swap()
-
-    def late(self, t):
-        self.step(t, EARLY, len(self.groups))
+            pl.semaphore_signal(self.r["free"].at[g], inc=1, device_id=d, device_id_type=MESH)
+        self.partners = len(ids)
+
+    def swap(self, g):
+        for slot in sorted({s for s, _ in SLOTS[g - EARLY]} - self.opened):
+            pl.semaphore_wait(self.r["free"].at[slot], self.partners)
+            self.opened.add(slot)
+        for u in self.groups[g]:
+            u.swap()
 
     def save(self, value, name):
         c = self.count.local(value, self.r["out_" + name])
@@ -1269,6 +1369,88 @@
     return tn(a, d) + (tn(a, e) + tn(b, d)) + (tn(b, e) + tn(a, f) + tn(c, d))
 
 
+def backward_ff_linked(links, r, lens, mod, rs, sums):
+    frames, width = r["stage"].shape
+    quarters = r["in_wup"].shape[0] // width
+    packed, dpack, qa, wsp, dq, tmp, stage = [r[n] for n in ("packed", "dpack", "qa", "wsp", "dq", "tmp", "stage")]
+    block = lambda ref, k: ref.at[:, pl.ds(k * width, width)]
+    acts, slopes = (block(packed, 0), block(packed, 1)), (block(packed, 2), block(qa, 0))
+    downs, ups = (wsp.at[pl.ds(0, width)], wsp.at[pl.ds(width, width)]), (wsp.at[pl.ds(2 * width, width)], block(qa, 1))
+    ig, outs = block(dpack, 0), (block(dpack, 1), block(dpack, 2))
+    order = [n for n in range(0, quarters, 2)] + [n for n in range(1, quarters, 2)]
+    half = r["ffu"].shape[2]
+
+    def fetch(i):
+        n, k = order[i], i % 2
+        cols = pl.ds(n * width, width)
+        links.load_part(f"act{n}", r["in_act"].at[:, cols], acts[k])
+        links.load_part(f"down{n}", r["in_wdn"].at[:, cols], downs[k])
+        links.load_part(f"slope{n}", r["in_slope"].at[:, cols], slopes[k])
+        links.load_part(f"up{n}", r["in_wup"].at[cols, :], ups[k])
+
+    links.load("datt", "cot")
+    links.load("att", "br3")
+    fetch(0)
+    links.load("m", "m3")
+    links.load("xh", "xh3")
+    links.load("wo", "wco")
+    sums[...] = jnp.zeros_like(sums)
+    links.ready("cot", "br3")
+
+    def start(at):
+        rows = pl.ds(at, TILE)
+        own = owners_column(lens, at, TILE)
+        gate_tile(lens, at, own, mod, r["datt"][rows, :].astype(F32), r["att"], 2, sums, dq, width)
+
+    tiles(frames, start)
+    links.load("att", "br2")
+    for i, n in enumerate(order):
+        k = i % 2
+        if i + 1 < quarters:
+            fetch(i + 1)
+        links.ready(f"act{n}", f"down{n}", f"slope{n}", f"up{n}")
+        cols = pl.ds(n * width, width)
+        grad = r["grad1"] if k == 0 else r["grad2"]
+        value = tn(dq[...], acts[k][...]).astype(BF16)
+        if i >= 2:
+            links.written()
+        c8 = grad.shape[2]
+        for b in range(width // c8):
+            grad[b // 2, b % 2] = value[b * c8 : (b + 1) * c8, :]
+        links.write(grad, r["ffd"].at[:, :, :, cols])
+        ig[...] = (nn(dq[...], downs[k][...]) * slopes[k][...].astype(F32)).astype(BF16)
+        if i == 0:
+            links.ready("m3")
+        outs[k][...] = tn(ig[...], r["m"][...]).astype(BF16)
+        for y in range(2):
+            links.write(outs[k].at[pl.ds(y * half, half)], r["ffu"].at[n, y])
+        part = nn(ig[...], ups[k][...])
+        if i == 0:
+            tmp[...] = part
+        else:
+            tmp[...] += part
+        if i == 1:
+            links.written()
+            links.met()
+            links.early(0)
+        if i == quarters - 2:
+            links.tick()
+        if i == quarters - 1:
+            links.written()
+            links.early(1, 2, 3)
+    links.ready("xh3", "br2")
+
+    def last(at):
+        rows = pl.ds(at, TILE)
+        own = owners_column(lens, at, TILE)
+        s = r["datt"][rows, :].astype(F32) + norm_back_tile(lens, at, own, mod, tmp[rows, :], r["xh"], rs, 2, sums, width)
+        stage[rows, :] = s
+        gate_tile(lens, at, own, mod, s, r["att"], 1, sums, dq, width)
+
+    tiles(frames, last)
+    links.tick()
+
+
 def backward_linked(links, r, lens, tlens, keep, mod, text, rs, sums):
     frames, width = r["stage"].shape
     slots = text.shape[0]
@@ -1277,35 +1459,37 @@
     mem = packed.at[pl.ds(0, slots), pl.ds(0, 2 * width)]
     dmem = dpack.at[pl.ds(0, slots), pl.ds(0, 2 * width)]
     grads = r["flat"]
-    links.load("dq", "b2")
     links.load("att", "att2")
-    links.load("wo", "wco")
     links.load("qa", "qa2")
     links.load("mem", to=mem)
     links.load("m", "m2")
     links.load("xh", "xh2")
-    links.load("stage", "g")
     links.load("wsp")
     fill_masks(lens, tlens, r["aq"], r["aks"], r["akc"])
-    links.ready("b2", "att2", "wco")
-    grads(4, dq, att, width)
+    links.ready("wco")
     datt[...] = nn(dq[...], wo[...]).astype(BF16)
     links.load("wo", "wcq")
+    links.ready("att2")
+    grads(4, dq, att, width)
     links.ready("qa2", "mem")
     links.tick()
-    attention_backward(qa, mem, 0, width, r["akc"], att, datt, dq, dmem, 0, width, acc, links.tick)
+    steps = iter((links.tick, lambda: None))
+    attention_backward(qa, mem, 0, width, r["akc"], att, datt, dq, dmem, 0, width, acc, lambda: next(steps)())
     links.load("qa", "qa1")
     links.load("att", "att1")
     links.load("packed")
     links.load("datt", "br1")
     links.ready("m2")
     grads(2, dq, m, width)
+    links.swap(4)
     links.load("m", "m1")
     grads(3, dmem, text, width)
     links.ready("wcq")
     tmp[...] = nn(dq[...], wo[...])
     links.load("wo", "wso")
-    links.ready("xh2", "g", "br1")
+    links.tick()
+    links.swap(5)
+    links.ready("xh2", "br1")
 
     def middle(at):
         rows = pl.ds(at, TILE)
@@ -1317,21 +1501,21 @@
     tiles(frames, middle)
     links.load("xh", "xh1")
     links.ready("att1", "wso")
-    links.tick()
     grads(1, dq, att, width)
     datt[...] = nn(dq[...], wo[...]).astype(BF16)
     links.load("wo", "tout")
+    links.tick()
+    links.swap(6)
     links.ready("qa1", "packed")
-    links.drain_early()
-    links.swap(4, 5)
-    steps = iter((0, 1))
+    steps = iter((links.tick, links.tick, lambda: None))
     attention_backward(qa, packed, width, 2 * width, r["aks"], att, datt, dpack, dpack, width, 2 * width, acc,
-                       lambda: links.late(next(steps)))
+                       lambda: next(steps)(), 2)
     links.ready("m1", "wsp")
     grads(0, dpack, m, width)
-    links.swap(6, 7)
+    links.swap(7)
+    links.swap(8)
     tmp[...] = nn(dpack[...], r["wsp"][...])
-    links.late(2)
+    links.tick()
     links.ready("xh1")
 
     def last(at):
@@ -1346,26 +1530,27 @@
     pre1, pre2 = tmp.at[pl.ds(0, r["in_pre1"].shape[0])], tmp.at[pl.ds(r["in_pre1"].shape[0], r["in_pre1"].shape[0])]
     links.load("pre2", to=pre2)
     links.load("pre1", to=pre1)
-    links.late(3)
+    links.tick()
     links.ready("pre2")
     links.condition_back(pre2)
-    links.late(4)
+    links.tick()
     links.condition_spread()
-    links.late(5)
+    links.tick()
     links.ready("pre1", "tout")
     links.time_back(pre1, pre2, wo)
-    for t in range(6, len(SUM_GROUPS) - EARLY + 3):
-        links.late(t)
-
-
-def reduce_backward(mesh, lens, tlens, keep, small, big, grads_ff, tables):
+    while links.now < len(ORDER):
+        links.tick()
+
+
+def reduce_backward(mesh, lens, tlens, keep, small, big):
     ndp, ncore = mesh.shape["dp"], mesh.shape["fsdp"]
     depth, total = ndp // 2, ndp * ncore
     d = big["wso"].shape[0]
-    t = big["g"].shape[0]
+    t = big["cot"].shape[0]
+    ff = big["wup"].shape[0]
     x = small["text"].shape[0]
-    cols = (3 * d, d, d, 2 * d, d, grads_ff[0].shape[0], grads_ff[1].shape[0])
-    rows_of = (d, d, d, d, d, grads_ff[0].shape[1], grads_ff[1].shape[1])
+    cols = (3 * d, d, d, 2 * d, d, ff, d)
+    rows_of = (d, d, d, d, d, d, ff)
     shapes = [(c // ndp, rw // ncore) for c, rw in zip(cols, rows_of)]
     vm = lambda shape, kind=BF16: pltpu.VMEM(shape, kind)
     wide = HEADS * PAIR
@@ -1387,30 +1572,21 @@
         scratch[f"final{w}"] = vm((c8 // 2, 2 * share), F32)
         scratch[f"part{w}"] = vm((c8 // 2, share), F32)
     dims = lambda u: unit_shape(u, shapes)
-    size = {}
-    for gi, g in enumerate(SUM_GROUPS):
-        early = gi < EARLY
-        for k, u in enumerate(g):
+    slot_names = {}
+    for gi in range(EARLY):
+        for k, u in enumerate(SUM_GROUPS[gi]):
             _, _, n, _, nl, route, _ = dims(u)
-            key = (gi - (0 if early else EARLY), k)
-            size.setdefault(key, {})[early] = (n, nl, route)
-    slot_names = {}
-    for (gi, k), kinds in size.items():
-        same = len(kinds) == 2 and kinds[True] == kinds[False]
-        for early, (n, nl, route) in kinds.items():
-            tag = f"slot{gi}_{k}" + ("" if same else ("e" if early else "l"))
-            slot_names[(gi + (0 if early else EARLY), k)] = tag
-            if tag + "a" not in scratch:
-                scratch[tag + "a"] = vm((2, depth, 2, n, nl))
-                scratch[tag + "b"] = vm((depth, 2, n, nl) if route == 0 else (2, depth, n, nl))
-                scratch[tag + "c"] = vm((depth, n, nl))
-                scratch[tag + "d"] = vm((depth - 1, n, nl))
+            tag = slot_names[(gi, k)] = f"slot{gi}_{k}"
+            scratch[tag + "a"] = vm((2, depth, 2, n, nl))
+            scratch[tag + "b"] = vm((depth, 2, n, nl) if route == 0 else (2, depth, n, nl))
+            scratch[tag + "c"] = vm((depth, n, nl))
+            scratch[tag + "d"] = vm((depth - 1, n, nl))
     for gi in range(EARLY):
         for k, u in enumerate(SUM_GROUPS[gi]):
             _, _, n, _, nl, _, _ = dims(u)
             scratch[f"own{gi % 2}_{k}"] = vm((2, depth, 2, n, nl))
-    ns = sum(len(g) * (4 + 2 + depth - 1) for g in SUM_GROUPS) + len(shapes) + 2 * (total - 1) + ndp + 40
-    scratch.update(send=pltpu.SemaphoreType.DMA((ns,)), recv=pltpu.SemaphoreType.DMA((ns,)), free=pltpu.SemaphoreType.REGULAR)
+    ns = sum(len(g) * (4 + 2 + depth - 1) for g in SUM_GROUPS) + len(shapes) + 2 * (total - 1) + ndp + 80
+    scratch.update(send=pltpu.SemaphoreType.DMA((ns,)), recv=pltpu.SemaphoreType.DMA((ns,)), free=pltpu.SemaphoreType.REGULAR((EARLY,)))
     names = list(scratch)
     small_names, big_names = list(small), list(big)
     outs = dict(latents=((t, d), F32), mg=((deep, mcols), F32), tig=((tin_rows, t_cols), F32), tog=((d // ncore, t_cols), F32))
@@ -1420,24 +1596,22 @@
         at = 3
         r = {}
         for n in small_names:
-            r["sums_in" if n == "sums" else n] = refs[at]
+            r[n] = refs[at]
             at += 1
         for n in big_names:
             r["in_" + n] = refs[at]
             at += 1
-        ff = refs[at : at + 2]
-        at += 2
         r["out_latents"] = refs[at]
         r["mg"], r["tig"], r["tog"] = refs[at + 1 : at + 4]
         at += 4
         r["shares"] = refs[at : at + len(shapes)]
         at += len(shapes)
+        r["ffu"], r["ffd"] = refs[at : at + 2]
+        at += 2
         r.update(zip(names, refs[at:]))
-        r["grads"] = [r[f"grad{w}"] for w in range(5)] + list(ff)
+        r["grads"] = [r[f"grad{w}"] for w in range(5)] + [r["ffu"], r["ffd"]]
         r["final"] = [r[f"final{w}"] for w in range(len(shapes))]
         r["part"] = [r[f"part{w}"] for w in range(len(shapes))]
-        r["sums"][...] = r["sums_in"][...]
-
         def flat(w, left, right, width):
             out = r[f"grad{w}"]
             c8 = shapes[w][0]
@@ -1461,25 +1635,26 @@
             tagged[(gi, k)] = [r[tag + e] for e in "abcd"]
         r["slot_of"] = tagged
         links = BackwardLinks(mesh, shapes, r)
+        backward_ff_linked(links, r, lens, r["mod"], r["rs"], r["sums"])
         backward_linked(links, r, lens, tlens, keep, r["mod"], r["text"], r["rs"], r["sums"])
         links.finish()
 
     got = pl.pallas_call(
         kernel,
-        out_shape=[sds(*outs[n]) for n in outs] + [sds(s, F32) for s in shapes],
-        in_specs=[SM] * 3 + [VM] * len(small) + [ANY] * (len(big) + 2),
-        out_specs=[ANY] + [VM] * (3 + len(shapes)),
+        out_shape=[sds(*outs[n]) for n in outs] + [sds(s, F32) for s in shapes]
+        + [sds((depth, 2) + (shapes[w][0], shapes[w][1] * ncore)) for w in (5, 6)],
+        in_specs=[SM] * 3 + [VM] * len(small) + [ANY] * len(big),
+        out_specs=[ANY] + [VM] * (3 + len(shapes)) + [ANY] * 2,
         scratch_shapes=list(scratch.values()),
         cost_estimate=pl.CostEstimate(flops=int(6e10), bytes_accessed=int(8e7), transcendentals=0),
         compiler_params=pltpu.CompilerParams(collective_id=1, has_side_effects=True, vmem_limit_bytes=63 * MIB),
-    )(lens, tlens, keep, *small.values(), *big.values(),
-      *[g.reshape(depth, 2, shapes[5 + k][0], g.shape[1]) for k, g in enumerate(grads_ff)])
+    )(lens, tlens, keep, *small.values(), *big.values())
     turned = pl.pallas_call(
         partial(turn_body, len(shapes)),
         out_shape=[sds(s[::-1], F32) for s in shapes],
         in_specs=[VM] * len(shapes),
         out_specs=[VM] * len(shapes),
-    )(*got[4:])
+    )(*got[4 : 4 + len(shapes)])
     return got[:4], turned
 
 
@@ -1524,7 +1699,7 @@
 def fits(mesh, frames, weights):
     if mesh.shape["fsdp"] != 4 or mesh.shape["dp"] % 2:
         return False
-    if mesh.shape["dp"] * mesh.shape["fsdp"] * 16 > frames:
+    if mesh.shape["dp"] * mesh.shape["fsdp"] * 16 > frames or frames != weights[1].shape[0] * mesh.shape["fsdp"]:
         return False
     return all(w.shape[0] * 2 % 128 == 0 and w.shape[1] % 32 == 0 for w in weights)
 
@@ -1549,16 +1724,16 @@
         full, saved = gather_forward(mesh, item_lengths, text_lengths, keep, loud, embedding, latents, noise_draw, text,
                                      modulation, sent)
         mod = saved["mod"]
-        first = [saved[n] for n in SAVED[4:]]
         weights = full[2:]
-        second = run_ff(item_lengths, mod, first[0], *weights[5:])
-        g, b2, dwd, dwu, sums = run_ff_back(item_lengths, mod, cotangent, saved["br2"], second, *weights[5:])
-        small = dict(mod=mod, text=text, rs=saved["rs"], sums=sums, modw=modulation, eall=saved["eall"])
-        big = {n: saved[n] for n in ("att2", "qa2", "mem", "m2", "xh2", "qa1", "att1", "packed", "br1", "m1", "xh1", "pre1", "pre2")}
-        big.update(b2=b2, g=g, wsp=weights[0], wso=weights[1], wcq=weights[2], wco=weights[4], tout=full[1])
+        small = dict(mod=mod, text=text, rs=saved["rs"], modw=modulation, eall=saved["eall"])
+        names = ("att2", "qa2", "mem", "m2", "xh2", "qa1", "att1", "packed", "br1", "m1", "xh1", "br2", "pre1", "pre2",
+                 "xh3", "m3", "act", "slope", "br3")
+        big = {n: saved[n] for n in names}
+        big.update(cot=cotangent, wsp=weights[0], wso=weights[1], wcq=weights[2], wco=weights[4], wup=weights[5],
+                   wdn=weights[6], tout=full[1])
         (lat_grad, modulation_grad, time_in_grad, time_out_grad), shares = reduce_backward(
-            mesh, item_lengths, text_lengths, keep, small, big, (dwu, dwd), None)
-        return (second[5], lat_grad, time_in_grad, time_out_grad, modulation_grad, *shares)
+            mesh, item_lengths, text_lengths, keep, small, big)
+        return (saved["out"], lat_grad, time_in_grad, time_out_grad, modulation_grad, *shares)
     full = [plain_gather(w) for w in sent]
     t_in, t_out = full[0].astype(F32), full[1].astype(F32)
     embedding = lax.all_gather(embedding, BOTH, axis=0, tiled=True)

time: 375 us -> 337 us (0.90)
  Pallas kernels: 358 us -> 320 us
    pallas_call x2 -> x0, Pallas kernels: 58.8 us -> none  [call(): pl.pallas_call(body, out_shape=outs, in_specs=[SM] * len(scalars) + [VM]...]
    pallas_call x1, Pallas kernels: 145 us -> 160 us  [gather_forward(): pl.pallas_call(kernel, out_shape=[sds((depth, 2, c8, share * ncore)) for...]
    pallas_call x1, Pallas kernels: 152 us -> 158 us  [reduce_backward(): pl.pallas_call(kernel, out_shape=[sds(*outs[n]) for n in outs] + [sds(s,...]
    unnamed x12 -> x17, local copies, waits for them, and re-layouts: 9 us -> 9.2 us
where the time goes in v4:
time: 337 us; the launch traced here: 333 us
  Pallas kernels  320 us (95%)
  local copies, waits for them, and re-layouts  9.2 us (3%)
    pallas_call x1, Pallas kernels, gather_forward(): pl.pallas_call(kernel, out_shape=[sds((depth, 2, c8, share * ncore)) for...  160 us
    pallas_call x1, Pallas kernels, reduce_backward(): pl.pallas_call(kernel, out_shape=[sds(*outs[n]) for n in outs] + [sds(s,...  158 us
    unnamed x17, local copies, waits for them, and re-layouts  9.2 us

profile of v4, /device:TPU:0, one launch (start us, length us, event | category | flops | bytes accessed | tf_op | source)
XLA Modules:
  0.0 333.2 jit_solution(11296257199893065068)
XLA Ops:
  0.6 0.7 convert_element_type.5
  1.3 1.2 subtract_sqrt_fusion
  2.5 0.1 multiply_cosine_fusion
  2.7 0.6 select_maximum_fusion.refs_4_
  3.3 1.7 copy.29.refs_17_
  5.0 159.8 %shard_map.256 = (bf16[4,2,96,256]{3,2,1,0:T(8,128)(2,1)}, bf16[4,2,96,768]{3,2,1,0:T(8,128)(2,1)}, bf16[4,2,288,768]{3,2,1,0:T(8,128)(2,1)}, bf16[4,2,96,768]{3...) custom-call(s32[1,3]{1,0:T(1,128)} %refs_0_.3, ...), custom_call_target="tpu_custom_call" | custom-call | flops 30000001024 | bytes 60000000 | tf_op jit(solution)/shard_map/pallas_call | solution.py:982
  164.8 157.6 %shard_map.257 = (f32[768,768]{1,0:T(8,128)}, f32[192,864]{1,0:T(8,128)}, f32[64,96]{1,0:T(8,128)}, f32[192,96]{1,0:T(8,128)}, f32[288,192]{1,0:T(8,128)}, /*ind...) custom-call(s32[1,3]{1,0:T(1,128)} %refs_0_.3, ...), custom_call_target="tpu_custom_call" | custom-call | flops 60000002048 | bytes 80000000 | tf_op jit(solution)/shard_map/pallas_call | solution.py:1642
  322.5 0.0 copy-start.1
  322.5 2.8 shard_map.258
  325.3 1.9 copy.30
  327.1 0.0 copy-done.1
  327.1 0.0 copy-start
  327.1 1.0 copy.36
  328.2 1.1 copy-done
  329.2 0.0 copy-start.4
  329.2 0.0 copy-start.3
  329.2 0.0 copy-start.2
  329.2 1.4 copy.37
  330.6 0.0 copy-done.4
  330.6 0.6 copy.38
  331.3 0.0 copy-done.3
  331.3 0.6 copy.39
  331.9 0.0 copy-done.2
  331.9 0.8 copy.40
  (1 shorter events, 0.0 us)
Async XLA Ops:
  322.5 4.7 %copy-start.1 = (bf16[768,768]{1,0:T(8,128)(2,1)S(1)}, bf16[768,768]{1,0:T(8,128)(2,1)}, u32[]{:S(2)}) copy-start(bf16[768,768]{1,0:T(8,128)(2,1)} %get-tuple-element.136) | copy-start | bytes 3538948
  327.1 2.1 copy-start
  329.2 1.4 copy-start.4
  329.2 2.0 copy-start.3
  329.2 2.7 copy-start.2
